TPU v7x, 128 devices: a whole 4x4x4 slice. The times are simulated.
128 devices in a mesh: dp: 4 (over z), cuts: 32 (over x, y, core).
Axes of the slice: x: 4, y: 4, z: 4, core: 2. Of those that a mesh axis runs over, the one named last changes fastest.
Arguments:
- tokens: bfloat16 [3072, 6144], P('dp', 'cuts'), may hold values from -6 to 6
- cotangent: bfloat16 [3072, 6144], P('dp', 'cuts'), may hold values from -6 to 6
- expert_ids: int32 [3072, 2], P('dp'), may hold values from 0 to 7, as said below
- gates: float32 [3072, 2], P('dp'), may hold values from 0.1 to 0.9
- w_gate: bfloat16 [6144, 16384], P('dp', 'cuts'), may hold values from -0.078125 to 0.078125
- w_up: bfloat16 [6144, 16384], P('dp', 'cuts'), may hold values from -0.078125 to 0.078125
- w_down: bfloat16 [6144, 16384], P('dp', 'cuts'), may hold values from -0.046875 to 0.046875
Outputs:
- grad_tokens: bfloat16 [3072, 6144], P('dp', 'cuts')
- grad_gate: bfloat16 [6144, 16384], P('dp', 'cuts')
- grad_up: bfloat16 [6144, 16384], P('dp', 'cuts')
- grad_down: bfloat16 [6144, 16384], P('dp', 'cuts')
Inputs may be any that keep to these rules, and one draw needn't show every extreme that they name: `expert_ids`: each token names two different experts. In each token group at most 384 tokens name expert 0, and in some group exactly 384 do.
All inputs are finite; a program needn't handle non-finite values.
Results may differ from a plain program's by a relative error of at most 0.023.
Values may be sent and summed in bfloat16 or wider, within the bound.
No kernel may reach another device: no remote copies, remote signals or barrier semaphores. Data moves between devices by JAX's collectives and lax.ppermute only.
A program may use at most 128 MiB of HBM per device.

v0:
```python
import jax
import jax.numpy as jnp
from jax import lax
from jax.sharding import PartitionSpec as P

CAP = 384


def swiglu_backward(gate_pre, up_pre, grad_hidden):
    logistic = jax.nn.sigmoid(gate_pre)
    activated = gate_pre * logistic
    hidden = (activated * up_pre).astype(jnp.bfloat16)
    grad_up = (grad_hidden * activated).astype(jnp.bfloat16)
    grad_gate = (grad_hidden * up_pre * logistic * (1.0 + gate_pre * (1.0 - logistic))).astype(
        jnp.bfloat16
    )
    return (grad_gate, grad_up, hidden)


def over_rows(left_side, right_side):
    return lax.dot_general(
        left_side, right_side, (((0,), (0,)), ((), ())), preferred_element_type=jnp.float32
    )


def against_units(left_side, right_side):
    return lax.dot_general(
        left_side, right_side, (((1,), (1,)), ((), ())), preferred_element_type=jnp.float32
    )


def per_device(tokens, cotangent, expert_ids, gates, w_gate, w_up, w_down):
    routed = expert_ids == 0
    routed_weight = jnp.sum(jnp.where(routed, gates, 0.0), axis=1)
    is_routed = jnp.any(routed, axis=1)
    slot_rank = jnp.cumsum(is_routed.astype(jnp.int32)) - 1
    slot_index = jnp.arange(CAP, dtype=jnp.int32)
    selector = (slot_rank[None, :] == slot_index[:, None]) & is_routed[None, :]
    picker = selector.astype(jnp.bfloat16)
    x_slots = jnp.dot(picker, tokens, preferred_element_type=jnp.float32).astype(jnp.bfloat16)
    dy_slots = jnp.dot(picker, cotangent, preferred_element_type=jnp.float32).astype(jnp.bfloat16)
    slot_weight = jnp.sum(jnp.where(selector, routed_weight[None, :], 0.0), axis=1)
    x_rows, dy_rows = (
        lax.all_gather(x_slots, "cuts", axis=1, tiled=True),
        lax.all_gather(dy_slots, "cuts", axis=1, tiled=True),
    )
    scaled = (slot_weight[:, None] * dy_rows.astype(jnp.float32)).astype(jnp.bfloat16)
    unit_width = w_gate.shape[1]
    full_gate, full_up, full_down = (
        lax.all_gather(w_gate, "dp", axis=0, tiled=True),
        lax.all_gather(w_up, "dp", axis=0, tiled=True),
        lax.all_gather(w_down, "dp", axis=0, tiled=True),
    )
    gate_pre = jnp.dot(x_rows, full_gate, preferred_element_type=jnp.float32)
    up_pre = jnp.dot(x_rows, full_up, preferred_element_type=jnp.float32)
    grad_hidden = jnp.dot(scaled, full_down, preferred_element_type=jnp.float32)
    dgate, dup, hidden = swiglu_backward(gate_pre, up_pre, grad_hidden)
    slot_partial = against_units(dgate, full_gate) + against_units(dup, full_up)
    grad_total = lax.psum_scatter(
        jnp.concatenate(
            [over_rows(x_rows, dgate), over_rows(x_rows, dup), over_rows(scaled, hidden)], axis=1
        ).astype(jnp.bfloat16),
        "dp",
        scatter_dimension=0,
        tiled=True,
    ).astype(jnp.float32)
    grad_gate = grad_total[:, :unit_width].astype(jnp.bfloat16)
    grad_up = grad_total[:, unit_width : 2 * unit_width].astype(jnp.bfloat16)
    grad_down = grad_total[:, 2 * unit_width :].astype(jnp.bfloat16)
    feature_part = lax.psum_scatter(
        slot_partial.astype(jnp.bfloat16), "cuts", scatter_dimension=1, tiled=True
    ).astype(jnp.float32)
    placed = lax.dot_general(
        selector.astype(jnp.float32),
        feature_part,
        (((0,), (0,)), ((), ())),
        precision=lax.Precision.HIGHEST,
        preferred_element_type=jnp.float32,
    )
    return (placed.astype(jnp.bfloat16), grad_gate, grad_up, grad_down)


def solution(mesh):
    in_specs = (
        P("dp", "cuts"),
        P("dp", "cuts"),
        P("dp", None),
        P("dp", None),
        P("dp", "cuts"),
        P("dp", "cuts"),
        P("dp", "cuts"),
    )
    out_specs = (P("dp", "cuts"), P("dp", "cuts"), P("dp", "cuts"), P("dp", "cuts"))
    return jax.shard_map(
        per_device, mesh=mesh, in_specs=in_specs, out_specs=out_specs, check_vma=False
    )
```

profile of v0, /device:TPU:6, one launch (start us, length us, event | category | flops | bytes accessed | tf_op | source)
XLA Modules:
  0.0 597.7 jit_solution(4754396120023370952)
XLA Ops:
  7.2 0.0 copy-start
  7.2 0.0 copy-start.3
  7.2 0.0 copy-start.4
  7.2 0.0 all-gather.10.cloned.1.call-start
  7.2 0.8 fusion.23
  8.0 0.3 reduce-window.9
  8.3 0.1 slice.19
  8.4 0.1 slice_reduce_fusion
  8.5 0.1 add_bitcast_fusion
  8.6 0.0 copy-done
  8.6 1.1 fusion.11
  9.7 0.0 all-gather.10.cloned.1.call-update
  9.7 0.0 all-gather.14.cloned.1.call-start
  9.8 0.7 all-gather.14.cloned.1.call-update
  10.5 0.0 all-gather.12.cloned.1.call-start
  10.5 0.7 all-gather.12.cloned.1.call-update
  11.2 0.0 all-gather.6.cloned.1.call-start
  11.3 2.1 fusion.8
  13.3 0.0 all-gather.6.cloned.1.call-update
  13.4 0.0 all-gather.8.cloned.1.call-start
  13.4 0.5 all-gather.8.cloned.1.call-update
  14.0 0.0 reduce-scatter.7.cloned.1.call-start
  14.0 0.0 copy-done.3
  14.0 0.0 copy-done.4
  14.0 0.3 select_reduce_fusion
  14.4 45.2 %all-gather.10.cloned.1.call-done = bf16[384,6144]{0,1:T(8,128)(2,1)} async-done(((bf16[384,192]{0,1:T(8,128)(2,1)}), bf16[384,6144]{0,1:T(8,128)(2,1)}) %all-gather.10.cloned.1.call-update) | async-done | bytes 4718608 | tf_op jit(solution)/shard_map/all_gather | solution.py:44
  59.6 67.4 %all-gather.14.cloned.1.call-done = bf16[6144,512]{1,0:T(8,128)(2,1)} async-done(((bf16[1536,512]{1,0:T(8,128)(2,1)}), bf16[6144,512]{1,0:T(8,128)(2,1)}) %all-gather.14.cloned.1.call-update) | async-done | bytes 6291472 | tf_op jit(solution)/shard_map/all_gather | solution.py:50
  127.0 6.2 %fusion.27 = f32[384,512]{1,0:T(8,128)S(1)} fusion(bf16[384,6144]{0,1:T(8,128)(2,1)} %all-gather.10.cloned.1.call-done, bf16[6144,512]{1,0:T(8,128)(2,1)} %all-gather.14.cloned.1.call-done), kind=kOutput, calls=%fused_computation.37 | convolution fusion | flops 2415919104 | bytes 11796480 | tf_op jit(solution)/shard_map/dot_general | solution.py:54
  133.2 61.9 %all-gather.12.cloned.1.call-done = bf16[6144,512]{1,0:T(8,128)(2,1)} async-done(((bf16[1536,512]{1,0:T(8,128)(2,1)}), bf16[6144,512]{1,0:T(8,128)(2,1)}) %all-gather.12.cloned.1.call-update) | async-done | bytes 6291472 | tf_op jit(solution)/shard_map/all_gather | solution.py:51
  195.1 6.2 %fusion.26 = f32[384,512]{1,0:T(8,128)S(1)} fusion(bf16[384,6144]{0,1:T(8,128)(2,1)} %all-gather.10.cloned.1.call-done, bf16[6144,512]{1,0:T(8,128)(2,1)} %all-gather.12.cloned.1.call-done), kind=kOutput, calls=%fused_computation.36 | convolution fusion | flops 2415919104 | bytes 11796480 | tf_op jit(solution)/shard_map/dot_general | solution.py:55
  201.3 43.3 %all-gather.6.cloned.1.call-done = bf16[384,6144]{0,1:T(8,128)(2,1)} async-done(((bf16[384,192]{0,1:T(8,128)(2,1)}), bf16[384,6144]{0,1:T(8,128)(2,1)}) %all-gather.6.cloned.1.call-update) | async-done | bytes 4718608 | tf_op jit(solution)/shard_map/all_gather | solution.py:45
  244.6 67.2 %all-gather.8.cloned.1.call-done = bf16[6144,512]{1,0:T(8,128)(2,1)} async-done(((bf16[1536,512]{1,0:T(8,128)(2,1)}), bf16[6144,512]{1,0:T(8,128)(2,1)}) %all-gather.8.cloned.1.call-update) | async-done | bytes 6291472 | tf_op jit(solution)/shard_map/all_gather | solution.py:52
  311.9 7.1 %multiply_convert_fusion.4 = (bf16[384,512]{1,0:T(8,128)(2,1)S(1)}, bf16[384,512]{1,0:T(8,128)(2,1)S(1)}) fusion(f32[384,512]{1,0:T(8,128)S(1)} %fusion.27, f32[384,512]{1,0:T(8,128)S(1)} %fusion.26, bf16[6144,512]{1,0:T(8,128)(2,1)} %all-gather.8.cloned.1.call-done, bf16[384,6144]{0,1:T(8,128)(2,1)} %all-gather.6.cloned.1.call-done, ...), kind=kOutput, calls=%fused_computation.17 | convolution fusion | flops 2425552896 | bytes 13370880 | tf_op jit(solution)/shard_map/dot_general | solution.py:56
  318.9 0.0 copy-start.2
  319.0 5.8 fusion.28
  324.8 0.0 copy-done.2
  324.8 5.3 fusion
  330.1 0.0 reduce-scatter.7.cloned.1.call-update
  330.1 0.2 reduce-scatter.5.cloned.1.call-start
  330.3 6.1 %convolution_convert_fusion.1 = bf16[6144,512]{0,1:T(8,128)(2,1)S(1)} fusion(bf16[384,6144]{0,1:T(8,128)(2,1)} %all-gather.10.cloned.1.call-done, bf16[384,512]{1,0:T(8,128)(2,1)S(1)} %get-tuple-element.23), kind=kOutput, calls=%fused_computation.4 | convolution fusion | flops 2419064832 | bytes 11403264 | tf_op jit(solution)/shard_map/dot_general | solution.py:21
  336.4 6.1 %convolution_convert_fusion.2 = bf16[6144,512]{0,1:T(8,128)(2,1)S(1)} fusion(bf16[384,6144]{0,1:T(8,128)(2,1)} %all-gather.10.cloned.1.call-done, bf16[384,512]{1,0:T(8,128)(2,1)S(1)} %get-tuple-element.24), kind=kOutput, calls=%fused_computation.5 | convolution fusion | flops 2419064832 | bytes 11403264 | tf_op jit(solution)/shard_map/dot_general | solution.py:21
  342.5 6.3 %convolution_convert_fusion = bf16[6144,512]{0,1:T(8,128)(2,1)S(1)} fusion(bf16[384,6144]{0,1:T(8,128)(2,1)} %all-gather.6.cloned.1.call-done, f32[384]{0:T(512)S(1)} %select_reduce_fusion, f32[384,512]{1,0:T(8,128)S(1)} %fusion.26, f32[384,512]{1,0:T(8,128)S(1)} %fusion.27), kind=kOutput, calls=%fused_computation.3 | convolution fusion | flops 2427322368 | bytes 12584448 | tf_op jit(solution)/shard_map/dot_general | solution.py:21
  348.8 29.9 %pad_maximum_fusion = bf16[6144,1536]{0,1:T(8,128)(2,1)} fusion(bf16[6144,512]{0,1:T(8,128)(2,1)S(1)} %convolution_convert_fusion, bf16[6144,512]{0,1:T(8,128)(2,1)S(1)} %convolution_convert_fusion.1, bf16[6144,512]{0,1:T(8,128)(2,1)S(1)} %convolution_convert_fusion.2), kind=kLoop, calls=%fused_computation | loop fusion | flops 56623104 | bytes 37748736 | tf_op jit(solution)/shard_map/concatenate | solution.py:60
  378.7 0.0 reduce-scatter.5.cloned.1.call-update
  378.7 35.2 %reduce-scatter.7.cloned.1.call-done = bf16[192,384]{1,0:T(8,128)(2,1)} async-done(((bf16[6144,384]{1,0:T(8,128)(2,1)}), bf16[192,384]{1,0:T(8,128)(2,1)}) %reduce-scatter.7.cloned.1.call-update) | async-done | bytes 147472
  413.9 2.0 convolution_convert_fusion.3
  416.0 165.4 %reduce-scatter.5.cloned.1.call-done = bf16[1536,1536]{0,1:T(8,128)(2,1)} async-done(((bf16[6144,1536]{0,1:T(8,128)(2,1)}), bf16[1536,1536]{0,1:T(8,128)(2,1)}) %reduce-scatter.5.cloned.1.call-update) | async-done | bytes 4718608 | tf_op jit(solution)/shard_map/reduce_scatter | solution.py:59
  581.3 0.0 copy-start.1
  581.3 3.8 fusion.25
  585.2 2.6 copy.24
  587.8 1.6 copy.23
  589.3 1.6 copy.22
  590.9 0.0 copy-done.1
  (3 shorter events, 0.0 us)
Async XLA Ops:
  7.2 1.4 copy-start
  7.2 6.8 %copy-start.3 = (s32[768,2]{0,1:T(2,128)S(1)}, s32[768,2]{0,1:T(2,128)}, u32[]{:S(2)}) copy-start(s32[768,2]{0,1:T(2,128)} %param.9) | copy-start | bytes 18436
  7.2 6.8 %copy-start.4 = (f32[768,2]{0,1:T(2,128)S(1)}, f32[768,2]{0,1:T(2,128)}, u32[]{:S(2)}) copy-start(f32[768,2]{0,1:T(2,128)} %param.10) | copy-start | bytes 18436
  7.2 52.4 %all-gather.10.cloned.1.call-start = ((), (), s32[]{:S(2)}) async-start(), calls=%async_computation.4 | async-start | bytes 4866048 | tf_op jit(solution)/shard_map/all_gather | solution.py:44
  9.7 117.2 %all-gather.14.cloned.1.call-start = ((), (), s32[]{:S(2)}) async-start(), calls=%async_computation.6 | async-start | bytes 7864320 | tf_op jit(solution)/shard_map/all_gather | solution.py:50
  10.5 184.6 %all-gather.12.cloned.1.call-start = ((), (), s32[]{:S(2)}) async-start(), calls=%async_computation.5 | async-start | bytes 7864320 | tf_op jit(solution)/shard_map/all_gather | solution.py:51
  11.2 233.4 %all-gather.6.cloned.1.call-start = ((), (), s32[]{:S(2)}) async-start(), calls=%async_computation.2 | async-start | bytes 4866048 | tf_op jit(solution)/shard_map/all_gather | solution.py:45
  13.4 298.5 %all-gather.8.cloned.1.call-start = ((), (), s32[]{:S(2)}) async-start(), calls=%async_computation.3 | async-start | bytes 7864320 | tf_op jit(solution)/shard_map/all_gather | solution.py:52
  14.0 400.0 %reduce-scatter.7.cloned.1.call-start = ((), (), s32[]{:S(2)}) async-start(), calls=%async_computation.8 | async-start | bytes 4866048
  318.9 5.8 copy-start.2
  330.1 251.2 %reduce-scatter.5.cloned.1.call-start = ((), (), s32[]{:S(2)}) async-start(), calls=%async_computation.7 | async-start | bytes 23592960 | tf_op jit(solution)/shard_map/reduce_scatter | solution.py:59
  581.3 9.6 %copy-start.1 = (bf16[768,192]{0,1:T(8,128)(2,1)S(1)}, bf16[768,192]{0,1:T(8,128)(2,1)}, u32[]{:S(2)}) copy-start(bf16[768,192]{0,1:T(8,128)(2,1)} %param.7) | copy-start | bytes 884740
Sparse Core Ops, SparseCore 0:
  10.9 48.6 all-gather.9
  61.2 65.6 all-gather.13
  128.6 66.4 all-gather.11
  197.8 46.8 all-gather.5
  246.1 65.6 all-gather.7
  330.2 83.6 reduce-scatter.6
  416.5 164.7 reduce-scatter.4
where the time goes:
time: 599 us; the launch traced here: 598 us
  waiting for transfers between devices  488 us (81%)
  matrix products  54.3 us (9%)
  other arithmetic  31.4 us (5%)
  between operations  14.3 us (2%)
  local copies, waits for them, and re-layouts  9.78 us (2%)
    reduce_scatter x1, waiting for transfers between devices, per_device(): lax.psum_scatter(jnp.concatenate([over_rows(x_rows, dgate), over_rows(x_r...  165 us
    all_gather x1, waiting for transfers between devices, per_device(): lax.all_gather(w_gate, 'dp', axis=0, tiled=True)  67.4 us
    all_gather x1, waiting for transfers between devices, per_device(): lax.all_gather(w_down, 'dp', axis=0, tiled=True)  67.2 us
    all_gather x1, waiting for transfers between devices, per_device(): lax.all_gather(w_up, 'dp', axis=0, tiled=True)  61.9 us
    all_gather x1, waiting for transfers between devices, per_device(): lax.all_gather(x_slots, 'cuts', axis=1, tiled=True)  45.2 us
    all_gather x1, waiting for transfers between devices, per_device(): lax.all_gather(dy_slots, 'cuts', axis=1, tiled=True)  43.3 us
    unnamed x8, waiting for transfers between devices  37.2 us
    concatenate x1, other arithmetic, per_device(): jnp.concatenate([over_rows(x_rows, dgate), over_rows(x_rows, dup), over_r...  29.9 us
  transfers between devices with their start and end apart: 7, of which 7 were waited for; matrix products, arithmetic and copies ran while one was open for 11% of the time, Pallas kernels for 0%

commit v1 on v0

v1 whole, which is shorter than its diff:
```python
import functools

import jax
import jax.numpy as jnp
from jax import lax
from jax.experimental import pallas as pl
from jax.experimental.pallas import tpu as pltpu
from jax.sharding import Mesh
from jax.sharding import PartitionSpec as P

CAP = 384
BF = jnp.bfloat16
F32 = jnp.float32
N = 4


def index_of(z, x, y, c):
    return ((z * N + x) * N + y) * 2 + c


def every(function):
    pairs = []
    for z in range(N):
        for x in range(N):
            for y in range(N):
                for c in range(2):
                    pairs.append((index_of(z, x, y, c), index_of(*function(z, x, y, c))))
    return pairs


def move(a, function):
    return lax.ppermute(a, ("z", "x", "y", "core"), every(function))


def shift(order, j):
    def function(z, x, y, c):
        return (z, x, (y + j) % N, c) if order[c] == "y" else (z, (x + j) % N, y, c)

    return function


def other_core(a):
    return lax.ppermute(a, "core", [(0, 1), (1, 0)])


def along_z(a, k):
    return lax.ppermute(a, "z", [(i, (i + k) % N) for i in range(N)])


def block(a, index):
    return lax.dynamic_index_in_dim(a, index % N, 0, keepdims=False)


def put(a, value, index):
    return lax.dynamic_update_slice(a, value[None], (index % N,) + (0,) * value.ndim)


def cost(flops, nbytes):
    return pl.CostEstimate(flops=int(flops), bytes_accessed=int(nbytes), transcendentals=0)


def params(mib):
    return pltpu.CompilerParams(vmem_limit_bytes=mib * 1024 * 1024)


def dot(a, b, dims):
    return lax.dot_general(a, b, (dims, ((), ())), preferred_element_type=F32)


def places(where):
    core, x, y = where[0], where[1], where[2]
    for first, side in ((0, core), (N, 1 - core)):
        for j in range(N):
            m = lax.rem(jnp.where(side == 0, y, x) + (N - j), N)
            for b in range(N):
                n = lax.rem(jnp.where(side == 0, x, y) + (N - b), N)
                group = jnp.where(side == 0, n, m)
                row = jnp.where(side == 0, 2 * m, 2 * n + 1)
                yield first + j, b, group, pl.multiple_of(row * 192, 192)


def forward_kernel(count, where, *refs):
    pieces = refs[: 2 * N]
    weights = refs[2 * N : 2 * N + count]
    out, xg_out, xg, held, out_sems, x_sems = refs[2 * N + count :]
    for j, b, group, row in places(where):
        xg[group, pl.ds(row, 192), :] = pieces[j][b]
    stores = []
    for g in range(N):
        copy = pltpu.make_async_copy(xg.at[g], xg_out.at[g], x_sems.at[g])
        copy.start()
        stores.append(copy)
    for p in range(2):
        a = jnp.concatenate([xg[2 * p], xg[2 * p + 1]], axis=1)
        for k in range(count):
            total = dot(weights[k][...], a, ((0,), (0,))).astype(BF)
            for h in range(2):
                g = 2 * p + h
                held[g, k] = total[:, h * CAP : (h + 1) * CAP]
                copy = pltpu.make_async_copy(
                    held.at[g, k], out.at[g, k], out_sems.at[g * count + k]
                )
                copy.start()
                stores.append(copy)
    for copy in stores:
        copy.wait()


def forward(where, pieces, *weights):
    count = len(weights)
    vm = pl.BlockSpec(memory_space=pltpu.VMEM)
    return pl.pallas_call(
        functools.partial(forward_kernel, count),
        out_shape=(
            jax.ShapeDtypeStruct((N, count, 512, CAP), BF),
            jax.ShapeDtypeStruct((N, 1536, CAP), BF),
        ),
        in_specs=[pl.BlockSpec(memory_space=pltpu.SMEM)] + [vm] * (2 * N + count),
        out_specs=(pl.BlockSpec(memory_space=pl.ANY), pl.BlockSpec(memory_space=pl.ANY)),
        scratch_shapes=[
            pltpu.VMEM((N, 1536, CAP), BF),
            pltpu.VMEM((N, count, 512, CAP), BF),
            pltpu.SemaphoreType.DMA((N * count,)),
            pltpu.SemaphoreType.DMA((N,)),
        ],
        compiler_params=params(28),
        cost_estimate=cost(count * 2 * 1536 * 1536 * 512, 5e6 * (1 + count)),
        name="forward_%d" % count,
    )(where, *pieces, *weights)


def slot_kernel(where, wg, wu, dgu, out):
    side = where[0]
    w = jnp.concatenate(
        [
            jnp.concatenate(
                [r[pl.ds(pl.multiple_of((2 * f + side) * 192, 192), 192), :] for f in range(N)]
            )
            for r in (wg, wu)
        ],
        axis=1,
    )
    for p in range(2):
        d = jnp.concatenate(
            [jnp.concatenate([dgu[2 * p + h, k] for k in range(2)]) for h in range(2)], axis=1
        )
        total = dot(w, d, ((1,), (0,))).astype(BF)
        for h in range(2):
            g = 2 * p + h
            for f in range(N):
                index = jnp.where(side == 0, f * N + g, g * N + f)
                out[index] = total[f * 192 : (f + 1) * 192, h * CAP : (h + 1) * CAP]


def slot_partials(side, wg, wu, dgu):
    vm = pl.BlockSpec(memory_space=pltpu.VMEM)
    return pl.pallas_call(
        slot_kernel,
        out_shape=jax.ShapeDtypeStruct((N * N, 192, CAP), BF),
        in_specs=[pl.BlockSpec(memory_space=pltpu.SMEM)] + [vm] * 3,
        out_specs=vm,
        compiler_params=params(24),
        cost_estimate=cost(2 * 1536 * 1536 * 512, 9e6),
        name="slot_partials",
    )(side.reshape(1).astype(jnp.int32), wg, wu, dgu)


def weight_kernel(x, d, *outs):
    for k, out in enumerate(outs):
        total = 0.0
        for p in range(2):
            left = jnp.concatenate([x[2 * p], x[2 * p + 1]], axis=1)
            right = jnp.concatenate([d[2 * p, k], d[2 * p + 1, k]], axis=1)
            total += dot(left, right, ((1,), (1,)))
        out[...] = total.astype(BF)


def weight_grads(x, d):
    n = d.shape[1]
    rows = 256
    return pl.pallas_call(
        weight_kernel,
        grid=(1536 // rows,),
        out_shape=[jax.ShapeDtypeStruct((1536, 512), BF)] * n,
        in_specs=[
            pl.BlockSpec((N, rows, CAP), lambda i: (0, i, 0)),
            pl.BlockSpec((N, n, 512, CAP), lambda i: (0, 0, 0, 0)),
        ],
        out_specs=[pl.BlockSpec((rows, 512), lambda i: (i, 0))] * n,
        compiler_params=params(20),
        cost_estimate=cost(n * 2 * 1536 * 1536 * 512, 8e6),
        name="weight_grads_%d" % n,
    )(x, d)


def sum_over_z(a, z):
    far = block(a, z + 2)
    up_half = along_z(far[0], 1)
    down_half = along_z(far[1], 3)
    right, left = block(a, z + 1), block(a, z + 3)
    right = jnp.stack([right[0] + up_half, right[1]])
    left = jnp.stack([left[0], left[1] + down_half])
    from_left, from_right = along_z(right, 1), along_z(left, 3)
    return block(a, z).astype(F32) + from_left.astype(F32) + from_right.astype(F32)


def neighbours_over_z(a):
    return along_z(a, 1), along_z(a, 3)


def gather_over_z(a, near, z):
    from_left, from_right = near
    far0 = along_z(from_left[0], 1)
    far1 = along_z(from_right[1], 3)
    out = jnp.zeros((N,) + a.shape, a.dtype)
    out = put(out, a, z)
    out = put(out, from_left, z + 3)
    out = put(out, from_right, z + 1)
    return put(out, jnp.stack([far0, far1]), z + 2)


def sum_of(arrays):
    return sum(a.astype(F32) for a in arrays)


def per_device(tokens, cotangent, expert_ids, gates, w_gate, w_up, w_down):
    z, x, y, core = (lax.axis_index(a) for a in ("z", "x", "y", "core"))
    where = jnp.stack([core, (x - z + N) % N, y]).astype(jnp.int32)
    routed = expert_ids == 0
    routed_weight = jnp.sum(jnp.where(routed, gates, 0.0), axis=1)
    is_routed = jnp.any(routed, axis=1)
    slot_rank = jnp.cumsum(is_routed.astype(jnp.int32)) - 1
    slot_index = jnp.arange(CAP, dtype=jnp.int32)
    selector = (slot_rank[None, :] == slot_index[:, None]) & is_routed[None, :]
    picker = selector.astype(BF)
    slot_weight = jnp.sum(jnp.where(selector, routed_weight[None, :], 0.0), axis=1)
    x_slots = dot(tokens, picker, ((0,), (1,))).astype(BF)
    dy_slots = dot(cotangent, picker, ((0,), (1,))).astype(BF)
    scaled = (slot_weight[None, :] * dy_slots.astype(F32)).astype(BF)

    both = jnp.stack([x_slots, scaled])
    both = move(both, lambda z, x, y, c: (x, (z + x) % N, y, c))
    hop = [both] + [move(both, shift("xy", j)) for j in range(1, N)]
    x_held = jnp.stack([a[0] for a in hop])
    dy_held = jnp.stack([a[1] for a in hop])
    x_own = [x_held] + [move(x_held, shift("yx", j)) for j in range(1, N)]
    x_pieces = x_own + [other_core(a) for a in x_own]
    dy_held, _ = lax.optimization_barrier((dy_held, x_own[2]))
    dy_own = [dy_held] + [move(dy_held, shift("yx", j)) for j in range(1, N)]
    dy_pieces = dy_own + [other_core(a) for a in dy_own]

    gu, xg = forward(where, x_pieces, w_gate, w_up)
    gh, dyg = forward(where, dy_pieces, w_down)
    gate_up = sum_over_z(gu, z)
    gate_pre, up_pre = gate_up[0], gate_up[1]
    grad_hidden = sum_over_z(gh.reshape(N, 2, 256, CAP), z).reshape(512, CAP)

    logistic = jax.nn.sigmoid(gate_pre)
    activated = gate_pre * logistic
    hidden = (activated * up_pre).astype(BF)
    dup = (grad_hidden * activated).astype(BF)
    dgate = (grad_hidden * up_pre * logistic * (1.0 + gate_pre * (1.0 - logistic))).astype(BF)

    dgu = jnp.stack([dgate, dup])
    near = neighbours_over_z(dgu)
    dgu = gather_over_z(dgu, near, z)
    hidden, _ = lax.optimization_barrier((hidden.reshape(2, 256, CAP), near[0]))
    hidden_near = neighbours_over_z(hidden)

    theirs = other_core(slot_partials(1 - core, w_gate, w_up, dgu))
    total = slot_partials(core, w_gate, w_up, dgu)
    total = sum_of((total, theirs)).astype(BF).reshape(N, N, 192, CAP)
    dgu, total = lax.optimization_barrier((dgu, total))
    total = plane_sum(total, jnp.where(core == 0, y, x), "yx")
    hidden_near, _ = lax.optimization_barrier((hidden_near, total))
    hidden_all = gather_over_z(hidden, hidden_near, z).reshape(N, 1, 512, CAP)
    grad_gate, grad_up = weight_grads(xg, dgu)
    total, grad_gate = lax.optimization_barrier((total, grad_gate))
    total = plane_sum(total, jnp.where(core == 0, x, y), "xy")
    (grad_down,) = weight_grads(dyg, hidden_all)
    slot_grad = move(total, lambda z, x, y, c: (x, z, y, c))
    grad_tokens = dot(picker, slot_grad, ((0,), (1,))).astype(BF)
    return grad_tokens, grad_gate, grad_up, grad_down


def plane_sum(a, index, order):
    got = [block(a, index)]
    got += [move(block(a, index + j), shift(order, j)) for j in range(1, N)]
    return sum_of(got).astype(BF)


def solution(mesh):
    fine = Mesh(mesh.devices.reshape(N, N, N, 2), ("z", "x", "y", "core"))
    cuts = ("x", "y", "core")
    split, rows = P("z", cuts), P("z", None)
    return jax.shard_map(
        per_device,
        mesh=fine,
        in_specs=(split, split, rows, rows, split, split, split),
        out_specs=(split, split, split, split),
        check_vma=False,
    )
```

time: 599 us -> 233 us (0.39)
  waiting for transfers between devices: 488 us -> 81.4 us
  starting transfers between devices: 0.46 us -> 62.3 us
  matrix products: 54.3 us -> 2.99 us
  Pallas kernels: 0 us -> 38 us
  local copies, waits for them, and re-layouts: 9.78 us -> 28.7 us
  other arithmetic: 31.4 us -> 16.9 us
  between operations: 14.3 us -> 1.15 us
    all_gather x5 -> x0, waiting for transfers between devices: 285 us -> none  [the longest x1 67.4 us: per_device(): lax.all_gather(w_gate, 'dp', axis=0, tiled=True)]
    reduce_scatter x1 -> x0, waiting for transfers between devices: 165 us -> none  [per_device(): lax.psum_scatter(jnp.concatenate([over_rows(x_rows, dgate), over_rows(x_r...]
    ppermute x0 -> x42, waiting for transfers between devices: none -> 81.4 us  [the longest x16 41.5 us: along_z(): return lax.ppermute(a, 'z', [(i, (i + k) % N) for i in range(N)])]
    ppermute x0 -> x42, starting transfers between devices: none -> 62.3 us  [the longest x17 31.5 us: move(): return lax.ppermute(a, ('z', 'x', 'y', 'core'), every(function))]
    dot_general x11 -> x3, matrix products: 54.3 us -> 2.99 us  [dot(): return lax.dot_general(a, b, (dims, ((), ())), preferred_element_type=F32)]
    pallas_call x0 -> x6, Pallas kernels: none -> 38 us  [the longest x2 19.1 us: forward(): pl.pallas_call(functools.partial(forward_kernel, count), out_shape=(jax.S...]
    unnamed x8 -> x0, waiting for transfers between devices: 37.2 us -> none
    concatenate x1 -> x0, other arithmetic: 29.9 us -> none  [per_device(): jnp.concatenate([over_rows(x_rows, dgate), over_rows(x_rows, dup), over_r...]
  transfers between devices with their start and end apart: 7 -> 42, of which waited for: 7 -> 20; matrix products, arithmetic and copies ran while one was open for 11% -> 8% of each run, Pallas kernels for 0% -> 15%
where the time goes in v1:
time: 233 us; the launch traced here: 231 us
  waiting for transfers between devices  81.4 us (35%)
  starting transfers between devices  62.3 us (27%)
  Pallas kernels  38 us (16%)
  local copies, waits for them, and re-layouts  28.7 us (12%)
  other arithmetic  16.9 us (7%)
  matrix products  2.99 us (1%)
    ppermute x16, waiting for transfers between devices, along_z(): return lax.ppermute(a, 'z', [(i, (i + k) % N) for i in range(N)])  41.5 us
    ppermute x17, waiting for transfers between devices, move(): return lax.ppermute(a, ('z', 'x', 'y', 'core'), every(function))  39.9 us
    ppermute x17, starting transfers between devices, move(): return lax.ppermute(a, ('z', 'x', 'y', 'core'), every(function))  31.5 us
    ppermute x16, starting transfers between devices, along_z(): return lax.ppermute(a, 'z', [(i, (i + k) % N) for i in range(N)])  29.6 us
    unnamed x60, local copies, waits for them, and re-layouts  19.8 us
    pallas_call x2, Pallas kernels, forward(): pl.pallas_call(functools.partial(forward_kernel, count), out_shape=(jax.S...  19.1 us
    pallas_call x2, Pallas kernels, weight_grads(): pl.pallas_call(weight_kernel, grid=(1536 // rows,), out_shape=[jax.ShapeD...  12.2 us
    pallas_call x2, Pallas kernels, slot_partials(): pl.pallas_call(slot_kernel, out_shape=jax.ShapeDtypeStruct((N * N, 192, C...  6.63 us
  transfers between devices with their start and end apart: 42, of which 20 were waited for; matrix products, arithmetic and copies ran while one was open for 8% of the time, Pallas kernels for 15%

profile of v1, /device:TPU:6, one launch (start us, length us, event | category | flops | bytes accessed | tf_op | source)
XLA Modules:
  0.0 231.4 jit_solution(14975744080109291666)
XLA Ops:
  3.5 1.4 fusion.25
  4.9 5.9 %collective-permute-start = (bf16[2,192,384]{2,1,0:T(8,128)(2,1)S(1)}, bf16[2,192,384]{2,1,0:T(8,128)(2,1)S(1)}, u32[]{:S(2)}, u32[]{:S(2)}) collective-permute-start(bf16[2,192,384]{2,1,0:T(8,128)(2,1)S(1)} %pad_maximum_fusion.7), channel_id=1, source_target_pairs={{0,0},{1,1},{2,2},{3,3},{4,4},{5,5},{6,6},{7,7},{8,40},{9,41},{10,... | collective-permute-start | bytes 884744 | tf_op jit(solution)/shard_map/ppermute | solution.py:32
  10.9 8.0 %collective-permute-done = bf16[2,192,384]{2,1,0:T(8,128)(2,1)S(1)} collective-permute-done((bf16[2,192,384]{2,1,0:T(8,128)(2,1)S(1)}, bf16[2,192,384]{2,1,0:T(8,128)(2,1)S(1)}, u32[]{:S(2)}, u32[]{:S(2)}) %collective-permute-start) | collective-permute-done | bytes 294944 | tf_op jit(solution)/shard_map/ppermute | solution.py:32
  18.9 3.5 %collective-permute-start.2 = (bf16[2,192,384]{2,1,0:T(8,128)(2,1)S(1)}, bf16[2,192,384]{2,1,0:T(8,128)(2,1)S(1)}, u32[]{:S(2)}, u32[]{:S(2)}) collective-permute-start(bf16[2,192,384]{2,1,0:T(8,128)(2,1)S(1)} %collective-permute-done), channel_id=1, source_target_pairs={{0,16},{1,5},{2,18},{3,7},{4,20},{5,1},{6,22},{7,3},{8,24},{9,13},... | collective-permute-start | bytes 884744 | tf_op jit(solution)/shard_map/ppermute | solution.py:32
  23.1 2.5 %collective-permute-done.1 = bf16[2,192,384]{2,1,0:T(8,128)(2,1)S(1)} collective-permute-done((bf16[2,192,384]{2,1,0:T(8,128)(2,1)S(1)}, bf16[2,192,384]{2,1,0:T(8,128)(2,1)S(1)}, u32[]{:S(2)}, u32[]{:S(2)}) %collective-permute-start.1) | collective-permute-done | bytes 294944 | tf_op jit(solution)/shard_map/ppermute | solution.py:32
  27.8 2.5 %collective-permute-done.3 = bf16[2,192,384]{2,1,0:T(8,128)(2,1)S(1)} collective-permute-done((bf16[2,192,384]{2,1,0:T(8,128)(2,1)S(1)}, bf16[2,192,384]{2,1,0:T(8,128)(2,1)S(1)}, u32[]{:S(2)}, u32[]{:S(2)}) %collective-permute-start.3) | collective-permute-done | bytes 294944 | tf_op jit(solution)/shard_map/ppermute | solution.py:32
  31.1 3.3 %collective-permute-start.4 = (bf16[4,192,384]{2,1,0:T(8,128)(2,1)S(1)}, bf16[4,192,384]{2,1,0:T(8,128)(2,1)S(1)}, u32[]{:S(2)}, u32[]{:S(2)}) collective-permute-start(bf16[4,192,384]{2,1,0:T(8,128)(2,1)S(1)} %pad_maximum_fusion.4.refs_0_), channel_id=1, source_target_pairs={{0,4},{1,17},{2,6},{3,19},{4,0},{5,21},{6,2},{7,23},{8,12},{9,25},... | collective-permute-start | bytes 1769480 | tf_op jit(solution)/shard_map/ppermute | solution.py:32
  35.1 2.6 %collective-permute-start.17 = (bf16[4,192,384]{2,1,0:T(8,128)(2,1)S(1)}, bf16[4,192,384]{2,1,0:T(8,128)(2,1)S(1)}, u32[]{:S(2)}, u32[]{:S(2)}) collective-permute-start(bf16[4,192,384]{2,1,0:T(8,128)(2,1)S(1)} %pad_maximum_fusion.4.refs_0_), channel_id=1, source_target_pairs={{0,6},{1,25},{2,0},{3,27},{4,2},{5,29},{6,4},{7,31},{8,14},{9,1},{... | collective-permute-start | bytes 1769480 | tf_op jit(solution)/shard_map/ppermute | solution.py:32
  37.6 5.1 %collective-permute-done.4.refs_2_ = bf16[4,192,384]{2,1,0:T(8,128)(2,1)S(1)} collective-permute-done((bf16[4,192,384]{2,1,0:T(8,128)(2,1)S(1)}, bf16[4,192,384]{2,1,0:T(8,128)(2,1)S(1)}, u32[]{:S(2)}, u32[]{:S(2)}) %collective-permute-start.4) | collective-permute-done | bytes 589856 | tf_op jit(solution)/shard_map/ppermute | solution.py:32
  42.7 6.2 %collective-permute-done.16.refs_1_ = bf16[4,192,384]{2,1,0:T(8,128)(2,1)S(1)} collective-permute-done((bf16[4,192,384]{2,1,0:T(8,128)(2,1)S(1)}, bf16[4,192,384]{2,1,0:T(8,128)(2,1)S(1)}, u32[]{:S(2)}, u32[]{:S(2)}) %collective-permute-start.16) | collective-permute-done | bytes 589856 | tf_op jit(solution)/shard_map/ppermute | solution.py:32
  51.1 1.2 pad_maximum_fusion.3.refs_0_
  52.4 2.5 %collective-permute-start.6 = (bf16[4,192,384]{2,1,0:T(8,128)(2,1)S(1)}, bf16[4,192,384]{2,1,0:T(8,128)(2,1)S(1)}, u32[]{:S(2)}, u32[]{:S(2)}) collective-permute-start(bf16[4,192,384]{2,1,0:T(8,128)(2,1)S(1)} %pad_maximum_fusion.3.refs_0_), channel_id=1, source_target_pairs={{0,4},{1,17},{2,6},{3,19},{4,0},{5,21},{6,2},{7,23},{8,12},{9,25},... | collective-permute-start | bytes 1769480 | tf_op jit(solution)/shard_map/ppermute | solution.py:32
  55.7 2.0 collective-permute-start.7
  58.6 1.1 copy-done.4
  59.6 1.4 copy-done.6
  61.0 1.4 copy-done.9
  62.4 1.1 copy-done.13
  63.5 1.1 copy-done.15
  64.6 1.1 copy-done.17
  65.6 1.1 copy-done.19
  66.7 1.1 copy-done.21
  67.8 12.3 %forward_2.1 = (bf16[4,2,512,384]{3,2,1,0:T(8,128)(2,1)S(1)}, bf16[4,1536,384]{2,1,0:T(8,128)(2,1)S(1)}) custom-call(s32[3]{0:T(128)S(1)} %pad_add_fusion.where, bf16[4,192,384]{2,1,0:T(8,128)(2,1)S(1)} %copy-done.4, bf16[4,192,384]{2,1,0:T(8,128)(2,1)S(1)} %copy-done.15, bf16[4,192,384]{2,1,0:T(8,128)(2,1)S(1)} %copy-done.13, ...), custom_call_target="tpu_custom_call" | custom-call | flops 4831838208 | bytes 15000000 | tf_op jit(solution)/shard_map/forward_2/pallas_call | solution.py:112
  80.0 2.1 copy-done.23
  82.4 1.7 collective-permute-start.22
  84.0 3.1 %collective-permute-start.24 = (bf16[512,384]{1,0:T(8,128)(2,1)S(1)}, bf16[512,384]{1,0:T(8,128)(2,1)S(1)}, u32[]{:S(2)}, u32[]{:S(2)}) collective-permute-start(bf16[512,384]{1,0:T(8,128)(2,1)S(1)} %get-tuple-element.36), channel_id=1, source_target_pairs={{0,96},{32,0},{64,32},{96,64},{1,97},{33,1},{65,33},{97,65},{2,98}... | collective-permute-start | bytes 1179656 | tf_op jit(solution)/shard_map/ppermute | solution.py:47
  87.8 7.0 %collective-permute-done.22 = bf16[512,384]{1,0:T(8,128)(2,1)S(1)} collective-permute-done((bf16[512,384]{1,0:T(8,128)(2,1)S(1)}, bf16[512,384]{1,0:T(8,128)(2,1)S(1)}, u32[]{:S(2)}, u32[]{:S(2)}) %collective-permute-start.22) | collective-permute-done | bytes 393248 | tf_op jit(solution)/shard_map/ppermute | solution.py:47
  97.8 2.2 collective-permute-start.25
  100.1 6.9 %forward_1.1 = (bf16[4,1,512,384]{3,2,1,0:T(8,128)(2,1)S(1)}, bf16[4,1536,384]{2,1,0:T(8,128)(2,1)S(1)}) custom-call(s32[3]{0:T(128)S(1)} %pad_add_fusion.where, bf16[4,192,384]{2,1,0:T(8,128)(2,1)S(1)} %pad_maximum_fusion.3.refs_0_, bf16[4,192,384]{2,1,0:T(8,128)(2,1)S(1)} %collective-permute-done.5.refs_1_, ...), custom_call_target="tpu_custom_call" | custom-call | flops 2415919104 | bytes 10000000 | tf_op jit(solution)/shard_map/forward_1/pallas_call | solution.py:112
  107.0 2.2 copy-done.22
  109.3 3.2 %collective-permute-start.14 = (bf16[256,384]{1,0:T(8,128)(2,1)S(1)}, bf16[256,384]{1,0:T(8,128)(2,1)S(1)}, u32[]{:S(2)}, u32[]{:S(2)}) collective-permute-start(bf16[256,384]{1,0:T(8,128)(2,1)S(1)} %get-tuple-element.49), channel_id=1, source_target_pairs={{0,96},{32,0},{64,32},{96,64},{1,97},{33,1},{65,33},{97,65},{2,98}... | collective-permute-start | bytes 589832 | tf_op jit(solution)/shard_map/ppermute | solution.py:47
  112.6 8.9 %collective-permute-done.12 = bf16[256,384]{1,0:T(8,128)(2,1)S(1)} collective-permute-done((bf16[256,384]{1,0:T(8,128)(2,1)S(1)}, bf16[256,384]{1,0:T(8,128)(2,1)S(1)}, u32[]{:S(2)}, u32[]{:S(2)}) %collective-permute-start.12) | collective-permute-done | bytes 196640 | tf_op jit(solution)/shard_map/ppermute | solution.py:47
  123.2 3.2 %collective-permute-start.15 = (bf16[2,256,384]{2,1,0:T(8,128)(2,1)}, bf16[2,256,384]{2,1,0:T(8,128)(2,1)}, u32[]{:S(2)}, u32[]{:S(2)}) collective-permute-start(bf16[2,256,384]{2,1,0:T(8,128)(2,1)} %pad_maximum_fusion.6), channel_id=1, source_target_pairs={{0,96},{32,0},{64,32},{96,64},{1,97},{33,1},{65,33},{97,65},{2,98}... | collective-permute-start | bytes 1179656 | tf_op jit(solution)/shard_map/ppermute | solution.py:47
  126.4 1.6 fusion
  128.1 6.3 %collective-permute-done.13 = bf16[2,256,384]{2,1,0:T(8,128)(2,1)} collective-permute-done((bf16[2,256,384]{2,1,0:T(8,128)(2,1)S(1)}, bf16[2,256,384]{2,1,0:T(8,128)(2,1)}, u32[]{:S(2)}, u32[]{:S(2)}) %collective-permute-start.13) | collective-permute-done | bytes 393248 | tf_op jit(solution)/shard_map/ppermute | solution.py:47
  134.7 1.4 fusion.32
  136.1 1.5 fusion.35
  139.3 1.9 collective-permute-start.26
  141.2 1.8 collective-permute-start.27
  144.2 15.3 %collective-permute-done.26 = bf16[2,512,384]{2,1,0:T(8,128)(2,1)} collective-permute-done((bf16[2,512,384]{2,1,0:T(8,128)(2,1)}, bf16[2,512,384]{2,1,0:T(8,128)(2,1)}, u32[]{:S(2)}, u32[]{:S(2)}) %collective-permute-start.26) | collective-permute-done | bytes 786464 | tf_op jit(solution)/shard_map/ppermute | solution.py:47
  161.7 3.5 %collective-permute-start.29 = (bf16[512,384]{1,0:T(8,128)(2,1)S(1)}, bf16[512,384]{1,0:T(8,128)(2,1)S(1)}, u32[]{:S(2)}, u32[]{:S(2)}) collective-permute-start(bf16[512,384]{1,0:T(8,128)(2,1)S(1)} %slice_bitcast_fusion), channel_id=1, source_target_pairs={{0,96},{32,0},{64,32},{96,64},{1,97},{33,1},{65,33},{97,65},{2,98}... | collective-permute-start | bytes 1179656 | tf_op jit(solution)/shard_map/ppermute | solution.py:47
  165.2 1.3 bitcast_dynamic-update-slice_fusion.1
  166.5 1.4 bitcast_dynamic-update-slice_fusion
  167.9 2.8 %collective-permute-done.28 = bf16[512,384]{1,0:T(8,128)(2,1)S(1)} collective-permute-done((bf16[512,384]{1,0:T(8,128)(2,1)S(1)}, bf16[512,384]{1,0:T(8,128)(2,1)S(1)}, u32[]{:S(2)}, u32[]{:S(2)}) %collective-permute-start.28) | collective-permute-done | bytes 393248 | tf_op jit(solution)/shard_map/ppermute | solution.py:47
  171.5 4.0 %slot_partials.3 = bf16[16,192,384]{2,1,0:T(8,128)(2,1)} custom-call(s32[1]{0:T(128)} %bitcast.37.where, bf16[1536,512]{1,0:T(8,128)(2,1)S(1)} %copy-done.7, bf16[1536,512]{1,0:T(8,128)(2,1)S(1)} %copy-done.10, bf16[4,2,512,384]{3,2,1,0:T(8,128)(2,1)S(1)} %fusion.31.dgu.d), custom_call_target="tpu_custom_call" | custom-call | flops 2415919104 | bytes 9000000 | tf_op jit(solution)/shard_map/slot_partials/pallas_call | solution.py:157
  175.5 1.7 multiply_convert_fusion
  177.7 3.4 %collective-permute-start.39 = (bf16[2,256,384]{2,1,0:T(8,128)(2,1)S(1)}, bf16[2,256,384]{2,1,0:T(8,128)(2,1)S(1)}, u32[]{:S(2)}, u32[]{:S(2)}) collective-permute-start(bf16[2,256,384]{2,1,0:T(8,128)(2,1)S(1)} %multiply_convert_fusion), channel_id=1, source_target_pairs={{0,96},{32,0},{64,32},{96,64},{1,97},{33,1},{65,33},{97,65},{2,98}... | collective-permute-start | bytes 1179656 | tf_op jit(solution)/shard_map/ppermute | solution.py:47
  181.1 1.4 copy-done.11
  182.5 2.6 %slot_partials.2 = bf16[16,192,384]{2,1,0:T(8,128)(2,1)S(1)} custom-call(s32[1]{0:T(128)} %bitcast.2.where, bf16[1536,512]{1,0:T(8,128)(2,1)S(1)} %copy-done.8, bf16[1536,512]{1,0:T(8,128)(2,1)S(1)} %copy-done.11, bf16[4,2,512,384]{3,2,1,0:T(8,128)(2,1)S(1)} %fusion.31.dgu.d), custom_call_target="tpu_custom_call" | custom-call | flops 2415919104 | bytes 9000000 | tf_op jit(solution)/shard_map/slot_partials/pallas_call | solution.py:157
  185.1 2.4 %add_convert_fusion = bf16[16,192,384]{2,1,0:T(8,128)(2,1)S(1)} fusion(bf16[16,192,384]{2,1,0:T(8,128)(2,1)} %collective-permute-done.30, bf16[16,192,384]{2,1,0:T(8,128)(2,1)S(1)} %slot_partials.2), kind=kLoop, calls=%fused_computation | loop fusion | flops 4718592 | bytes 7077888 | tf_op jit(solution)/shard_map/convert_element_type | solution.py:272
  187.7 1.8 collective-permute-start.31
  189.5 1.9 collective-permute-start.32
  191.4 1.4 collective-permute-start.33
  193.1 7.3 %weight_grads_2.1 = (bf16[1536,512]{1,0:T(8,128)(2,1)}, bf16[1536,512]{1,0:T(8,128)(2,1)}) custom-call(bf16[4,1536,384]{2,1,0:T(8,128)(2,1)S(1)} %bitcast.147, bf16[4,2,512,384]{3,2,1,0:T(8,128)(2,1)S(1)} %fusion.31.dgu.d), custom_call_target="tpu_custom_call" | custom-call | flops 4831838208 | bytes 8000000 | tf_op jit(solution)/shard_map/weight_grads_2/pallas_call | solution.py:181
  200.4 5.2 %collective-permute-done.32 = bf16[4,192,384]{2,1,0:T(8,128)(2,1)S(1)} collective-permute-done((bf16[4,192,384]{2,1,0:T(8,128)(2,1)S(1)}, bf16[4,192,384]{2,1,0:T(8,128)(2,1)S(1)}, u32[]{:S(2)}, u32[]{:S(2)}) %collective-permute-start.32) | collective-permute-done | bytes 589856 | tf_op jit(solution)/shard_map/ppermute | solution.py:32
  206.6 3.3 %collective-permute-start.41 = (bf16[256,384]{1,0:T(8,128)(2,1)S(1)}, bf16[256,384]{1,0:T(8,128)(2,1)S(1)}, u32[]{:S(2)}, u32[]{:S(2)}) collective-permute-start(bf16[256,384]{1,0:T(8,128)(2,1)S(1)} %slice_bitcast_fusion.2), channel_id=1, source_target_pairs={{0,96},{32,0},{64,32},{96,64},{1,97},{33,1},{65,33},{97,65},{2,98}... | collective-permute-start | bytes 589832 | tf_op jit(solution)/shard_map/ppermute | solution.py:47
  210.0 1.5 collective-permute-start.34
  211.5 1.2 collective-permute-start.35
  213.4 1.8 collective-permute-done.34
  215.2 3.0 %collective-permute-done.35 = bf16[192,384]{1,0:T(8,128)(2,1)S(1)} collective-permute-done((bf16[192,384]{1,0:T(8,128)(2,1)S(1)}, bf16[192,384]{1,0:T(8,128)(2,1)S(1)}, u32[]{:S(2)}, u32[]{:S(2)}) %collective-permute-start.35) | collective-permute-done | bytes 147488 | tf_op jit(solution)/shard_map/ppermute | solution.py:32
  218.2 1.5 collective-permute-done.36
  219.8 2.6 %collective-permute-start.37 = (bf16[192,384]{1,0:T(8,128)(2,1)S(1)}, bf16[192,384]{1,0:T(8,128)(2,1)S(1)}, u32[]{:S(2)}, u32[]{:S(2)}) collective-permute-start(bf16[192,384]{1,0:T(8,128)(2,1)S(1)} %fusion.50), channel_id=1, source_target_pairs={{0,0},{1,1},{2,2},{3,3},{4,4},{5,5},{6,6},{7,7},{8,32},{9,33},{10,... | collective-permute-start | bytes 442376 | tf_op jit(solution)/shard_map/ppermute | solution.py:32
  222.6 4.9 %weight_grads_1.1 = bf16[1536,512]{1,0:T(8,128)(2,1)} custom-call(bf16[4,1536,384]{2,1,0:T(8,128)(2,1)S(1)} %bitcast.145, bf16[4,1,512,384]{3,2,1,0:T(8,128)(2,1)S(1)} %bitcast.143), custom_call_target="tpu_custom_call" | custom-call | flops 2415919104 | bytes 8000000 | tf_op jit(solution)/shard_map/weight_grads_1/pallas_call | solution.py:181
  227.5 2.8 %collective-permute-done.37 = bf16[192,384]{1,0:T(8,128)(2,1)S(1)} collective-permute-done((bf16[192,384]{1,0:T(8,128)(2,1)S(1)}, bf16[192,384]{1,0:T(8,128)(2,1)S(1)}, u32[]{:S(2)}, u32[]{:S(2)}) %collective-permute-start.37) | collective-permute-done | bytes 147488 | tf_op jit(solution)/shard_map/ppermute | solution.py:32
  230.3 1.1 convolution_convert_fusion
  (140 shorter events, 25.8 us)
Async XLA Ops:
  0.6 2.4 %copy-start = (bf16[768,192]{0,1:T(8,128)(2,1)S(1)}, bf16[768,192]{0,1:T(8,128)(2,1)}, u32[]{:S(2)}) copy-start(bf16[768,192]{0,1:T(8,128)(2,1)} %param.7) | copy-start | bytes 884740
  4.9 14.0 %collective-permute-start = (bf16[2,192,384]{2,1,0:T(8,128)(2,1)S(1)}, bf16[2,192,384]{2,1,0:T(8,128)(2,1)S(1)}, u32[]{:S(2)}, u32[]{:S(2)}) collective-permute-start(bf16[2,192,384]{2,1,0:T(8,128)(2,1)S(1)} %pad_maximum_fusion.7), channel_id=1, source_target_pairs={{0,0},{1,1},{2,2},{3,3},{4,4},{5,5},{6,6},{7,7},{8,40},{9,41},{10,... | collective-permute-start | bytes 884744 | tf_op jit(solution)/shard_map/ppermute | solution.py:32
  18.9 6.7 %collective-permute-start.1 = (bf16[2,192,384]{2,1,0:T(8,128)(2,1)S(1)}, bf16[2,192,384]{2,1,0:T(8,128)(2,1)S(1)}, u32[]{:S(2)}, u32[]{:S(2)}) collective-permute-start(bf16[2,192,384]{2,1,0:T(8,128)(2,1)S(1)} %collective-permute-done), channel_id=1, source_target_pairs={{0,8},{1,3},{2,10},{3,5},{4,12},{5,7},{6,14},{7,1},{8,16},{9,11},{... | collective-permute-start | bytes 884744 | tf_op jit(solution)/shard_map/ppermute | solution.py:32
  18.9 8.2 %collective-permute-start.2 = (bf16[2,192,384]{2,1,0:T(8,128)(2,1)S(1)}, bf16[2,192,384]{2,1,0:T(8,128)(2,1)S(1)}, u32[]{:S(2)}, u32[]{:S(2)}) collective-permute-start(bf16[2,192,384]{2,1,0:T(8,128)(2,1)S(1)} %collective-permute-done), channel_id=1, source_target_pairs={{0,16},{1,5},{2,18},{3,7},{4,20},{5,1},{6,22},{7,3},{8,24},{9,13},... | collective-permute-start | bytes 884744 | tf_op jit(solution)/shard_map/ppermute | solution.py:32
  22.4 7.9 %collective-permute-start.3 = (bf16[2,192,384]{2,1,0:T(8,128)(2,1)S(1)}, bf16[2,192,384]{2,1,0:T(8,128)(2,1)S(1)}, u32[]{:S(2)}, u32[]{:S(2)}) collective-permute-start(bf16[2,192,384]{2,1,0:T(8,128)(2,1)S(1)} %collective-permute-done), channel_id=1, source_target_pairs={{0,24},{1,7},{2,26},{3,1},{4,28},{5,3},{6,30},{7,5},{8,0},{9,15},{... | collective-permute-start | bytes 884744 | tf_op jit(solution)/shard_map/ppermute | solution.py:32
  31.1 27.4 %copy-start.3 = (bf16[4,192,384]{2,1,0:T(8,128)(2,1)}, bf16[4,192,384]{2,1,0:T(8,128)(2,1)S(1)}, u32[]{:S(2)}) copy-start(bf16[4,192,384]{2,1,0:T(8,128)(2,1)S(1)} %pad_maximum_fusion.4.refs_0_) | copy-start | bytes 1769476
  31.1 11.6 %collective-permute-start.4 = (bf16[4,192,384]{2,1,0:T(8,128)(2,1)S(1)}, bf16[4,192,384]{2,1,0:T(8,128)(2,1)S(1)}, u32[]{:S(2)}, u32[]{:S(2)}) collective-permute-start(bf16[4,192,384]{2,1,0:T(8,128)(2,1)S(1)} %pad_maximum_fusion.4.refs_0_), channel_id=1, source_target_pairs={{0,4},{1,17},{2,6},{3,19},{4,0},{5,21},{6,2},{7,23},{8,12},{9,25},... | collective-permute-start | bytes 1769480 | tf_op jit(solution)/shard_map/ppermute | solution.py:32
  34.4 14.5 %collective-permute-start.16 = (bf16[4,192,384]{2,1,0:T(8,128)(2,1)S(1)}, bf16[4,192,384]{2,1,0:T(8,128)(2,1)S(1)}, u32[]{:S(2)}, u32[]{:S(2)}) collective-permute-start(bf16[4,192,384]{2,1,0:T(8,128)(2,1)S(1)} %pad_maximum_fusion.4.refs_0_), channel_id=1, source_target_pairs={{0,2},{1,9},{2,4},{3,11},{4,6},{5,13},{6,0},{7,15},{8,10},{9,17},{... | collective-permute-start | bytes 1769480 | tf_op jit(solution)/shard_map/ppermute | solution.py:32
  35.1 14.7 %collective-permute-start.17 = (bf16[4,192,384]{2,1,0:T(8,128)(2,1)S(1)}, bf16[4,192,384]{2,1,0:T(8,128)(2,1)S(1)}, u32[]{:S(2)}, u32[]{:S(2)}) collective-permute-start(bf16[4,192,384]{2,1,0:T(8,128)(2,1)S(1)} %pad_maximum_fusion.4.refs_0_), channel_id=1, source_target_pairs={{0,6},{1,25},{2,0},{3,27},{4,2},{5,29},{6,4},{7,31},{8,14},{9,1},{... | collective-permute-start | bytes 1769480 | tf_op jit(solution)/shard_map/ppermute | solution.py:32
  37.6 17.2 %collective-permute-start.18 = (bf16[4,192,384]{2,1,0:T(8,128)(2,1)S(1)}, bf16[4,192,384]{2,1,0:T(8,128)(2,1)S(1)}, u32[]{:S(2)}, u32[]{:S(2)}) collective-permute-start(bf16[4,192,384]{2,1,0:T(8,128)(2,1)S(1)} %pad_maximum_fusion.4.refs_0_), channel_id=1, source_target_pairs={{0,1},{1,0},{2,3},{3,2},{4,5},{5,4},{6,7},{7,6},{8,9},{9,8},{10,11... | collective-permute-start | bytes 1769480 | tf_op jit(solution)/shard_map/ppermute | solution.py:43
  42.7 15.8 %copy-start.12 = (bf16[4,192,384]{2,1,0:T(8,128)(2,1)}, bf16[4,192,384]{2,1,0:T(8,128)(2,1)S(1)}, u32[]{:S(2)}) copy-start(bf16[4,192,384]{2,1,0:T(8,128)(2,1)S(1)} %collective-permute-done.4.refs_2_) | copy-start | bytes 1769476
  42.7 15.0 %collective-permute-start.20 = (bf16[4,192,384]{2,1,0:T(8,128)(2,1)S(1)}, bf16[4,192,384]{2,1,0:T(8,128)(2,1)S(1)}, u32[]{:S(2)}, u32[]{:S(2)}) collective-permute-start(bf16[4,192,384]{2,1,0:T(8,128)(2,1)S(1)} %collective-permute-done.4.refs_2_), channel_id=1, source_target_pairs={{0,1},{1,0},{2,3},{3,2},{4,5},{5,4},{6,7},{7,6},{8,9},{9,8},{10,11... | collective-permute-start | bytes 1769480 | tf_op jit(solution)/shard_map/ppermute | solution.py:43
  48.9 9.6 %collective-permute-start.19 = (bf16[4,192,384]{2,1,0:T(8,128)(2,1)S(1)}, bf16[4,192,384]{2,1,0:T(8,128)(2,1)}, u32[]{:S(2)}, u32[]{:S(2)}) collective-permute-start(bf16[4,192,384]{2,1,0:T(8,128)(2,1)S(1)} %collective-permute-done.16.refs_1_), channel_id=1, source_target_pairs={{0,1},{1,0},{2,3},{3,2},{4,5},{5,4},{6,7},{7,6},{8,9},{9,8},{10,11... | collective-permute-start | bytes 1769480 | tf_op jit(solution)/shard_map/ppermute | solution.py:43
  49.7 8.8 %collective-permute-start.21 = (bf16[4,192,384]{2,1,0:T(8,128)(2,1)S(1)}, bf16[4,192,384]{2,1,0:T(8,128)(2,1)}, u32[]{:S(2)}, u32[]{:S(2)}) collective-permute-start(bf16[4,192,384]{2,1,0:T(8,128)(2,1)S(1)} %collective-permute-done.17.refs_3_), channel_id=1, source_target_pairs={{0,1},{1,0},{2,3},{3,2},{4,5},{5,4},{6,7},{7,6},{8,9},{9,8},{10,11... | collective-permute-start | bytes 1769480 | tf_op jit(solution)/shard_map/ppermute | solution.py:43
  52.4 34.8 %collective-permute-start.6 = (bf16[4,192,384]{2,1,0:T(8,128)(2,1)S(1)}, bf16[4,192,384]{2,1,0:T(8,128)(2,1)S(1)}, u32[]{:S(2)}, u32[]{:S(2)}) collective-permute-start(bf16[4,192,384]{2,1,0:T(8,128)(2,1)S(1)} %pad_maximum_fusion.3.refs_0_), channel_id=1, source_target_pairs={{0,4},{1,17},{2,6},{3,19},{4,0},{5,21},{6,2},{7,23},{8,12},{9,25},... | collective-permute-start | bytes 1769480 | tf_op jit(solution)/shard_map/ppermute | solution.py:32
  55.7 31.5 %collective-permute-start.7 = (bf16[4,192,384]{2,1,0:T(8,128)(2,1)S(1)}, bf16[4,192,384]{2,1,0:T(8,128)(2,1)S(1)}, u32[]{:S(2)}, u32[]{:S(2)}) collective-permute-start(bf16[4,192,384]{2,1,0:T(8,128)(2,1)S(1)} %pad_maximum_fusion.3.refs_0_), channel_id=1, source_target_pairs={{0,6},{1,25},{2,0},{3,27},{4,2},{5,29},{6,4},{7,31},{8,14},{9,1},{... | collective-permute-start | bytes 1769480 | tf_op jit(solution)/shard_map/ppermute | solution.py:32
  58.5 29.2 %collective-permute-start.5 = (bf16[4,192,384]{2,1,0:T(8,128)(2,1)S(1)}, bf16[4,192,384]{2,1,0:T(8,128)(2,1)S(1)}, u32[]{:S(2)}, u32[]{:S(2)}) collective-permute-start(bf16[4,192,384]{2,1,0:T(8,128)(2,1)S(1)} %pad_maximum_fusion.3.refs_0_), channel_id=1, source_target_pairs={{0,2},{1,9},{2,4},{3,11},{4,6},{5,13},{6,0},{7,15},{8,10},{9,17},{... | collective-permute-start | bytes 1769480 | tf_op jit(solution)/shard_map/ppermute | solution.py:32
  58.6 1.1 copy-start.4
  59.6 1.4 copy-start.6
  61.0 1.4 copy-start.9
  64.6 1.1 copy-start.17
  65.6 1.1 copy-start.19
  66.7 1.1 copy-start.21
  80.0 2.2 copy-start.23
  82.4 12.4 %collective-permute-start.22 = (bf16[512,384]{1,0:T(8,128)(2,1)S(1)}, bf16[512,384]{1,0:T(8,128)(2,1)S(1)}, u32[]{:S(2)}, u32[]{:S(2)}) collective-permute-start(bf16[512,384]{1,0:T(8,128)(2,1)S(1)} %get-tuple-element.34), channel_id=1, source_target_pairs={{0,32},{32,64},{64,96},{96,0},{1,33},{33,65},{65,97},{97,1},{2,34}... | collective-permute-start | bytes 1179656 | tf_op jit(solution)/shard_map/ppermute | solution.py:47
  84.0 10.8 %collective-permute-start.24 = (bf16[512,384]{1,0:T(8,128)(2,1)S(1)}, bf16[512,384]{1,0:T(8,128)(2,1)S(1)}, u32[]{:S(2)}, u32[]{:S(2)}) collective-permute-start(bf16[512,384]{1,0:T(8,128)(2,1)S(1)} %get-tuple-element.36), channel_id=1, source_target_pairs={{0,96},{32,0},{64,32},{96,64},{1,97},{33,1},{65,33},{97,65},{2,98}... | collective-permute-start | bytes 1179656 | tf_op jit(solution)/shard_map/ppermute | solution.py:47
  87.2 10.7 %collective-permute-start.8 = (bf16[4,192,384]{2,1,0:T(8,128)(2,1)S(1)}, bf16[4,192,384]{2,1,0:T(8,128)(2,1)S(1)}, u32[]{:S(2)}, u32[]{:S(2)}) collective-permute-start(bf16[4,192,384]{2,1,0:T(8,128)(2,1)S(1)} %pad_maximum_fusion.3.refs_0_), channel_id=1, source_target_pairs={{0,1},{1,0},{2,3},{3,2},{4,5},{5,4},{6,7},{7,6},{8,9},{9,8},{10,11... | collective-permute-start | bytes 1769480 | tf_op jit(solution)/shard_map/ppermute | solution.py:43
  87.2 12.9 %collective-permute-start.10 = (bf16[4,192,384]{2,1,0:T(8,128)(2,1)S(1)}, bf16[4,192,384]{2,1,0:T(8,128)(2,1)S(1)}, u32[]{:S(2)}, u32[]{:S(2)}) collective-permute-start(bf16[4,192,384]{2,1,0:T(8,128)(2,1)S(1)} %collective-permute-done.6.refs_2_), channel_id=1, source_target_pairs={{0,1},{1,0},{2,3},{3,2},{4,5},{5,4},{6,7},{7,6},{8,9},{9,8},{10,11... | collective-permute-start | bytes 1769480 | tf_op jit(solution)/shard_map/ppermute | solution.py:43
  87.7 12.4 %collective-permute-start.11 = (bf16[4,192,384]{2,1,0:T(8,128)(2,1)S(1)}, bf16[4,192,384]{2,1,0:T(8,128)(2,1)S(1)}, u32[]{:S(2)}, u32[]{:S(2)}) collective-permute-start(bf16[4,192,384]{2,1,0:T(8,128)(2,1)S(1)} %collective-permute-done.7.refs_3_), channel_id=1, source_target_pairs={{0,1},{1,0},{2,3},{3,2},{4,5},{5,4},{6,7},{7,6},{8,9},{9,8},{10,11... | collective-permute-start | bytes 1769480 | tf_op jit(solution)/shard_map/ppermute | solution.py:43
  94.8 5.3 %collective-permute-start.9 = (bf16[4,192,384]{2,1,0:T(8,128)(2,1)S(1)}, bf16[4,192,384]{2,1,0:T(8,128)(2,1)S(1)}, u32[]{:S(2)}, u32[]{:S(2)}) collective-permute-start(bf16[4,192,384]{2,1,0:T(8,128)(2,1)S(1)} %collective-permute-done.5.refs_1_), channel_id=1, source_target_pairs={{0,1},{1,0},{2,3},{3,2},{4,5},{5,4},{6,7},{7,6},{8,9},{9,8},{10,11... | collective-permute-start | bytes 1769480 | tf_op jit(solution)/shard_map/ppermute | solution.py:43
  94.9 5.2 %copy-start.5 = (bf16[1536,512]{1,0:T(8,128)(2,1)S(1)}, bf16[1536,512]{1,0:T(8,128)(2,1)}, u32[]{:S(2)}) copy-start(bf16[1536,512]{1,0:T(8,128)(2,1)} %refs_8_.2) | copy-start | bytes 4718596
  95.9 30.6 %collective-permute-start.23 = (bf16[2,512,384]{2,1,0:T(8,128)(2,1)}, bf16[2,512,384]{2,1,0:T(8,128)(2,1)}, u32[]{:S(2)}, u32[]{:S(2)}) collective-permute-start(bf16[2,512,384]{2,1,0:T(8,128)(2,1)} %pad_maximum_fusion), channel_id=1, source_target_pairs={{0,32},{32,64},{64,96},{96,0},{1,33},{33,65},{65,97},{97,1},{2,34}... | collective-permute-start | bytes 2359304 | tf_op jit(solution)/shard_map/ppermute | solution.py:47
  97.8 28.6 %collective-permute-start.25 = (bf16[2,512,384]{2,1,0:T(8,128)(2,1)}, bf16[2,512,384]{2,1,0:T(8,128)(2,1)}, u32[]{:S(2)}, u32[]{:S(2)}) collective-permute-start(bf16[2,512,384]{2,1,0:T(8,128)(2,1)} %pad_maximum_fusion.1), channel_id=1, source_target_pairs={{0,96},{32,0},{64,32},{96,64},{1,97},{33,1},{65,33},{97,65},{2,98}... | collective-permute-start | bytes 2359304 | tf_op jit(solution)/shard_map/ppermute | solution.py:47
  107.0 2.2 copy-start.22
  109.2 12.7 %copy-start.2 = (bf16[4,1,512,384]{3,2,1,0:T(8,128)(2,1)}, bf16[4,1,512,384]{3,2,1,0:T(8,128)(2,1)S(1)}, u32[]{:S(2)}) copy-start(bf16[4,1,512,384]{3,2,1,0:T(8,128)(2,1)S(1)} %get-tuple-element.19) | copy-start | bytes 4718596
  109.3 12.2 %collective-permute-start.12 = (bf16[256,384]{1,0:T(8,128)(2,1)S(1)}, bf16[256,384]{1,0:T(8,128)(2,1)S(1)}, u32[]{:S(2)}, u32[]{:S(2)}) collective-permute-start(bf16[256,384]{1,0:T(8,128)(2,1)S(1)} %get-tuple-element.47), channel_id=1, source_target_pairs={{0,32},{32,64},{64,96},{96,0},{1,33},{33,65},{65,97},{97,1},{2,34}... | collective-permute-start | bytes 589832 | tf_op jit(solution)/shard_map/ppermute | solution.py:47
  109.3 12.4 %collective-permute-start.14 = (bf16[256,384]{1,0:T(8,128)(2,1)S(1)}, bf16[256,384]{1,0:T(8,128)(2,1)S(1)}, u32[]{:S(2)}, u32[]{:S(2)}) collective-permute-start(bf16[256,384]{1,0:T(8,128)(2,1)S(1)} %get-tuple-element.49), channel_id=1, source_target_pairs={{0,96},{32,0},{64,32},{96,64},{1,97},{33,1},{65,33},{97,65},{2,98}... | collective-permute-start | bytes 589832 | tf_op jit(solution)/shard_map/ppermute | solution.py:47
  121.8 12.6 %collective-permute-start.13 = (bf16[2,256,384]{2,1,0:T(8,128)(2,1)S(1)}, bf16[2,256,384]{2,1,0:T(8,128)(2,1)}, u32[]{:S(2)}, u32[]{:S(2)}) collective-permute-start(bf16[2,256,384]{2,1,0:T(8,128)(2,1)S(1)} %pad_maximum_fusion.5), channel_id=1, source_target_pairs={{0,32},{32,64},{64,96},{96,0},{1,33},{33,65},{65,97},{97,1},{2,34}... | collective-permute-start | bytes 1179656 | tf_op jit(solution)/shard_map/ppermute | solution.py:47
  123.2 11.4 %collective-permute-start.15 = (bf16[2,256,384]{2,1,0:T(8,128)(2,1)}, bf16[2,256,384]{2,1,0:T(8,128)(2,1)}, u32[]{:S(2)}, u32[]{:S(2)}) collective-permute-start(bf16[2,256,384]{2,1,0:T(8,128)(2,1)} %pad_maximum_fusion.6), channel_id=1, source_target_pairs={{0,96},{32,0},{64,32},{96,64},{1,97},{33,1},{65,33},{97,65},{2,98}... | collective-permute-start | bytes 1179656 | tf_op jit(solution)/shard_map/ppermute | solution.py:47
  139.3 20.2 %collective-permute-start.26 = (bf16[2,512,384]{2,1,0:T(8,128)(2,1)}, bf16[2,512,384]{2,1,0:T(8,128)(2,1)}, u32[]{:S(2)}, u32[]{:S(2)}) collective-permute-start(bf16[2,512,384]{2,1,0:T(8,128)(2,1)} %pad_maximum_fusion.2), channel_id=1, source_target_pairs={{0,32},{32,64},{64,96},{96,0},{1,33},{33,65},{65,97},{97,1},{2,34}... | collective-permute-start | bytes 2359304 | tf_op jit(solution)/shard_map/ppermute | solution.py:47
  141.2 19.5 %collective-permute-start.27 = (bf16[2,512,384]{2,1,0:T(8,128)(2,1)}, bf16[2,512,384]{2,1,0:T(8,128)(2,1)}, u32[]{:S(2)}, u32[]{:S(2)}) collective-permute-start(bf16[2,512,384]{2,1,0:T(8,128)(2,1)} %pad_maximum_fusion.2), channel_id=1, source_target_pairs={{0,96},{32,0},{64,32},{96,64},{1,97},{33,1},{65,33},{97,65},{2,98}... | collective-permute-start | bytes 2359304 | tf_op jit(solution)/shard_map/ppermute | solution.py:47
  160.6 10.1 %collective-permute-start.28 = (bf16[512,384]{1,0:T(8,128)(2,1)S(1)}, bf16[512,384]{1,0:T(8,128)(2,1)S(1)}, u32[]{:S(2)}, u32[]{:S(2)}) collective-permute-start(bf16[512,384]{1,0:T(8,128)(2,1)S(1)} %slice_bitcast_fusion.1), channel_id=1, source_target_pairs={{0,32},{32,64},{64,96},{96,0},{1,33},{33,65},{65,97},{97,1},{2,34}... | collective-permute-start | bytes 1179656 | tf_op jit(solution)/shard_map/ppermute | solution.py:47
  161.7 9.6 %collective-permute-start.29 = (bf16[512,384]{1,0:T(8,128)(2,1)S(1)}, bf16[512,384]{1,0:T(8,128)(2,1)S(1)}, u32[]{:S(2)}, u32[]{:S(2)}) collective-permute-start(bf16[512,384]{1,0:T(8,128)(2,1)S(1)} %slice_bitcast_fusion), channel_id=1, source_target_pairs={{0,96},{32,0},{64,32},{96,64},{1,97},{33,1},{65,33},{97,65},{2,98}... | collective-permute-start | bytes 1179656 | tf_op jit(solution)/shard_map/ppermute | solution.py:47
  166.5 5.0 %copy-start.7 = (bf16[1536,512]{1,0:T(8,128)(2,1)S(1)}, bf16[1536,512]{1,0:T(8,128)(2,1)}, u32[]{:S(2)}) copy-start(bf16[1536,512]{1,0:T(8,128)(2,1)} %wg.3) | copy-start | bytes 4718596
  166.5 5.0 %copy-start.10 = (bf16[1536,512]{1,0:T(8,128)(2,1)S(1)}, bf16[1536,512]{1,0:T(8,128)(2,1)}, u32[]{:S(2)}) copy-start(bf16[1536,512]{1,0:T(8,128)(2,1)} %wu.3) | copy-start | bytes 4718596
  175.5 9.6 %collective-permute-start.30 = (bf16[16,192,384]{2,1,0:T(8,128)(2,1)}, bf16[16,192,384]{2,1,0:T(8,128)(2,1)}, u32[]{:S(2)}, u32[]{:S(2)}) collective-permute-start(bf16[16,192,384]{2,1,0:T(8,128)(2,1)} %slot_partials.3), channel_id=1, source_target_pairs={{0,1},{1,0},{2,3},{3,2},{4,5},{5,4},{6,7},{7,6},{8,9},{9,8},{10,11... | collective-permute-start | bytes 7077896 | tf_op jit(solution)/shard_map/ppermute | solution.py:43
  175.5 5.6 %copy-start.8 = (bf16[1536,512]{1,0:T(8,128)(2,1)S(1)}, bf16[1536,512]{1,0:T(8,128)(2,1)}, u32[]{:S(2)}) copy-start(bf16[1536,512]{1,0:T(8,128)(2,1)} %wg.3) | copy-start | bytes 4718596
  177.2 29.2 %collective-permute-start.38 = (bf16[2,256,384]{2,1,0:T(8,128)(2,1)S(1)}, bf16[2,256,384]{2,1,0:T(8,128)(2,1)S(1)}, u32[]{:S(2)}, u32[]{:S(2)}) collective-permute-start(bf16[2,256,384]{2,1,0:T(8,128)(2,1)S(1)} %multiply_convert_fusion), channel_id=1, source_target_pairs={{0,32},{32,64},{64,96},{96,0},{1,33},{33,65},{65,97},{97,1},{2,34}... | collective-permute-start | bytes 1179656 | tf_op jit(solution)/shard_map/ppermute | solution.py:47
  177.7 28.7 %collective-permute-start.39 = (bf16[2,256,384]{2,1,0:T(8,128)(2,1)S(1)}, bf16[2,256,384]{2,1,0:T(8,128)(2,1)S(1)}, u32[]{:S(2)}, u32[]{:S(2)}) collective-permute-start(bf16[2,256,384]{2,1,0:T(8,128)(2,1)S(1)} %multiply_convert_fusion), channel_id=1, source_target_pairs={{0,96},{32,0},{64,32},{96,64},{1,97},{33,1},{65,33},{97,65},{2,98}... | collective-permute-start | bytes 1179656 | tf_op jit(solution)/shard_map/ppermute | solution.py:47
  181.1 1.4 copy-start.11
  182.5 10.6 %slice-start.2 = ((s8[4718592]{0:T(1024)(128)(4,1)}), s8[4194304]{0:T(1024)(128)(4,1)S(1)}, s32[]{:S(2)}) async-start(s8[4718592]{0:T(1024)(128)(4,1)} %bitcast.146), calls=%async_computation.2 | async-start | bytes 8388608
  185.1 8.0 %slice-start.3 = ((s8[4718592]{0:T(1024)(128)(4,1)}), s8[524288]{0:T(1024)(128)(4,1)S(1)}, s32[]{:S(2)}) async-start(s8[4718592]{0:T(1024)(128)(4,1)} %bitcast.146), calls=%async_computation.3 | async-start | bytes 1048576
  187.7 12.7 %collective-permute-start.31 = (bf16[4,192,384]{2,1,0:T(8,128)(2,1)S(1)}, bf16[4,192,384]{2,1,0:T(8,128)(2,1)S(1)}, u32[]{:S(2)}, u32[]{:S(2)}) collective-permute-start(bf16[4,192,384]{2,1,0:T(8,128)(2,1)S(1)} %get-tuple-element.38), channel_id=1, source_target_pairs={{0,2},{1,9},{2,4},{3,11},{4,6},{5,13},{6,0},{7,15},{8,10},{9,17},{... | collective-permute-start | bytes 1769480 | tf_op jit(solution)/shard_map/ppermute | solution.py:32
  189.5 16.1 %collective-permute-start.32 = (bf16[4,192,384]{2,1,0:T(8,128)(2,1)S(1)}, bf16[4,192,384]{2,1,0:T(8,128)(2,1)S(1)}, u32[]{:S(2)}, u32[]{:S(2)}) collective-permute-start(bf16[4,192,384]{2,1,0:T(8,128)(2,1)S(1)} %get-tuple-element.40), channel_id=1, source_target_pairs={{0,4},{1,17},{2,6},{3,19},{4,0},{5,21},{6,2},{7,23},{8,12},{9,25},... | collective-permute-start | bytes 1769480 | tf_op jit(solution)/shard_map/ppermute | solution.py:32
  191.4 14.7 %collective-permute-start.33 = (bf16[4,192,384]{2,1,0:T(8,128)(2,1)S(1)}, bf16[4,192,384]{2,1,0:T(8,128)(2,1)S(1)}, u32[]{:S(2)}, u32[]{:S(2)}) collective-permute-start(bf16[4,192,384]{2,1,0:T(8,128)(2,1)S(1)} %get-tuple-element.39), channel_id=1, source_target_pairs={{0,6},{1,25},{2,0},{3,27},{4,2},{5,29},{6,4},{7,31},{8,14},{9,1},{... | collective-permute-start | bytes 1769480 | tf_op jit(solution)/shard_map/ppermute | solution.py:32
  192.8 29.7 %slice-start = ((s8[4718592]{0:T(1024)(128)(4,1)}), s8[4194304]{0:T(1024)(128)(4,1)S(1)}, s32[]{:S(2)}) async-start(s8[4718592]{0:T(1024)(128)(4,1)} %bitcast.144), calls=%async_computation | async-start | bytes 8388608
  193.1 29.5 %slice-start.1 = ((s8[4718592]{0:T(1024)(128)(4,1)}), s8[524288]{0:T(1024)(128)(4,1)S(1)}, s32[]{:S(2)}) async-start(s8[4718592]{0:T(1024)(128)(4,1)} %bitcast.144), calls=%async_computation.1 | async-start | bytes 1048576
  206.5 15.9 %collective-permute-start.40 = (bf16[256,384]{1,0:T(8,128)(2,1)S(1)}, bf16[256,384]{1,0:T(8,128)(2,1)S(1)}, u32[]{:S(2)}, u32[]{:S(2)}) collective-permute-start(bf16[256,384]{1,0:T(8,128)(2,1)S(1)} %slice_bitcast_fusion.3), channel_id=1, source_target_pairs={{0,32},{32,64},{64,96},{96,0},{1,33},{33,65},{65,97},{97,1},{2,34}... | collective-permute-start | bytes 589832 | tf_op jit(solution)/shard_map/ppermute | solution.py:47
  206.6 15.8 %collective-permute-start.41 = (bf16[256,384]{1,0:T(8,128)(2,1)S(1)}, bf16[256,384]{1,0:T(8,128)(2,1)S(1)}, u32[]{:S(2)}, u32[]{:S(2)}) collective-permute-start(bf16[256,384]{1,0:T(8,128)(2,1)S(1)} %slice_bitcast_fusion.2), channel_id=1, source_target_pairs={{0,96},{32,0},{64,32},{96,64},{1,97},{33,1},{65,33},{97,65},{2,98}... | collective-permute-start | bytes 589832 | tf_op jit(solution)/shard_map/ppermute | solution.py:47
  210.0 5.2 %collective-permute-start.34 = (bf16[192,384]{1,0:T(8,128)(2,1)S(1)}, bf16[192,384]{1,0:T(8,128)(2,1)S(1)}, u32[]{:S(2)}, u32[]{:S(2)}) collective-permute-start(bf16[192,384]{1,0:T(8,128)(2,1)S(1)} %get-tuple-element.51), channel_id=1, source_target_pairs={{0,8},{1,3},{2,10},{3,5},{4,12},{5,7},{6,14},{7,1},{8,16},{9,11},{... | collective-permute-start | bytes 442376 | tf_op jit(solution)/shard_map/ppermute | solution.py:32
  211.5 6.7 %collective-permute-start.35 = (bf16[192,384]{1,0:T(8,128)(2,1)S(1)}, bf16[192,384]{1,0:T(8,128)(2,1)S(1)}, u32[]{:S(2)}, u32[]{:S(2)}) collective-permute-start(bf16[192,384]{1,0:T(8,128)(2,1)S(1)} %get-tuple-element.53), channel_id=1, source_target_pairs={{0,16},{1,5},{2,18},{3,7},{4,20},{5,1},{6,22},{7,3},{8,24},{9,13},... | collective-permute-start | bytes 442376 | tf_op jit(solution)/shard_map/ppermute | solution.py:32
  212.7 7.0 %collective-permute-start.36 = (bf16[192,384]{1,0:T(8,128)(2,1)S(1)}, bf16[192,384]{1,0:T(8,128)(2,1)S(1)}, u32[]{:S(2)}, u32[]{:S(2)}) collective-permute-start(bf16[192,384]{1,0:T(8,128)(2,1)S(1)} %get-tuple-element.52), channel_id=1, source_target_pairs={{0,24},{1,7},{2,26},{3,1},{4,28},{5,3},{6,30},{7,5},{8,0},{9,15},{... | collective-permute-start | bytes 442376 | tf_op jit(solution)/shard_map/ppermute | solution.py:32
  219.8 10.5 %collective-permute-start.37 = (bf16[192,384]{1,0:T(8,128)(2,1)S(1)}, bf16[192,384]{1,0:T(8,128)(2,1)S(1)}, u32[]{:S(2)}, u32[]{:S(2)}) collective-permute-start(bf16[192,384]{1,0:T(8,128)(2,1)S(1)} %fusion.50), channel_id=1, source_target_pairs={{0,0},{1,1},{2,2},{3,3},{4,4},{5,5},{6,6},{7,7},{8,32},{9,33},{10,... | collective-permute-start | bytes 442376 | tf_op jit(solution)/shard_map/ppermute | solution.py:32
  222.6 8.8 %copy-start.1 = (bf16[768,192]{0,1:T(8,128)(2,1)S(1)}, bf16[768,192]{0,1:T(8,128)(2,1)}, u32[]{:S(2)}) copy-start(bf16[768,192]{0,1:T(8,128)(2,1)} %param.7) | copy-start | bytes 884740
  (8 other events, 7.2 us)

commit v2 on v1

--- a/solution.py
+++ b/solution.py
@@ -69,44 +69,30 @@
 
 def places(where):
     core, x, y = where[0], where[1], where[2]
-    for first, side in ((0, core), (N, 1 - core)):
+    for operand, side in ((0, core), (1, 1 - core)):
         for j in range(N):
             m = lax.rem(jnp.where(side == 0, y, x) + (N - j), N)
             for b in range(N):
                 n = lax.rem(jnp.where(side == 0, x, y) + (N - b), N)
                 group = jnp.where(side == 0, n, m)
                 row = jnp.where(side == 0, 2 * m, 2 * n + 1)
-                yield first + j, b, group, pl.multiple_of(row * 192, 192)
+                yield operand, j, b, group, pl.multiple_of(row * 192, 192)
 
 
 def forward_kernel(count, where, *refs):
-    pieces = refs[: 2 * N]
-    weights = refs[2 * N : 2 * N + count]
-    out, xg_out, xg, held, out_sems, x_sems = refs[2 * N + count :]
-    for j, b, group, row in places(where):
-        xg[group, pl.ds(row, 192), :] = pieces[j][b]
-    stores = []
-    for g in range(N):
-        copy = pltpu.make_async_copy(xg.at[g], xg_out.at[g], x_sems.at[g])
-        copy.start()
-        stores.append(copy)
+    pieces, weights = refs[:2], refs[2 : 2 + count]
+    out, xg = refs[2 + count :]
+    for operand, j, b, group, row in places(where):
+        xg[group, pl.ds(row, 192), :] = pieces[operand][j, b]
     for p in range(2):
         a = jnp.concatenate([xg[2 * p], xg[2 * p + 1]], axis=1)
         for k in range(count):
             total = dot(weights[k][...], a, ((0,), (0,))).astype(BF)
             for h in range(2):
-                g = 2 * p + h
-                held[g, k] = total[:, h * CAP : (h + 1) * CAP]
-                copy = pltpu.make_async_copy(
-                    held.at[g, k], out.at[g, k], out_sems.at[g * count + k]
-                )
-                copy.start()
-                stores.append(copy)
-    for copy in stores:
-        copy.wait()
-
-
-def forward(where, pieces, *weights):
+                out[2 * p + h, k] = total[:, h * CAP : (h + 1) * CAP]
+
+
+def forward(where, own, sib, *weights):
     count = len(weights)
     vm = pl.BlockSpec(memory_space=pltpu.VMEM)
     return pl.pallas_call(
@@ -115,18 +101,12 @@
             jax.ShapeDtypeStruct((N, count, 512, CAP), BF),
             jax.ShapeDtypeStruct((N, 1536, CAP), BF),
         ),
-        in_specs=[pl.BlockSpec(memory_space=pltpu.SMEM)] + [vm] * (2 * N + count),
-        out_specs=(pl.BlockSpec(memory_space=pl.ANY), pl.BlockSpec(memory_space=pl.ANY)),
-        scratch_shapes=[
-            pltpu.VMEM((N, 1536, CAP), BF),
-            pltpu.VMEM((N, count, 512, CAP), BF),
-            pltpu.SemaphoreType.DMA((N * count,)),
-            pltpu.SemaphoreType.DMA((N,)),
-        ],
-        compiler_params=params(28),
+        in_specs=[pl.BlockSpec(memory_space=pltpu.SMEM)] + [vm] * (2 + count),
+        out_specs=(vm, vm),
+        compiler_params=params(24),
         cost_estimate=cost(count * 2 * 1536 * 1536 * 512, 5e6 * (1 + count)),
         name="forward_%d" % count,
-    )(where, *pieces, *weights)
+    )(where, own, sib, *weights)
 
 
 def slot_kernel(where, wg, wu, dgu, out):
@@ -244,13 +224,15 @@
     x_held = jnp.stack([a[0] for a in hop])
     dy_held = jnp.stack([a[1] for a in hop])
     x_own = [x_held] + [move(x_held, shift("yx", j)) for j in range(1, N)]
-    x_pieces = x_own + [other_core(a) for a in x_own]
     dy_held, _ = lax.optimization_barrier((dy_held, x_own[2]))
+    x_own = jnp.stack(x_own)
+    x_sib = other_core(x_own)
+    gu, xg = forward(where, x_own, x_sib, w_gate, w_up)
     dy_own = [dy_held] + [move(dy_held, shift("yx", j)) for j in range(1, N)]
-    dy_pieces = dy_own + [other_core(a) for a in dy_own]
-
-    gu, xg = forward(where, x_pieces, w_gate, w_up)
-    gh, dyg = forward(where, dy_pieces, w_down)
+    dy_own, gu = lax.optimization_barrier((dy_own, gu))
+    dy_own = jnp.stack(dy_own)
+    dy_sib = other_core(dy_own)
+    gh, dyg = forward(where, dy_own, dy_sib, w_down)
     gate_up = sum_over_z(gu, z)
     gate_pre, up_pre = gate_up[0], gate_up[1]
     grad_hidden = sum_over_z(gh.reshape(N, 2, 256, CAP), z).reshape(512, CAP)

time: 233 us -> 223 us (0.957)
  local copies, waits for them, and re-layouts: 28.7 us -> 17.3 us
  waiting for transfers between devices: 81.4 us -> 89.3 us
  Pallas kernels: 38 us -> 31.5 us
  other arithmetic: 16.9 us -> 20.4 us
  starting transfers between devices: 62.3 us -> 59.3 us
    unnamed x60 -> x40, local copies, waits for them, and re-layouts: 19.8 us -> 11.1 us
    pallas_call x2, Pallas kernels: 19.1 us -> 12.7 us  [forward(): pl.pallas_call(functools.partial(forward_kernel, count), out_shape=(jax.S...]
    ppermute x17, waiting for transfers between devices: 39.9 us -> 46.1 us  [move(): return lax.ppermute(a, ('z', 'x', 'y', 'core'), every(function))]
    another operation x3 -> x5, other arithmetic: 0.4 us -> 4.15 us  [the longest x1 3.36 us: per_device(): dy_own = jnp.stack(dy_own)]
    slice x4, local copies, waits for them, and re-layouts: 2.78 us -> 0.12 us  [per_device(): x_held = jnp.stack([a[0] for a in hop])]
  transfers between devices with their start and end apart: 42 -> 36, of which waited for: 20 -> 21; matrix products, arithmetic and copies ran while one was open for 8% -> 7% of each run, Pallas kernels for 15% -> 12%
where the time goes in v2:
time: 223 us; the launch traced here: 222 us
  waiting for transfers between devices  89.3 us (40%)
  starting transfers between devices  59.3 us (27%)
  Pallas kernels  31.5 us (14%)
  other arithmetic  20.4 us (9%)
  local copies, waits for them, and re-layouts  17.3 us (8%)
  matrix products  2.99 us (1%)
    ppermute x17, waiting for transfers between devices, move(): return lax.ppermute(a, ('z', 'x', 'y', 'core'), every(function))  46.1 us
    ppermute x16, waiting for transfers between devices, along_z(): return lax.ppermute(a, 'z', [(i, (i + k) % N) for i in range(N)])  43.2 us
    ppermute x17, starting transfers between devices, move(): return lax.ppermute(a, ('z', 'x', 'y', 'core'), every(function))  30.2 us
    ppermute x16, starting transfers between devices, along_z(): return lax.ppermute(a, 'z', [(i, (i + k) % N) for i in range(N)])  29 us
    pallas_call x2, Pallas kernels, forward(): pl.pallas_call(functools.partial(forward_kernel, count), out_shape=(jax.S...  12.7 us
    pallas_call x2, Pallas kernels, weight_grads(): pl.pallas_call(weight_kernel, grid=(1536 // rows,), out_shape=[jax.ShapeD...  12.3 us
    unnamed x40, local copies, waits for them, and re-layouts  11.1 us
    pallas_call x2, Pallas kernels, slot_partials(): pl.pallas_call(slot_kernel, out_shape=jax.ShapeDtypeStruct((N * N, 192, C...  6.61 us
  transfers between devices with their start and end apart: 36, of which 21 were waited for; matrix products, arithmetic and copies ran while one was open for 7% of the time, Pallas kernels for 12%

profile of v2, /device:TPU:6, one launch (start us, length us, event | category | flops | bytes accessed | tf_op | source)
XLA Modules:
  0.0 222.0 jit_solution(9586921117420644758)
XLA Ops:
  3.5 1.4 fusion.25
  4.9 5.9 %collective-permute-start = (bf16[2,192,384]{2,1,0:T(8,128)(2,1)S(1)}, bf16[2,192,384]{2,1,0:T(8,128)(2,1)S(1)}, u32[]{:S(2)}, u32[]{:S(2)}) collective-permute-start(bf16[2,192,384]{2,1,0:T(8,128)(2,1)S(1)} %pad_maximum_fusion.9), channel_id=1, source_target_pairs={{0,0},{1,1},{2,2},{3,3},{4,4},{5,5},{6,6},{7,7},{8,40},{9,41},{10,... | collective-permute-start | bytes 884744 | tf_op jit(solution)/shard_map/ppermute | solution.py:32
  10.9 8.0 %collective-permute-done = bf16[2,192,384]{2,1,0:T(8,128)(2,1)S(1)} collective-permute-done((bf16[2,192,384]{2,1,0:T(8,128)(2,1)S(1)}, bf16[2,192,384]{2,1,0:T(8,128)(2,1)S(1)}, u32[]{:S(2)}, u32[]{:S(2)}) %collective-permute-start) | collective-permute-done | bytes 294944 | tf_op jit(solution)/shard_map/ppermute | solution.py:32
  18.9 3.5 %collective-permute-start.2 = (bf16[2,192,384]{2,1,0:T(8,128)(2,1)S(1)}, bf16[2,192,384]{2,1,0:T(8,128)(2,1)S(1)}, u32[]{:S(2)}, u32[]{:S(2)}) collective-permute-start(bf16[2,192,384]{2,1,0:T(8,128)(2,1)S(1)} %collective-permute-done), channel_id=1, source_target_pairs={{0,16},{1,5},{2,18},{3,7},{4,20},{5,1},{6,22},{7,3},{8,24},{9,13},... | collective-permute-start | bytes 884744 | tf_op jit(solution)/shard_map/ppermute | solution.py:32
  22.4 3.2 %collective-permute-done.1 = bf16[2,192,384]{2,1,0:T(8,128)(2,1)S(1)} collective-permute-done((bf16[2,192,384]{2,1,0:T(8,128)(2,1)S(1)}, bf16[2,192,384]{2,1,0:T(8,128)(2,1)S(1)}, u32[]{:S(2)}, u32[]{:S(2)}) %collective-permute-start.1) | collective-permute-done | bytes 294944 | tf_op jit(solution)/shard_map/ppermute | solution.py:32
  25.7 1.5 collective-permute-done.2
  27.2 3.1 %collective-permute-done.3 = bf16[2,192,384]{2,1,0:T(8,128)(2,1)S(1)} collective-permute-done((bf16[2,192,384]{2,1,0:T(8,128)(2,1)S(1)}, bf16[2,192,384]{2,1,0:T(8,128)(2,1)S(1)}, u32[]{:S(2)}, u32[]{:S(2)}) %collective-permute-start.3) | collective-permute-done | bytes 294944 | tf_op jit(solution)/shard_map/ppermute | solution.py:32
  30.5 3.3 %collective-permute-start.4 = (bf16[4,192,384]{2,1,0:T(8,128)(2,1)S(1)}, bf16[4,192,384]{2,1,0:T(8,128)(2,1)S(1)}, u32[]{:S(2)}, u32[]{:S(2)}) collective-permute-start(bf16[4,192,384]{2,1,0:T(8,128)(2,1)S(1)} %get-tuple-element.65), channel_id=1, source_target_pairs={{0,4},{1,17},{2,6},{3,19},{4,0},{5,21},{6,2},{7,23},{8,12},{9,25},... | collective-permute-start | bytes 1769480 | tf_op jit(solution)/shard_map/ppermute | solution.py:32
  34.7 2.3 %collective-permute-start.9 = (bf16[4,192,384]{2,1,0:T(8,128)(2,1)S(1)}, bf16[4,192,384]{2,1,0:T(8,128)(2,1)S(1)}, u32[]{:S(2)}, u32[]{:S(2)}) collective-permute-start(bf16[4,192,384]{2,1,0:T(8,128)(2,1)S(1)} %get-tuple-element.65), channel_id=1, source_target_pairs={{0,6},{1,25},{2,0},{3,27},{4,2},{5,29},{6,4},{7,31},{8,14},{9,1},{... | collective-permute-start | bytes 1769480 | tf_op jit(solution)/shard_map/ppermute | solution.py:32
  37.0 5.1 %collective-permute-done.4 = bf16[4,192,384]{2,1,0:T(8,128)(2,1)S(1)} collective-permute-done((bf16[4,192,384]{2,1,0:T(8,128)(2,1)S(1)}, bf16[4,192,384]{2,1,0:T(8,128)(2,1)S(1)}, u32[]{:S(2)}, u32[]{:S(2)}) %collective-permute-start.4) | collective-permute-done | bytes 589856 | tf_op jit(solution)/shard_map/ppermute | solution.py:32
  42.1 6.2 %collective-permute-done.8 = bf16[4,192,384]{2,1,0:T(8,128)(2,1)S(1)} collective-permute-done((bf16[4,192,384]{2,1,0:T(8,128)(2,1)S(1)}, bf16[4,192,384]{2,1,0:T(8,128)(2,1)S(1)}, u32[]{:S(2)}, u32[]{:S(2)}) %collective-permute-start.8) | collective-permute-done | bytes 589856 | tf_op jit(solution)/shard_map/ppermute | solution.py:32
  49.4 1.5 copy-done.2
  51.8 1.1 collective-permute-start.5
  52.9 3.0 %collective-permute-start.6 = (bf16[4,192,384]{2,1,0:T(8,128)(2,1)}, bf16[4,192,384]{2,1,0:T(8,128)(2,1)}, u32[]{:S(2)}, u32[]{:S(2)}) collective-permute-start(bf16[4,192,384]{2,1,0:T(8,128)(2,1)} %pad_maximum_fusion.5), channel_id=1, source_target_pairs={{0,4},{1,17},{2,6},{3,19},{4,0},{5,21},{6,2},{7,23},{8,12},{9,25},... | collective-permute-start | bytes 1769480 | tf_op jit(solution)/shard_map/ppermute | solution.py:32
  56.5 1.7 copy-done.3
  58.2 1.4 copy-done.6
  59.6 1.4 copy-done.9
  61.0 7.2 %forward_2.1 = (bf16[4,2,512,384]{3,2,1,0:T(8,128)(2,1)S(1)}, bf16[4,1536,384]{2,1,0:T(8,128)(2,1)S(1)}) custom-call(s32[3]{0:T(128)S(1)} %pad_add_fusion.where, bf16[4,4,192,384]{3,2,1,0:T(8,128)(2,1)S(1)} %copy-done.3, bf16[4,4,192,384]{3,2,1,0:T(8,128)(2,1)} %collective-permute-done.10.refs_1_, bf16[1536,512]{1,0:T(8,128)(2,1)S(1)} %copy-done.6, ...), custom_call_target="tpu_custom_call" | custom-call | flops 4831838208 | bytes 15000000 | tf_op jit(solution)/shard_map/forward_2/pallas_call | solution.py:98
  68.2 2.1 collective-permute-done.6
  70.4 3.4 %pad_maximum_fusion.1.refs_0_ = bf16[4,4,192,384]{3,2,1,0:T(8,128)(2,1)} fusion(bf16[1,4,192,384]{3,2,1,0:T(8,128)(2,1)} %bitcast.16, bf16[1,4,192,384]{3,2,1,0:T(8,128)(2,1)} %bitcast.15, bf16[1,4,192,384]{3,2,1,0:T(8,128)(2,1)} %bitcast.14, bf16[1,4,192,384]{3,2,1,0:T(8,128)(2,1)} %bitcast.13), kind=kLoop, calls=%fused_computation.2 | loop fusion | flops 3538944 | bytes 4718592 | tf_op jit(solution)/shard_map/stack | solution.py:233
  74.0 1.2 collective-permute-start.16
  75.2 3.2 %collective-permute-start.18 = (bf16[512,384]{1,0:T(8,128)(2,1)S(1)}, bf16[512,384]{1,0:T(8,128)(2,1)S(1)}, u32[]{:S(2)}, u32[]{:S(2)}) collective-permute-start(bf16[512,384]{1,0:T(8,128)(2,1)S(1)} %get-tuple-element.46), channel_id=1, source_target_pairs={{0,96},{32,0},{64,32},{96,64},{1,97},{33,1},{65,33},{97,65},{2,98}... | collective-permute-start | bytes 1179656 | tf_op jit(solution)/shard_map/ppermute | solution.py:47
  78.4 9.7 %collective-permute-done.16 = bf16[512,384]{1,0:T(8,128)(2,1)S(1)} collective-permute-done((bf16[512,384]{1,0:T(8,128)(2,1)S(1)}, bf16[512,384]{1,0:T(8,128)(2,1)S(1)}, u32[]{:S(2)}, u32[]{:S(2)}) %collective-permute-start.16) | collective-permute-done | bytes 393248 | tf_op jit(solution)/shard_map/ppermute | solution.py:47
  89.2 1.1 collective-permute-start.17
  91.3 2.1 collective-permute-start.19
  93.4 5.5 %forward_1.1 = (bf16[4,1,512,384]{3,2,1,0:T(8,128)(2,1)S(1)}, bf16[4,1536,384]{2,1,0:T(8,128)(2,1)S(1)}) custom-call(s32[3]{0:T(128)S(1)} %pad_add_fusion.where, bf16[4,4,192,384]{3,2,1,0:T(8,128)(2,1)} %pad_maximum_fusion.1.refs_0_, bf16[4,4,192,384]{3,2,1,0:T(8,128)(2,1)} %collective-permute-done.11.refs_1_, bf16[1536,512]{1,0:T(8,128)(2,1)S(1)} %copy-done.5), custom_call_target="tpu_custom_call" | custom-call | flops 2415919104 | bytes 10000000 | tf_op jit(solution)/shard_map/forward_1/pallas_call | solution.py:98
  98.9 2.2 copy-done.12
  101.2 3.2 %collective-permute-start.14 = (bf16[256,384]{1,0:T(8,128)(2,1)S(1)}, bf16[256,384]{1,0:T(8,128)(2,1)S(1)}, u32[]{:S(2)}, u32[]{:S(2)}) collective-permute-start(bf16[256,384]{1,0:T(8,128)(2,1)S(1)} %get-tuple-element.59), channel_id=1, source_target_pairs={{0,96},{32,0},{64,32},{96,64},{1,97},{33,1},{65,33},{97,65},{2,98}... | collective-permute-start | bytes 589832 | tf_op jit(solution)/shard_map/ppermute | solution.py:47
  104.4 9.8 %collective-permute-done.12 = bf16[256,384]{1,0:T(8,128)(2,1)S(1)} collective-permute-done((bf16[256,384]{1,0:T(8,128)(2,1)S(1)}, bf16[256,384]{1,0:T(8,128)(2,1)S(1)}, u32[]{:S(2)}, u32[]{:S(2)}) %collective-permute-start.12) | collective-permute-done | bytes 196640 | tf_op jit(solution)/shard_map/ppermute | solution.py:47
  114.7 1.6 collective-permute-start.13
  117.2 2.0 collective-permute-start.15
  119.1 1.6 fusion
  120.8 5.7 %collective-permute-done.13 = bf16[2,256,384]{2,1,0:T(8,128)(2,1)} collective-permute-done((bf16[2,256,384]{2,1,0:T(8,128)(2,1)S(1)}, bf16[2,256,384]{2,1,0:T(8,128)(2,1)}, u32[]{:S(2)}, u32[]{:S(2)}) %collective-permute-start.13) | collective-permute-done | bytes 393248 | tf_op jit(solution)/shard_map/ppermute | solution.py:47
  126.8 1.4 fusion.32
  128.1 1.5 fusion.35
  131.4 1.8 collective-permute-start.20
  133.2 1.8 collective-permute-start.21
  136.2 14.7 %collective-permute-done.20 = bf16[2,512,384]{2,1,0:T(8,128)(2,1)} collective-permute-done((bf16[2,512,384]{2,1,0:T(8,128)(2,1)}, bf16[2,512,384]{2,1,0:T(8,128)(2,1)}, u32[]{:S(2)}, u32[]{:S(2)}) %collective-permute-start.20) | collective-permute-done | bytes 786464 | tf_op jit(solution)/shard_map/ppermute | solution.py:47
  150.9 1.0 slice_bitcast_fusion.1
  152.0 1.0 slice_bitcast_fusion
  153.0 3.3 %collective-permute-start.23 = (bf16[512,384]{1,0:T(8,128)(2,1)S(1)}, bf16[512,384]{1,0:T(8,128)(2,1)S(1)}, u32[]{:S(2)}, u32[]{:S(2)}) collective-permute-start(bf16[512,384]{1,0:T(8,128)(2,1)S(1)} %slice_bitcast_fusion), channel_id=1, source_target_pairs={{0,96},{32,0},{64,32},{96,64},{1,97},{33,1},{65,33},{97,65},{2,98}... | collective-permute-start | bytes 1179656 | tf_op jit(solution)/shard_map/ppermute | solution.py:47
  156.3 1.3 bitcast_dynamic-update-slice_fusion.1
  157.6 1.4 bitcast_dynamic-update-slice_fusion
  159.1 2.3 %collective-permute-done.22 = bf16[512,384]{1,0:T(8,128)(2,1)S(1)} collective-permute-done((bf16[512,384]{1,0:T(8,128)(2,1)S(1)}, bf16[512,384]{1,0:T(8,128)(2,1)S(1)}, u32[]{:S(2)}, u32[]{:S(2)}) %collective-permute-start.22) | collective-permute-done | bytes 393248 | tf_op jit(solution)/shard_map/ppermute | solution.py:47
  161.9 4.0 %slot_partials.3 = bf16[16,192,384]{2,1,0:T(8,128)(2,1)} custom-call(s32[1]{0:T(128)} %bitcast.45.where, bf16[1536,512]{1,0:T(8,128)(2,1)S(1)} %copy-done.7, bf16[1536,512]{1,0:T(8,128)(2,1)S(1)} %copy-done.10, bf16[4,2,512,384]{3,2,1,0:T(8,128)(2,1)S(1)} %fusion.31.dgu.d), custom_call_target="tpu_custom_call" | custom-call | flops 2415919104 | bytes 9000000 | tf_op jit(solution)/shard_map/slot_partials/pallas_call | solution.py:137
  166.0 1.7 multiply_convert_fusion
  168.2 3.5 %collective-permute-start.33 = (bf16[2,256,384]{2,1,0:T(8,128)(2,1)S(1)}, bf16[2,256,384]{2,1,0:T(8,128)(2,1)S(1)}, u32[]{:S(2)}, u32[]{:S(2)}) collective-permute-start(bf16[2,256,384]{2,1,0:T(8,128)(2,1)S(1)} %multiply_convert_fusion), channel_id=1, source_target_pairs={{0,96},{32,0},{64,32},{96,64},{1,97},{33,1},{65,33},{97,65},{2,98}... | collective-permute-start | bytes 1179656 | tf_op jit(solution)/shard_map/ppermute | solution.py:47
  171.8 1.4 copy-done.11
  173.2 2.6 %slot_partials.2 = bf16[16,192,384]{2,1,0:T(8,128)(2,1)S(1)} custom-call(s32[1]{0:T(128)} %bitcast.2.where, bf16[1536,512]{1,0:T(8,128)(2,1)S(1)} %copy-done.8, bf16[1536,512]{1,0:T(8,128)(2,1)S(1)} %copy-done.11, bf16[4,2,512,384]{3,2,1,0:T(8,128)(2,1)S(1)} %fusion.31.dgu.d), custom_call_target="tpu_custom_call" | custom-call | flops 2415919104 | bytes 9000000 | tf_op jit(solution)/shard_map/slot_partials/pallas_call | solution.py:137
  175.8 2.4 %add_convert_fusion = bf16[16,192,384]{2,1,0:T(8,128)(2,1)S(1)} fusion(bf16[16,192,384]{2,1,0:T(8,128)(2,1)} %collective-permute-done.24, bf16[16,192,384]{2,1,0:T(8,128)(2,1)S(1)} %slot_partials.2), kind=kLoop, calls=%fused_computation | loop fusion | flops 4718592 | bytes 7077888 | tf_op jit(solution)/shard_map/convert_element_type | solution.py:254
  178.4 1.5 collective-permute-start.25
  179.8 2.7 %collective-permute-start.26 = (bf16[4,192,384]{2,1,0:T(8,128)(2,1)S(1)}, bf16[4,192,384]{2,1,0:T(8,128)(2,1)S(1)}, u32[]{:S(2)}, u32[]{:S(2)}) collective-permute-start(bf16[4,192,384]{2,1,0:T(8,128)(2,1)S(1)} %get-tuple-element.50), channel_id=1, source_target_pairs={{0,4},{1,17},{2,6},{3,19},{4,0},{5,21},{6,2},{7,23},{8,12},{9,25},... | collective-permute-start | bytes 1769480 | tf_op jit(solution)/shard_map/ppermute | solution.py:32
  183.4 7.3 %weight_grads_2.1 = (bf16[1536,512]{1,0:T(8,128)(2,1)}, bf16[1536,512]{1,0:T(8,128)(2,1)}) custom-call(bf16[4,1536,384]{2,1,0:T(8,128)(2,1)S(1)} %bitcast.156, bf16[4,2,512,384]{3,2,1,0:T(8,128)(2,1)S(1)} %fusion.31.dgu.d), custom_call_target="tpu_custom_call" | custom-call | flops 4831838208 | bytes 8000000 | tf_op jit(solution)/shard_map/weight_grads_2/pallas_call | solution.py:161
  190.7 6.0 %collective-permute-done.26 = bf16[4,192,384]{2,1,0:T(8,128)(2,1)S(1)} collective-permute-done((bf16[4,192,384]{2,1,0:T(8,128)(2,1)S(1)}, bf16[4,192,384]{2,1,0:T(8,128)(2,1)S(1)}, u32[]{:S(2)}, u32[]{:S(2)}) %collective-permute-start.26) | collective-permute-done | bytes 589856 | tf_op jit(solution)/shard_map/ppermute | solution.py:32
  197.3 3.3 %collective-permute-start.35 = (bf16[256,384]{1,0:T(8,128)(2,1)S(1)}, bf16[256,384]{1,0:T(8,128)(2,1)S(1)}, u32[]{:S(2)}, u32[]{:S(2)}) collective-permute-start(bf16[256,384]{1,0:T(8,128)(2,1)S(1)} %slice_bitcast_fusion.2), channel_id=1, source_target_pairs={{0,96},{32,0},{64,32},{96,64},{1,97},{33,1},{65,33},{97,65},{2,98}... | collective-permute-start | bytes 589832 | tf_op jit(solution)/shard_map/ppermute | solution.py:47
  200.7 1.3 collective-permute-start.28
  202.0 1.1 collective-permute-start.29
  203.2 2.7 %collective-permute-done.28 = bf16[192,384]{1,0:T(8,128)(2,1)S(1)} collective-permute-done((bf16[192,384]{1,0:T(8,128)(2,1)S(1)}, bf16[192,384]{1,0:T(8,128)(2,1)S(1)}, u32[]{:S(2)}, u32[]{:S(2)}) %collective-permute-start.28) | collective-permute-done | bytes 147488 | tf_op jit(solution)/shard_map/ppermute | solution.py:32
  205.9 2.8 %collective-permute-done.29 = bf16[192,384]{1,0:T(8,128)(2,1)S(1)} collective-permute-done((bf16[192,384]{1,0:T(8,128)(2,1)S(1)}, bf16[192,384]{1,0:T(8,128)(2,1)S(1)}, u32[]{:S(2)}, u32[]{:S(2)}) %collective-permute-start.29) | collective-permute-done | bytes 147488 | tf_op jit(solution)/shard_map/ppermute | solution.py:32
  208.7 1.5 collective-permute-done.30
  210.3 2.4 %collective-permute-start.31 = (bf16[192,384]{1,0:T(8,128)(2,1)S(1)}, bf16[192,384]{1,0:T(8,128)(2,1)S(1)}, u32[]{:S(2)}, u32[]{:S(2)}) collective-permute-start(bf16[192,384]{1,0:T(8,128)(2,1)S(1)} %fusion.50), channel_id=1, source_target_pairs={{0,0},{1,1},{2,2},{3,3},{4,4},{5,5},{6,6},{7,7},{8,32},{9,33},{10,... | collective-permute-start | bytes 442376 | tf_op jit(solution)/shard_map/ppermute | solution.py:32
  212.8 4.9 %weight_grads_1.1 = bf16[1536,512]{1,0:T(8,128)(2,1)} custom-call(bf16[4,1536,384]{2,1,0:T(8,128)(2,1)S(1)} %bitcast.154, bf16[4,1,512,384]{3,2,1,0:T(8,128)(2,1)S(1)} %bitcast.152), custom_call_target="tpu_custom_call" | custom-call | flops 2415919104 | bytes 8000000 | tf_op jit(solution)/shard_map/weight_grads_1/pallas_call | solution.py:161
  217.7 3.1 %collective-permute-done.31 = bf16[192,384]{1,0:T(8,128)(2,1)S(1)} collective-permute-done((bf16[192,384]{1,0:T(8,128)(2,1)S(1)}, bf16[192,384]{1,0:T(8,128)(2,1)S(1)}, u32[]{:S(2)}, u32[]{:S(2)}) %collective-permute-start.31) | collective-permute-done | bytes 147488 | tf_op jit(solution)/shard_map/ppermute | solution.py:32
  220.8 1.1 convolution_convert_fusion
  (110 shorter events, 16.7 us)
Async XLA Ops:
  0.6 2.4 %copy-start = (bf16[768,192]{0,1:T(8,128)(2,1)S(1)}, bf16[768,192]{0,1:T(8,128)(2,1)}, u32[]{:S(2)}) copy-start(bf16[768,192]{0,1:T(8,128)(2,1)} %param.7) | copy-start | bytes 884740
  4.9 14.0 %collective-permute-start = (bf16[2,192,384]{2,1,0:T(8,128)(2,1)S(1)}, bf16[2,192,384]{2,1,0:T(8,128)(2,1)S(1)}, u32[]{:S(2)}, u32[]{:S(2)}) collective-permute-start(bf16[2,192,384]{2,1,0:T(8,128)(2,1)S(1)} %pad_maximum_fusion.9), channel_id=1, source_target_pairs={{0,0},{1,1},{2,2},{3,3},{4,4},{5,5},{6,6},{7,7},{8,40},{9,41},{10,... | collective-permute-start | bytes 884744 | tf_op jit(solution)/shard_map/ppermute | solution.py:32
  18.9 6.7 %collective-permute-start.1 = (bf16[2,192,384]{2,1,0:T(8,128)(2,1)S(1)}, bf16[2,192,384]{2,1,0:T(8,128)(2,1)S(1)}, u32[]{:S(2)}, u32[]{:S(2)}) collective-permute-start(bf16[2,192,384]{2,1,0:T(8,128)(2,1)S(1)} %collective-permute-done), channel_id=1, source_target_pairs={{0,8},{1,3},{2,10},{3,5},{4,12},{5,7},{6,14},{7,1},{8,16},{9,11},{... | collective-permute-start | bytes 884744 | tf_op jit(solution)/shard_map/ppermute | solution.py:32
  18.9 8.2 %collective-permute-start.2 = (bf16[2,192,384]{2,1,0:T(8,128)(2,1)S(1)}, bf16[2,192,384]{2,1,0:T(8,128)(2,1)S(1)}, u32[]{:S(2)}, u32[]{:S(2)}) collective-permute-start(bf16[2,192,384]{2,1,0:T(8,128)(2,1)S(1)} %collective-permute-done), channel_id=1, source_target_pairs={{0,16},{1,5},{2,18},{3,7},{4,20},{5,1},{6,22},{7,3},{8,24},{9,13},... | collective-permute-start | bytes 884744 | tf_op jit(solution)/shard_map/ppermute | solution.py:32
  22.4 7.9 %collective-permute-start.3 = (bf16[2,192,384]{2,1,0:T(8,128)(2,1)S(1)}, bf16[2,192,384]{2,1,0:T(8,128)(2,1)S(1)}, u32[]{:S(2)}, u32[]{:S(2)}) collective-permute-start(bf16[2,192,384]{2,1,0:T(8,128)(2,1)S(1)} %collective-permute-done), channel_id=1, source_target_pairs={{0,24},{1,7},{2,26},{3,1},{4,28},{5,3},{6,30},{7,5},{8,0},{9,15},{... | collective-permute-start | bytes 884744 | tf_op jit(solution)/shard_map/ppermute | solution.py:32
  30.5 11.6 %collective-permute-start.4 = (bf16[4,192,384]{2,1,0:T(8,128)(2,1)S(1)}, bf16[4,192,384]{2,1,0:T(8,128)(2,1)S(1)}, u32[]{:S(2)}, u32[]{:S(2)}) collective-permute-start(bf16[4,192,384]{2,1,0:T(8,128)(2,1)S(1)} %get-tuple-element.65), channel_id=1, source_target_pairs={{0,4},{1,17},{2,6},{3,19},{4,0},{5,21},{6,2},{7,23},{8,12},{9,25},... | collective-permute-start | bytes 1769480 | tf_op jit(solution)/shard_map/ppermute | solution.py:32
  33.8 14.5 %collective-permute-start.8 = (bf16[4,192,384]{2,1,0:T(8,128)(2,1)S(1)}, bf16[4,192,384]{2,1,0:T(8,128)(2,1)S(1)}, u32[]{:S(2)}, u32[]{:S(2)}) collective-permute-start(bf16[4,192,384]{2,1,0:T(8,128)(2,1)S(1)} %get-tuple-element.65), channel_id=1, source_target_pairs={{0,2},{1,9},{2,4},{3,11},{4,6},{5,13},{6,0},{7,15},{8,10},{9,17},{... | collective-permute-start | bytes 1769480 | tf_op jit(solution)/shard_map/ppermute | solution.py:32
  34.7 14.2 %collective-permute-start.9 = (bf16[4,192,384]{2,1,0:T(8,128)(2,1)S(1)}, bf16[4,192,384]{2,1,0:T(8,128)(2,1)S(1)}, u32[]{:S(2)}, u32[]{:S(2)}) collective-permute-start(bf16[4,192,384]{2,1,0:T(8,128)(2,1)S(1)} %get-tuple-element.65), channel_id=1, source_target_pairs={{0,6},{1,25},{2,0},{3,27},{4,2},{5,29},{6,4},{7,31},{8,14},{9,1},{... | collective-permute-start | bytes 1769480 | tf_op jit(solution)/shard_map/ppermute | solution.py:32
  49.3 7.2 %collective-permute-start.10 = (bf16[4,4,192,384]{3,2,1,0:T(8,128)(2,1)S(1)}, bf16[4,4,192,384]{3,2,1,0:T(8,128)(2,1)}, u32[]{:S(2)}, u32[]{:S(2)}) collective-permute-start(bf16[4,4,192,384]{3,2,1,0:T(8,128)(2,1)S(1)} %pad_maximum_fusion.refs_0_), channel_id=1, source_target_pairs={{0,1},{1,0},{2,3},{3,2},{4,5},{5,4},{6,7},{7,6},{8,9},{9,8},{10,11... | collective-permute-start | bytes 7077896 | tf_op jit(solution)/shard_map/ppermute | solution.py:43
  49.4 1.5 copy-start.2
  51.8 16.5 %collective-permute-start.5 = (bf16[4,192,384]{2,1,0:T(8,128)(2,1)}, bf16[4,192,384]{2,1,0:T(8,128)(2,1)}, u32[]{:S(2)}, u32[]{:S(2)}) collective-permute-start(bf16[4,192,384]{2,1,0:T(8,128)(2,1)} %pad_maximum_fusion.5), channel_id=1, source_target_pairs={{0,2},{1,9},{2,4},{3,11},{4,6},{5,13},{6,0},{7,15},{8,10},{9,17},{... | collective-permute-start | bytes 1769480 | tf_op jit(solution)/shard_map/ppermute | solution.py:32
  52.9 17.5 %collective-permute-start.6 = (bf16[4,192,384]{2,1,0:T(8,128)(2,1)}, bf16[4,192,384]{2,1,0:T(8,128)(2,1)}, u32[]{:S(2)}, u32[]{:S(2)}) collective-permute-start(bf16[4,192,384]{2,1,0:T(8,128)(2,1)} %pad_maximum_fusion.5), channel_id=1, source_target_pairs={{0,4},{1,17},{2,6},{3,19},{4,0},{5,21},{6,2},{7,23},{8,12},{9,25},... | collective-permute-start | bytes 1769480 | tf_op jit(solution)/shard_map/ppermute | solution.py:32
  55.9 14.5 %collective-permute-start.7 = (bf16[4,192,384]{2,1,0:T(8,128)(2,1)}, bf16[4,192,384]{2,1,0:T(8,128)(2,1)}, u32[]{:S(2)}, u32[]{:S(2)}) collective-permute-start(bf16[4,192,384]{2,1,0:T(8,128)(2,1)} %pad_maximum_fusion.5), channel_id=1, source_target_pairs={{0,6},{1,25},{2,0},{3,27},{4,2},{5,29},{6,4},{7,31},{8,14},{9,1},{... | collective-permute-start | bytes 1769480 | tf_op jit(solution)/shard_map/ppermute | solution.py:32
  56.5 1.7 copy-start.3
  58.2 1.4 copy-start.6
  59.6 1.4 copy-start.9
  68.2 5.5 %copy-start.13 = (bf16[4,1536,384]{2,1,0:T(8,128)(2,1)}, bf16[4,1536,384]{2,1,0:T(8,128)(2,1)S(1)}, u32[]{:S(2)}) copy-start(bf16[4,1536,384]{2,1,0:T(8,128)(2,1)S(1)} %get-tuple-element.32.x) | copy-start | bytes 14155780
  73.8 19.6 %collective-permute-start.11 = (bf16[4,4,192,384]{3,2,1,0:T(8,128)(2,1)}, bf16[4,4,192,384]{3,2,1,0:T(8,128)(2,1)}, u32[]{:S(2)}, u32[]{:S(2)}) collective-permute-start(bf16[4,4,192,384]{3,2,1,0:T(8,128)(2,1)} %pad_maximum_fusion.1.refs_0_), channel_id=1, source_target_pairs={{0,1},{1,0},{2,3},{3,2},{4,5},{5,4},{6,7},{7,6},{8,9},{9,8},{10,11... | collective-permute-start | bytes 7077896 | tf_op jit(solution)/shard_map/ppermute | solution.py:43
  74.0 14.1 %collective-permute-start.16 = (bf16[512,384]{1,0:T(8,128)(2,1)S(1)}, bf16[512,384]{1,0:T(8,128)(2,1)S(1)}, u32[]{:S(2)}, u32[]{:S(2)}) collective-permute-start(bf16[512,384]{1,0:T(8,128)(2,1)S(1)} %get-tuple-element.44), channel_id=1, source_target_pairs={{0,32},{32,64},{64,96},{96,0},{1,33},{33,65},{65,97},{97,1},{2,34}... | collective-permute-start | bytes 1179656 | tf_op jit(solution)/shard_map/ppermute | solution.py:47
  75.2 12.9 %collective-permute-start.18 = (bf16[512,384]{1,0:T(8,128)(2,1)S(1)}, bf16[512,384]{1,0:T(8,128)(2,1)S(1)}, u32[]{:S(2)}, u32[]{:S(2)}) collective-permute-start(bf16[512,384]{1,0:T(8,128)(2,1)S(1)} %get-tuple-element.46), channel_id=1, source_target_pairs={{0,96},{32,0},{64,32},{96,64},{1,97},{33,1},{65,33},{97,65},{2,98}... | collective-permute-start | bytes 1179656 | tf_op jit(solution)/shard_map/ppermute | solution.py:47
  88.2 5.2 %copy-start.5 = (bf16[1536,512]{1,0:T(8,128)(2,1)S(1)}, bf16[1536,512]{1,0:T(8,128)(2,1)}, u32[]{:S(2)}) copy-start(bf16[1536,512]{1,0:T(8,128)(2,1)} %refs_2_.3) | copy-start | bytes 4718596
  89.2 30.0 %collective-permute-start.17 = (bf16[2,512,384]{2,1,0:T(8,128)(2,1)}, bf16[2,512,384]{2,1,0:T(8,128)(2,1)}, u32[]{:S(2)}, u32[]{:S(2)}) collective-permute-start(bf16[2,512,384]{2,1,0:T(8,128)(2,1)} %pad_maximum_fusion.2), channel_id=1, source_target_pairs={{0,32},{32,64},{64,96},{96,0},{1,33},{33,65},{65,97},{97,1},{2,34}... | collective-permute-start | bytes 2359304 | tf_op jit(solution)/shard_map/ppermute | solution.py:47
  91.3 27.9 %collective-permute-start.19 = (bf16[2,512,384]{2,1,0:T(8,128)(2,1)}, bf16[2,512,384]{2,1,0:T(8,128)(2,1)}, u32[]{:S(2)}, u32[]{:S(2)}) collective-permute-start(bf16[2,512,384]{2,1,0:T(8,128)(2,1)} %pad_maximum_fusion.3), channel_id=1, source_target_pairs={{0,96},{32,0},{64,32},{96,64},{1,97},{33,1},{65,33},{97,65},{2,98}... | collective-permute-start | bytes 2359304 | tf_op jit(solution)/shard_map/ppermute | solution.py:47
  98.9 2.2 copy-start.12
  101.0 13.7 %copy-start.4 = (bf16[4,1,512,384]{3,2,1,0:T(8,128)(2,1)}, bf16[4,1,512,384]{3,2,1,0:T(8,128)(2,1)S(1)}, u32[]{:S(2)}) copy-start(bf16[4,1,512,384]{3,2,1,0:T(8,128)(2,1)S(1)} %get-tuple-element.29) | copy-start | bytes 4718596
  101.1 13.1 %collective-permute-start.12 = (bf16[256,384]{1,0:T(8,128)(2,1)S(1)}, bf16[256,384]{1,0:T(8,128)(2,1)S(1)}, u32[]{:S(2)}, u32[]{:S(2)}) collective-permute-start(bf16[256,384]{1,0:T(8,128)(2,1)S(1)} %get-tuple-element.57), channel_id=1, source_target_pairs={{0,32},{32,64},{64,96},{96,0},{1,33},{33,65},{65,97},{97,1},{2,34}... | collective-permute-start | bytes 589832 | tf_op jit(solution)/shard_map/ppermute | solution.py:47
  101.2 13.4 %collective-permute-start.14 = (bf16[256,384]{1,0:T(8,128)(2,1)S(1)}, bf16[256,384]{1,0:T(8,128)(2,1)S(1)}, u32[]{:S(2)}, u32[]{:S(2)}) collective-permute-start(bf16[256,384]{1,0:T(8,128)(2,1)S(1)} %get-tuple-element.59), channel_id=1, source_target_pairs={{0,96},{32,0},{64,32},{96,64},{1,97},{33,1},{65,33},{97,65},{2,98}... | collective-permute-start | bytes 589832 | tf_op jit(solution)/shard_map/ppermute | solution.py:47
  114.7 11.7 %collective-permute-start.13 = (bf16[2,256,384]{2,1,0:T(8,128)(2,1)S(1)}, bf16[2,256,384]{2,1,0:T(8,128)(2,1)}, u32[]{:S(2)}, u32[]{:S(2)}) collective-permute-start(bf16[2,256,384]{2,1,0:T(8,128)(2,1)S(1)} %pad_maximum_fusion.7), channel_id=1, source_target_pairs={{0,32},{32,64},{64,96},{96,0},{1,33},{33,65},{65,97},{97,1},{2,34}... | collective-permute-start | bytes 1179656 | tf_op jit(solution)/shard_map/ppermute | solution.py:47
  117.2 9.6 %collective-permute-start.15 = (bf16[2,256,384]{2,1,0:T(8,128)(2,1)}, bf16[2,256,384]{2,1,0:T(8,128)(2,1)}, u32[]{:S(2)}, u32[]{:S(2)}) collective-permute-start(bf16[2,256,384]{2,1,0:T(8,128)(2,1)} %pad_maximum_fusion.8), channel_id=1, source_target_pairs={{0,96},{32,0},{64,32},{96,64},{1,97},{33,1},{65,33},{97,65},{2,98}... | collective-permute-start | bytes 1179656 | tf_op jit(solution)/shard_map/ppermute | solution.py:47
  129.6 0.7 copy-start.14
  131.4 19.5 %collective-permute-start.20 = (bf16[2,512,384]{2,1,0:T(8,128)(2,1)}, bf16[2,512,384]{2,1,0:T(8,128)(2,1)}, u32[]{:S(2)}, u32[]{:S(2)}) collective-permute-start(bf16[2,512,384]{2,1,0:T(8,128)(2,1)} %pad_maximum_fusion.4), channel_id=1, source_target_pairs={{0,32},{32,64},{64,96},{96,0},{1,33},{33,65},{65,97},{97,1},{2,34}... | collective-permute-start | bytes 2359304 | tf_op jit(solution)/shard_map/ppermute | solution.py:47
  133.2 18.8 %collective-permute-start.21 = (bf16[2,512,384]{2,1,0:T(8,128)(2,1)}, bf16[2,512,384]{2,1,0:T(8,128)(2,1)}, u32[]{:S(2)}, u32[]{:S(2)}) collective-permute-start(bf16[2,512,384]{2,1,0:T(8,128)(2,1)} %pad_maximum_fusion.4), channel_id=1, source_target_pairs={{0,96},{32,0},{64,32},{96,64},{1,97},{33,1},{65,33},{97,65},{2,98}... | collective-permute-start | bytes 2359304 | tf_op jit(solution)/shard_map/ppermute | solution.py:47
  135.0 1.0 copy-start.15
  151.9 9.5 %collective-permute-start.22 = (bf16[512,384]{1,0:T(8,128)(2,1)S(1)}, bf16[512,384]{1,0:T(8,128)(2,1)S(1)}, u32[]{:S(2)}, u32[]{:S(2)}) collective-permute-start(bf16[512,384]{1,0:T(8,128)(2,1)S(1)} %slice_bitcast_fusion.1), channel_id=1, source_target_pairs={{0,32},{32,64},{64,96},{96,0},{1,33},{33,65},{65,97},{97,1},{2,34}... | collective-permute-start | bytes 1179656 | tf_op jit(solution)/shard_map/ppermute | solution.py:47
  153.0 8.7 %collective-permute-start.23 = (bf16[512,384]{1,0:T(8,128)(2,1)S(1)}, bf16[512,384]{1,0:T(8,128)(2,1)S(1)}, u32[]{:S(2)}, u32[]{:S(2)}) collective-permute-start(bf16[512,384]{1,0:T(8,128)(2,1)S(1)} %slice_bitcast_fusion), channel_id=1, source_target_pairs={{0,96},{32,0},{64,32},{96,64},{1,97},{33,1},{65,33},{97,65},{2,98}... | collective-permute-start | bytes 1179656 | tf_op jit(solution)/shard_map/ppermute | solution.py:47
  157.6 4.3 %copy-start.7 = (bf16[1536,512]{1,0:T(8,128)(2,1)S(1)}, bf16[1536,512]{1,0:T(8,128)(2,1)}, u32[]{:S(2)}) copy-start(bf16[1536,512]{1,0:T(8,128)(2,1)} %wg.3) | copy-start | bytes 4718596
  157.6 4.3 %copy-start.10 = (bf16[1536,512]{1,0:T(8,128)(2,1)S(1)}, bf16[1536,512]{1,0:T(8,128)(2,1)}, u32[]{:S(2)}) copy-start(bf16[1536,512]{1,0:T(8,128)(2,1)} %wu.3) | copy-start | bytes 4718596
  166.0 9.8 %collective-permute-start.24 = (bf16[16,192,384]{2,1,0:T(8,128)(2,1)}, bf16[16,192,384]{2,1,0:T(8,128)(2,1)}, u32[]{:S(2)}, u32[]{:S(2)}) collective-permute-start(bf16[16,192,384]{2,1,0:T(8,128)(2,1)} %slot_partials.3), channel_id=1, source_target_pairs={{0,1},{1,0},{2,3},{3,2},{4,5},{5,4},{6,7},{7,6},{8,9},{9,8},{10,11... | collective-permute-start | bytes 7077896 | tf_op jit(solution)/shard_map/ppermute | solution.py:43
  166.0 5.8 %copy-start.8 = (bf16[1536,512]{1,0:T(8,128)(2,1)S(1)}, bf16[1536,512]{1,0:T(8,128)(2,1)}, u32[]{:S(2)}) copy-start(bf16[1536,512]{1,0:T(8,128)(2,1)} %wg.3) | copy-start | bytes 4718596
  167.7 29.4 %collective-permute-start.32 = (bf16[2,256,384]{2,1,0:T(8,128)(2,1)S(1)}, bf16[2,256,384]{2,1,0:T(8,128)(2,1)S(1)}, u32[]{:S(2)}, u32[]{:S(2)}) collective-permute-start(bf16[2,256,384]{2,1,0:T(8,128)(2,1)S(1)} %multiply_convert_fusion), channel_id=1, source_target_pairs={{0,32},{32,64},{64,96},{96,0},{1,33},{33,65},{65,97},{97,1},{2,34}... | collective-permute-start | bytes 1179656 | tf_op jit(solution)/shard_map/ppermute | solution.py:47
  168.2 28.9 %collective-permute-start.33 = (bf16[2,256,384]{2,1,0:T(8,128)(2,1)S(1)}, bf16[2,256,384]{2,1,0:T(8,128)(2,1)S(1)}, u32[]{:S(2)}, u32[]{:S(2)}) collective-permute-start(bf16[2,256,384]{2,1,0:T(8,128)(2,1)S(1)} %multiply_convert_fusion), channel_id=1, source_target_pairs={{0,96},{32,0},{64,32},{96,64},{1,97},{33,1},{65,33},{97,65},{2,98}... | collective-permute-start | bytes 1179656 | tf_op jit(solution)/shard_map/ppermute | solution.py:47
  171.8 1.4 copy-start.11
  173.2 10.2 %slice-start.2 = ((s8[4718592]{0:T(1024)(128)(4,1)}), s8[4194304]{0:T(1024)(128)(4,1)S(1)}, s32[]{:S(2)}) async-start(s8[4718592]{0:T(1024)(128)(4,1)} %bitcast.155), calls=%async_computation.2 | async-start | bytes 8388608
  175.8 7.6 %slice-start.3 = ((s8[4718592]{0:T(1024)(128)(4,1)}), s8[524288]{0:T(1024)(128)(4,1)S(1)}, s32[]{:S(2)}) async-start(s8[4718592]{0:T(1024)(128)(4,1)} %bitcast.155), calls=%async_computation.3 | async-start | bytes 1048576
  178.4 12.3 %collective-permute-start.25 = (bf16[4,192,384]{2,1,0:T(8,128)(2,1)S(1)}, bf16[4,192,384]{2,1,0:T(8,128)(2,1)S(1)}, u32[]{:S(2)}, u32[]{:S(2)}) collective-permute-start(bf16[4,192,384]{2,1,0:T(8,128)(2,1)S(1)} %get-tuple-element.48), channel_id=1, source_target_pairs={{0,2},{1,9},{2,4},{3,11},{4,6},{5,13},{6,0},{7,15},{8,10},{9,17},{... | collective-permute-start | bytes 1769480 | tf_op jit(solution)/shard_map/ppermute | solution.py:32
  179.8 16.9 %collective-permute-start.26 = (bf16[4,192,384]{2,1,0:T(8,128)(2,1)S(1)}, bf16[4,192,384]{2,1,0:T(8,128)(2,1)S(1)}, u32[]{:S(2)}, u32[]{:S(2)}) collective-permute-start(bf16[4,192,384]{2,1,0:T(8,128)(2,1)S(1)} %get-tuple-element.50), channel_id=1, source_target_pairs={{0,4},{1,17},{2,6},{3,19},{4,0},{5,21},{6,2},{7,23},{8,12},{9,25},... | collective-permute-start | bytes 1769480 | tf_op jit(solution)/shard_map/ppermute | solution.py:32
  182.6 14.2 %collective-permute-start.27 = (bf16[4,192,384]{2,1,0:T(8,128)(2,1)S(1)}, bf16[4,192,384]{2,1,0:T(8,128)(2,1)S(1)}, u32[]{:S(2)}, u32[]{:S(2)}) collective-permute-start(bf16[4,192,384]{2,1,0:T(8,128)(2,1)S(1)} %get-tuple-element.49), channel_id=1, source_target_pairs={{0,6},{1,25},{2,0},{3,27},{4,2},{5,29},{6,4},{7,31},{8,14},{9,1},{... | collective-permute-start | bytes 1769480 | tf_op jit(solution)/shard_map/ppermute | solution.py:32
  183.1 29.7 %slice-start = ((s8[4718592]{0:T(1024)(128)(4,1)}), s8[4194304]{0:T(1024)(128)(4,1)S(1)}, s32[]{:S(2)}) async-start(s8[4718592]{0:T(1024)(128)(4,1)} %bitcast.153), calls=%async_computation | async-start | bytes 8388608
  183.4 29.4 %slice-start.1 = ((s8[4718592]{0:T(1024)(128)(4,1)}), s8[524288]{0:T(1024)(128)(4,1)S(1)}, s32[]{:S(2)}) async-start(s8[4718592]{0:T(1024)(128)(4,1)} %bitcast.153), calls=%async_computation.1 | async-start | bytes 1048576
  197.2 15.5 %collective-permute-start.34 = (bf16[256,384]{1,0:T(8,128)(2,1)S(1)}, bf16[256,384]{1,0:T(8,128)(2,1)S(1)}, u32[]{:S(2)}, u32[]{:S(2)}) collective-permute-start(bf16[256,384]{1,0:T(8,128)(2,1)S(1)} %slice_bitcast_fusion.3), channel_id=1, source_target_pairs={{0,32},{32,64},{64,96},{96,0},{1,33},{33,65},{65,97},{97,1},{2,34}... | collective-permute-start | bytes 589832 | tf_op jit(solution)/shard_map/ppermute | solution.py:47
  197.3 15.4 %collective-permute-start.35 = (bf16[256,384]{1,0:T(8,128)(2,1)S(1)}, bf16[256,384]{1,0:T(8,128)(2,1)S(1)}, u32[]{:S(2)}, u32[]{:S(2)}) collective-permute-start(bf16[256,384]{1,0:T(8,128)(2,1)S(1)} %slice_bitcast_fusion.2), channel_id=1, source_target_pairs={{0,96},{32,0},{64,32},{96,64},{1,97},{33,1},{65,33},{97,65},{2,98}... | collective-permute-start | bytes 589832 | tf_op jit(solution)/shard_map/ppermute | solution.py:47
  200.7 5.2 %collective-permute-start.28 = (bf16[192,384]{1,0:T(8,128)(2,1)S(1)}, bf16[192,384]{1,0:T(8,128)(2,1)S(1)}, u32[]{:S(2)}, u32[]{:S(2)}) collective-permute-start(bf16[192,384]{1,0:T(8,128)(2,1)S(1)} %get-tuple-element.61), channel_id=1, source_target_pairs={{0,8},{1,3},{2,10},{3,5},{4,12},{5,7},{6,14},{7,1},{8,16},{9,11},{... | collective-permute-start | bytes 442376 | tf_op jit(solution)/shard_map/ppermute | solution.py:32
  202.0 6.7 %collective-permute-start.29 = (bf16[192,384]{1,0:T(8,128)(2,1)S(1)}, bf16[192,384]{1,0:T(8,128)(2,1)S(1)}, u32[]{:S(2)}, u32[]{:S(2)}) collective-permute-start(bf16[192,384]{1,0:T(8,128)(2,1)S(1)} %get-tuple-element.63), channel_id=1, source_target_pairs={{0,16},{1,5},{2,18},{3,7},{4,20},{5,1},{6,22},{7,3},{8,24},{9,13},... | collective-permute-start | bytes 442376 | tf_op jit(solution)/shard_map/ppermute | solution.py:32
  203.1 7.1 %collective-permute-start.30 = (bf16[192,384]{1,0:T(8,128)(2,1)S(1)}, bf16[192,384]{1,0:T(8,128)(2,1)S(1)}, u32[]{:S(2)}, u32[]{:S(2)}) collective-permute-start(bf16[192,384]{1,0:T(8,128)(2,1)S(1)} %get-tuple-element.62), channel_id=1, source_target_pairs={{0,24},{1,7},{2,26},{3,1},{4,28},{5,3},{6,30},{7,5},{8,0},{9,15},{... | collective-permute-start | bytes 442376 | tf_op jit(solution)/shard_map/ppermute | solution.py:32
  210.3 10.6 %collective-permute-start.31 = (bf16[192,384]{1,0:T(8,128)(2,1)S(1)}, bf16[192,384]{1,0:T(8,128)(2,1)S(1)}, u32[]{:S(2)}, u32[]{:S(2)}) collective-permute-start(bf16[192,384]{1,0:T(8,128)(2,1)S(1)} %fusion.50), channel_id=1, source_target_pairs={{0,0},{1,1},{2,2},{3,3},{4,4},{5,5},{6,6},{7,7},{8,32},{9,33},{10,... | collective-permute-start | bytes 442376 | tf_op jit(solution)/shard_map/ppermute | solution.py:32
  212.8 9.2 %copy-start.1 = (bf16[768,192]{0,1:T(8,128)(2,1)S(1)}, bf16[768,192]{0,1:T(8,128)(2,1)}, u32[]{:S(2)}) copy-start(bf16[768,192]{0,1:T(8,128)(2,1)} %param.7) | copy-start | bytes 884740

commit v3 on v2

--- a/solution.py
+++ b/solution.py
@@ -173,13 +173,17 @@
     )(x, d)
 
 
-def sum_over_z(a, z):
+def start_sum_over_z(a, z):
     far = block(a, z + 2)
     up_half = along_z(far[0], 1)
     down_half = along_z(far[1], 3)
     right, left = block(a, z + 1), block(a, z + 3)
     right = jnp.stack([right[0] + up_half, right[1]])
     left = jnp.stack([left[0], left[1] + down_half])
+    return right, left
+
+
+def finish_sum_over_z(a, right, left, z):
     from_left, from_right = along_z(right, 1), along_z(left, 3)
     return block(a, z).astype(F32) + from_left.astype(F32) + from_right.astype(F32)
 
@@ -229,13 +233,16 @@
     x_sib = other_core(x_own)
     gu, xg = forward(where, x_own, x_sib, w_gate, w_up)
     dy_own = [dy_held] + [move(dy_held, shift("yx", j)) for j in range(1, N)]
-    dy_own, gu = lax.optimization_barrier((dy_own, gu))
+    right, left = start_sum_over_z(gu, z)
+    dy_own, _ = lax.optimization_barrier((dy_own, (right, left)))
     dy_own = jnp.stack(dy_own)
     dy_sib = other_core(dy_own)
     gh, dyg = forward(where, dy_own, dy_sib, w_down)
-    gate_up = sum_over_z(gu, z)
+    gate_up = finish_sum_over_z(gu, right, left, z)
     gate_pre, up_pre = gate_up[0], gate_up[1]
-    grad_hidden = sum_over_z(gh.reshape(N, 2, 256, CAP), z).reshape(512, CAP)
+    gh = gh.reshape(N, 2, 256, CAP)
+    right, left = start_sum_over_z(gh, z)
+    grad_hidden = finish_sum_over_z(gh, right, left, z).reshape(512, CAP)
 
     logistic = jax.nn.sigmoid(gate_pre)
     activated = gate_pre * logistic
@@ -246,13 +253,12 @@
     dgu = jnp.stack([dgate, dup])
     near = neighbours_over_z(dgu)
     dgu = gather_over_z(dgu, near, z)
-    hidden, _ = lax.optimization_barrier((hidden.reshape(2, 256, CAP), near[0]))
-    hidden_near = neighbours_over_z(hidden)
-
     theirs = other_core(slot_partials(1 - core, w_gate, w_up, dgu))
     total = slot_partials(core, w_gate, w_up, dgu)
     total = sum_of((total, theirs)).astype(BF).reshape(N, N, 192, CAP)
     dgu, total = lax.optimization_barrier((dgu, total))
+    hidden, _ = lax.optimization_barrier((hidden.reshape(2, 256, CAP), total))
+    hidden_near = neighbours_over_z(hidden)
     total = plane_sum(total, jnp.where(core == 0, y, x), "yx")
     hidden_near, _ = lax.optimization_barrier((hidden_near, total))
     hidden_all = gather_over_z(hidden, hidden_near, z).reshape(N, 1, 512, CAP)

time: 223 us -> 226 us (1.013)
  waiting for transfers between devices: 89.3 us -> 94 us
  other arithmetic: 20.4 us -> 16.7 us
  local copies, waits for them, and re-layouts: 17.3 us -> 20.9 us
    ppermute x3, waiting for transfers between devices: 0.01 us -> 4.14 us  [other_core(): return lax.ppermute(a, 'core', [(0, 1), (1, 0)])]
    another operation x1, other arithmetic: 3.36 us -> 0.36 us  [per_device(): dy_own = jnp.stack(dy_own)]
    ppermute x17, waiting for transfers between devices: 46.1 us -> 49 us  [move(): return lax.ppermute(a, ('z', 'x', 'y', 'core'), every(function))]
    ppermute x16, waiting for transfers between devices: 43.2 us -> 40.9 us  [along_z(): return lax.ppermute(a, 'z', [(i, (i + k) % N) for i in range(N)])]
    unnamed x40 -> x44, local copies, waits for them, and re-layouts: 11.1 us -> 13.4 us
  transfers between devices with their start and end apart: 36 -> 36, of which waited for: 21 -> 22; matrix products, arithmetic and copies ran while one was open for 7% -> 6% of each run, Pallas kernels for 12% -> 8%
where the time goes in v3:
time: 226 us
  waiting for transfers between devices  94 us (42%)
  starting transfers between devices  60.2 us (27%)
  Pallas kernels  29.7 us (13%)
  local copies, waits for them, and re-layouts  20.9 us (9%)
  other arithmetic  16.7 us (7%)
  matrix products  2.99 us (1%)
    ppermute x17, waiting for transfers between devices, move(): return lax.ppermute(a, ('z', 'x', 'y', 'core'), every(function))  49 us
    ppermute x16, waiting for transfers between devices, along_z(): return lax.ppermute(a, 'z', [(i, (i + k) % N) for i in range(N)])  40.9 us
    ppermute x17, starting transfers between devices, move(): return lax.ppermute(a, ('z', 'x', 'y', 'core'), every(function))  31.1 us
    ppermute x16, starting transfers between devices, along_z(): return lax.ppermute(a, 'z', [(i, (i + k) % N) for i in range(N)])  29 us
    unnamed x44, local copies, waits for them, and re-layouts  13.4 us
    pallas_call x2, Pallas kernels, weight_grads(): pl.pallas_call(weight_kernel, grid=(1536 // rows,), out_shape=[jax.ShapeD...  12.2 us
    pallas_call x2, Pallas kernels, forward(): pl.pallas_call(functools.partial(forward_kernel, count), out_shape=(jax.S...  10.9 us
    pallas_call x2, Pallas kernels, slot_partials(): pl.pallas_call(slot_kernel, out_shape=jax.ShapeDtypeStruct((N * N, 192, C...  6.61 us
  transfers between devices with their start and end apart: 36, of which 22 were waited for; matrix products, arithmetic and copies ran while one was open for 6% of the time, Pallas kernels for 8%

profile of v3, /device:TPU:6, one launch (start us, length us, event | category | flops | bytes accessed | tf_op | source)
XLA Modules:
  0.0 225.6 jit_solution(481966424860428037)
XLA Ops:
  3.5 1.4 fusion.25
  4.9 5.9 %collective-permute-start = (bf16[2,192,384]{2,1,0:T(8,128)(2,1)S(1)}, bf16[2,192,384]{2,1,0:T(8,128)(2,1)S(1)}, u32[]{:S(2)}, u32[]{:S(2)}) collective-permute-start(bf16[2,192,384]{2,1,0:T(8,128)(2,1)S(1)} %pad_maximum_fusion.9), channel_id=1, source_target_pairs={{0,0},{1,1},{2,2},{3,3},{4,4},{5,5},{6,6},{7,7},{8,40},{9,41},{10,... | collective-permute-start | bytes 884744 | tf_op jit(solution)/shard_map/ppermute | solution.py:32
  10.9 8.0 %collective-permute-done = bf16[2,192,384]{2,1,0:T(8,128)(2,1)S(1)} collective-permute-done((bf16[2,192,384]{2,1,0:T(8,128)(2,1)S(1)}, bf16[2,192,384]{2,1,0:T(8,128)(2,1)S(1)}, u32[]{:S(2)}, u32[]{:S(2)}) %collective-permute-start) | collective-permute-done | bytes 294944 | tf_op jit(solution)/shard_map/ppermute | solution.py:32
  18.9 3.5 %collective-permute-start.2 = (bf16[2,192,384]{2,1,0:T(8,128)(2,1)S(1)}, bf16[2,192,384]{2,1,0:T(8,128)(2,1)S(1)}, u32[]{:S(2)}, u32[]{:S(2)}) collective-permute-start(bf16[2,192,384]{2,1,0:T(8,128)(2,1)S(1)} %collective-permute-done), channel_id=1, source_target_pairs={{0,16},{1,5},{2,18},{3,7},{4,20},{5,1},{6,22},{7,3},{8,24},{9,13},... | collective-permute-start | bytes 884744 | tf_op jit(solution)/shard_map/ppermute | solution.py:32
  22.4 3.2 %collective-permute-done.1 = bf16[2,192,384]{2,1,0:T(8,128)(2,1)S(1)} collective-permute-done((bf16[2,192,384]{2,1,0:T(8,128)(2,1)S(1)}, bf16[2,192,384]{2,1,0:T(8,128)(2,1)S(1)}, u32[]{:S(2)}, u32[]{:S(2)}) %collective-permute-start.1) | collective-permute-done | bytes 294944 | tf_op jit(solution)/shard_map/ppermute | solution.py:32
  25.7 1.5 collective-permute-done.2
  27.8 2.5 %collective-permute-done.3 = bf16[2,192,384]{2,1,0:T(8,128)(2,1)S(1)} collective-permute-done((bf16[2,192,384]{2,1,0:T(8,128)(2,1)S(1)}, bf16[2,192,384]{2,1,0:T(8,128)(2,1)S(1)}, u32[]{:S(2)}, u32[]{:S(2)}) %collective-permute-start.3) | collective-permute-done | bytes 294944 | tf_op jit(solution)/shard_map/ppermute | solution.py:32
  31.1 3.3 %collective-permute-start.4 = (bf16[4,192,384]{2,1,0:T(8,128)(2,1)S(1)}, bf16[4,192,384]{2,1,0:T(8,128)(2,1)S(1)}, u32[]{:S(2)}, u32[]{:S(2)}) collective-permute-start(bf16[4,192,384]{2,1,0:T(8,128)(2,1)S(1)} %get-tuple-element.63), channel_id=1, source_target_pairs={{0,4},{1,17},{2,6},{3,19},{4,0},{5,21},{6,2},{7,23},{8,12},{9,25},... | collective-permute-start | bytes 1769480 | tf_op jit(solution)/shard_map/ppermute | solution.py:32
  35.1 2.6 %collective-permute-start.9 = (bf16[4,192,384]{2,1,0:T(8,128)(2,1)S(1)}, bf16[4,192,384]{2,1,0:T(8,128)(2,1)S(1)}, u32[]{:S(2)}, u32[]{:S(2)}) collective-permute-start(bf16[4,192,384]{2,1,0:T(8,128)(2,1)S(1)} %get-tuple-element.63), channel_id=1, source_target_pairs={{0,6},{1,25},{2,0},{3,27},{4,2},{5,29},{6,4},{7,31},{8,14},{9,1},{... | collective-permute-start | bytes 1769480 | tf_op jit(solution)/shard_map/ppermute | solution.py:32
  37.7 5.1 %collective-permute-done.4 = bf16[4,192,384]{2,1,0:T(8,128)(2,1)S(1)} collective-permute-done((bf16[4,192,384]{2,1,0:T(8,128)(2,1)S(1)}, bf16[4,192,384]{2,1,0:T(8,128)(2,1)S(1)}, u32[]{:S(2)}, u32[]{:S(2)}) %collective-permute-start.4) | collective-permute-done | bytes 589856 | tf_op jit(solution)/shard_map/ppermute | solution.py:32
  42.7 6.2 %collective-permute-done.8 = bf16[4,192,384]{2,1,0:T(8,128)(2,1)S(1)} collective-permute-done((bf16[4,192,384]{2,1,0:T(8,128)(2,1)S(1)}, bf16[4,192,384]{2,1,0:T(8,128)(2,1)S(1)}, u32[]{:S(2)}, u32[]{:S(2)}) %collective-permute-start.8) | collective-permute-done | bytes 589856 | tf_op jit(solution)/shard_map/ppermute | solution.py:32
  49.8 1.5 copy-done.2
  51.3 3.1 %collective-permute-done.10.refs_1_ = bf16[4,4,192,384]{3,2,1,0:T(8,128)(2,1)} collective-permute-done((bf16[4,4,192,384]{3,2,1,0:T(8,128)(2,1)S(1)}, bf16[4,4,192,384]{3,2,1,0:T(8,128)(2,1)}, u32[]{:S(2)}, u32[]{:S(2)}) %collective-permute-start.10) | collective-permute-done | bytes 2359328 | tf_op jit(solution)/shard_map/ppermute | solution.py:43
  54.4 1.7 copy-done.3
  56.1 1.4 copy-done.6
  57.5 1.4 copy-done.9
  58.9 7.2 %forward_2.1 = (bf16[4,2,512,384]{3,2,1,0:T(8,128)(2,1)S(1)}, bf16[4,1536,384]{2,1,0:T(8,128)(2,1)S(1)}) custom-call(s32[3]{0:T(128)S(1)} %pad_add_fusion.where, bf16[4,4,192,384]{3,2,1,0:T(8,128)(2,1)S(1)} %copy-done.3, bf16[4,4,192,384]{3,2,1,0:T(8,128)(2,1)} %collective-permute-done.10.refs_1_, bf16[1536,512]{1,0:T(8,128)(2,1)S(1)} %copy-done.6, ...), custom_call_target="tpu_custom_call" | custom-call | flops 4831838208 | bytes 15000000 | tf_op jit(solution)/shard_map/forward_2/pallas_call | solution.py:98
  66.1 2.2 copy-done.13
  68.5 1.5 collective-permute-start.11
  70.0 3.1 %collective-permute-start.12 = (bf16[512,384]{1,0:T(8,128)(2,1)S(1)}, bf16[512,384]{1,0:T(8,128)(2,1)S(1)}, u32[]{:S(2)}, u32[]{:S(2)}) collective-permute-start(bf16[512,384]{1,0:T(8,128)(2,1)S(1)} %get-tuple-element.42), channel_id=1, source_target_pairs={{0,96},{32,0},{64,32},{96,64},{1,97},{33,1},{65,33},{97,65},{2,98}... | collective-permute-start | bytes 1179656 | tf_op jit(solution)/shard_map/ppermute | solution.py:47
  73.2 1.4 collective-permute-start.5
  74.7 2.7 %collective-permute-start.6 = (bf16[4,192,384]{2,1,0:T(8,128)(2,1)S(1)}, bf16[4,192,384]{2,1,0:T(8,128)(2,1)S(1)}, u32[]{:S(2)}, u32[]{:S(2)}) collective-permute-start(bf16[4,192,384]{2,1,0:T(8,128)(2,1)S(1)} %pad_maximum_fusion.5), channel_id=1, source_target_pairs={{0,4},{1,17},{2,6},{3,19},{4,0},{5,21},{6,2},{7,23},{8,12},{9,25},... | collective-permute-start | bytes 1769480 | tf_op jit(solution)/shard_map/ppermute | solution.py:32
  78.0 4.5 %collective-permute-done.11 = bf16[512,384]{1,0:T(8,128)(2,1)S(1)} collective-permute-done((bf16[512,384]{1,0:T(8,128)(2,1)S(1)}, bf16[512,384]{1,0:T(8,128)(2,1)S(1)}, u32[]{:S(2)}, u32[]{:S(2)}) %collective-permute-start.11) | collective-permute-done | bytes 393248 | tf_op jit(solution)/shard_map/ppermute | solution.py:47
  82.6 1.0 pad_maximum_fusion.2
  84.5 7.1 %collective-permute-done.6 = bf16[4,192,384]{2,1,0:T(8,128)(2,1)S(1)} collective-permute-done((bf16[4,192,384]{2,1,0:T(8,128)(2,1)S(1)}, bf16[4,192,384]{2,1,0:T(8,128)(2,1)S(1)}, u32[]{:S(2)}, u32[]{:S(2)}) %collective-permute-start.6) | collective-permute-done | bytes 589856 | tf_op jit(solution)/shard_map/ppermute | solution.py:32
  92.3 3.2 %collective-permute-start.19 = (bf16[2,512,384]{2,1,0:T(8,128)(2,1)}, bf16[2,512,384]{2,1,0:T(8,128)(2,1)}, u32[]{:S(2)}, u32[]{:S(2)}) collective-permute-start(bf16[2,512,384]{2,1,0:T(8,128)(2,1)} %pad_maximum_fusion.3), channel_id=1, source_target_pairs={{0,96},{32,0},{64,32},{96,64},{1,97},{33,1},{65,33},{97,65},{2,98}... | collective-permute-start | bytes 2359304 | tf_op jit(solution)/shard_map/ppermute | solution.py:47
  95.6 1.0 collective-permute-done.13.refs_1_
  96.6 3.6 %forward_1.1 = (bf16[4,1,512,384]{3,2,1,0:T(8,128)(2,1)S(1)}, bf16[4,1536,384]{2,1,0:T(8,128)(2,1)S(1)}) custom-call(s32[3]{0:T(128)S(1)} %pad_add_fusion.where, bf16[4,4,192,384]{3,2,1,0:T(8,128)(2,1)S(1)} %pad_maximum_fusion.1.refs_0_, bf16[4,4,192,384]{3,2,1,0:T(8,128)(2,1)S(1)} %collective-permute-done.13.refs_1_, bf16[1536,512]{1,0:T(8,128)(2,1)S(1)} %copy-done.5), custom_call_target="tpu_custom_call" | custom-call | flops 2415919104 | bytes 10000000 | tf_op jit(solution)/shard_map/forward_1/pallas_call | solution.py:98
  100.3 2.2 copy-done.12
  102.6 3.2 %collective-permute-start.16 = (bf16[256,384]{1,0:T(8,128)(2,1)S(1)}, bf16[256,384]{1,0:T(8,128)(2,1)S(1)}, u32[]{:S(2)}, u32[]{:S(2)}) collective-permute-start(bf16[256,384]{1,0:T(8,128)(2,1)S(1)} %get-tuple-element.57), channel_id=1, source_target_pairs={{0,96},{32,0},{64,32},{96,64},{1,97},{33,1},{65,33},{97,65},{2,98}... | collective-permute-start | bytes 589832 | tf_op jit(solution)/shard_map/ppermute | solution.py:47
  105.8 11.8 %collective-permute-done.14 = bf16[256,384]{1,0:T(8,128)(2,1)S(1)} collective-permute-done((bf16[256,384]{1,0:T(8,128)(2,1)S(1)}, bf16[256,384]{1,0:T(8,128)(2,1)S(1)}, u32[]{:S(2)}, u32[]{:S(2)}) %collective-permute-start.14) | collective-permute-done | bytes 196640 | tf_op jit(solution)/shard_map/ppermute | solution.py:47
  118.8 3.1 %collective-permute-start.17 = (bf16[2,256,384]{2,1,0:T(8,128)(2,1)}, bf16[2,256,384]{2,1,0:T(8,128)(2,1)}, u32[]{:S(2)}, u32[]{:S(2)}) collective-permute-start(bf16[2,256,384]{2,1,0:T(8,128)(2,1)} %pad_maximum_fusion.8), channel_id=1, source_target_pairs={{0,96},{32,0},{64,32},{96,64},{1,97},{33,1},{65,33},{97,65},{2,98}... | collective-permute-start | bytes 1179656 | tf_op jit(solution)/shard_map/ppermute | solution.py:47
  121.9 1.6 fusion
  123.5 6.1 %collective-permute-done.15 = bf16[2,256,384]{2,1,0:T(8,128)(2,1)} collective-permute-done((bf16[2,256,384]{2,1,0:T(8,128)(2,1)S(1)}, bf16[2,256,384]{2,1,0:T(8,128)(2,1)}, u32[]{:S(2)}, u32[]{:S(2)}) %collective-permute-start.15) | collective-permute-done | bytes 393248 | tf_op jit(solution)/shard_map/ppermute | solution.py:47
  129.9 1.4 fusion.32
  131.3 1.5 fusion.35
  134.5 1.6 collective-permute-start.20
  136.1 2.1 collective-permute-start.21
  139.4 15.1 %collective-permute-done.20 = bf16[2,512,384]{2,1,0:T(8,128)(2,1)} collective-permute-done((bf16[2,512,384]{2,1,0:T(8,128)(2,1)}, bf16[2,512,384]{2,1,0:T(8,128)(2,1)}, u32[]{:S(2)}, u32[]{:S(2)}) %collective-permute-start.20) | collective-permute-done | bytes 786464 | tf_op jit(solution)/shard_map/ppermute | solution.py:47
  154.4 1.0 slice_bitcast_fusion.1
  155.6 1.0 slice_bitcast_fusion
  156.6 3.3 %collective-permute-start.23 = (bf16[512,384]{1,0:T(8,128)(2,1)S(1)}, bf16[512,384]{1,0:T(8,128)(2,1)S(1)}, u32[]{:S(2)}, u32[]{:S(2)}) collective-permute-start(bf16[512,384]{1,0:T(8,128)(2,1)S(1)} %slice_bitcast_fusion), channel_id=1, source_target_pairs={{0,96},{32,0},{64,32},{96,64},{1,97},{33,1},{65,33},{97,65},{2,98}... | collective-permute-start | bytes 1179656 | tf_op jit(solution)/shard_map/ppermute | solution.py:47
  159.9 1.3 bitcast_dynamic-update-slice_fusion.1
  161.2 1.4 bitcast_dynamic-update-slice_fusion
  162.6 2.7 %collective-permute-done.22 = bf16[512,384]{1,0:T(8,128)(2,1)S(1)} collective-permute-done((bf16[512,384]{1,0:T(8,128)(2,1)S(1)}, bf16[512,384]{1,0:T(8,128)(2,1)S(1)}, u32[]{:S(2)}, u32[]{:S(2)}) %collective-permute-start.22) | collective-permute-done | bytes 393248 | tf_op jit(solution)/shard_map/ppermute | solution.py:47
  165.9 4.0 %slot_partials.3 = bf16[16,192,384]{2,1,0:T(8,128)(2,1)} custom-call(s32[1]{0:T(128)} %bitcast.45.where, bf16[1536,512]{1,0:T(8,128)(2,1)S(1)} %copy-done.7, bf16[1536,512]{1,0:T(8,128)(2,1)S(1)} %copy-done.10, bf16[4,2,512,384]{3,2,1,0:T(8,128)(2,1)S(1)} %fusion.31.dgu.d), custom_call_target="tpu_custom_call" | custom-call | flops 2415919104 | bytes 9000000 | tf_op jit(solution)/shard_map/slot_partials/pallas_call | solution.py:137
  169.9 1.7 multiply_convert_fusion
  171.8 1.4 copy-done.11
  173.2 2.6 %slot_partials.2 = bf16[16,192,384]{2,1,0:T(8,128)(2,1)S(1)} custom-call(s32[1]{0:T(128)} %bitcast.2.where, bf16[1536,512]{1,0:T(8,128)(2,1)S(1)} %copy-done.8, bf16[1536,512]{1,0:T(8,128)(2,1)S(1)} %copy-done.11, bf16[4,2,512,384]{3,2,1,0:T(8,128)(2,1)S(1)} %fusion.31.dgu.d), custom_call_target="tpu_custom_call" | custom-call | flops 2415919104 | bytes 9000000 | tf_op jit(solution)/shard_map/slot_partials/pallas_call | solution.py:137
  175.8 2.5 %add_convert_fusion = bf16[16,192,384]{2,1,0:T(8,128)(2,1)S(1)} fusion(bf16[16,192,384]{2,1,0:T(8,128)(2,1)} %collective-permute-done.24, bf16[16,192,384]{2,1,0:T(8,128)(2,1)S(1)} %slot_partials.2), kind=kLoop, calls=%fused_computation | loop fusion | flops 4718592 | bytes 7077888 | tf_op jit(solution)/shard_map/convert_element_type | solution.py:258
  178.8 3.4 %collective-permute-start.33 = (bf16[2,256,384]{2,1,0:T(8,128)(2,1)S(1)}, bf16[2,256,384]{2,1,0:T(8,128)(2,1)S(1)}, u32[]{:S(2)}, u32[]{:S(2)}) collective-permute-start(bf16[2,256,384]{2,1,0:T(8,128)(2,1)S(1)} %multiply_convert_fusion), channel_id=1, source_target_pairs={{0,96},{32,0},{64,32},{96,64},{1,97},{33,1},{65,33},{97,65},{2,98}... | collective-permute-start | bytes 1179656 | tf_op jit(solution)/shard_map/ppermute | solution.py:47
  182.4 1.5 collective-permute-start.25
  183.8 2.7 %collective-permute-start.26 = (bf16[4,192,384]{2,1,0:T(8,128)(2,1)S(1)}, bf16[4,192,384]{2,1,0:T(8,128)(2,1)S(1)}, u32[]{:S(2)}, u32[]{:S(2)}) collective-permute-start(bf16[4,192,384]{2,1,0:T(8,128)(2,1)S(1)} %get-tuple-element.48), channel_id=1, source_target_pairs={{0,4},{1,17},{2,6},{3,19},{4,0},{5,21},{6,2},{7,23},{8,12},{9,25},... | collective-permute-start | bytes 1769480 | tf_op jit(solution)/shard_map/ppermute | solution.py:32
  187.1 7.3 %weight_grads_2.1 = (bf16[1536,512]{1,0:T(8,128)(2,1)}, bf16[1536,512]{1,0:T(8,128)(2,1)}) custom-call(bf16[4,1536,384]{2,1,0:T(8,128)(2,1)S(1)} %bitcast.156, bf16[4,2,512,384]{3,2,1,0:T(8,128)(2,1)S(1)} %fusion.31.dgu.d), custom_call_target="tpu_custom_call" | custom-call | flops 4831838208 | bytes 8000000 | tf_op jit(solution)/shard_map/weight_grads_2/pallas_call | solution.py:161
  194.7 6.0 %collective-permute-done.26 = bf16[4,192,384]{2,1,0:T(8,128)(2,1)S(1)} collective-permute-done((bf16[4,192,384]{2,1,0:T(8,128)(2,1)S(1)}, bf16[4,192,384]{2,1,0:T(8,128)(2,1)S(1)}, u32[]{:S(2)}, u32[]{:S(2)}) %collective-permute-start.26) | collective-permute-done | bytes 589856 | tf_op jit(solution)/shard_map/ppermute | solution.py:32
  201.3 3.3 %collective-permute-start.35 = (bf16[256,384]{1,0:T(8,128)(2,1)S(1)}, bf16[256,384]{1,0:T(8,128)(2,1)S(1)}, u32[]{:S(2)}, u32[]{:S(2)}) collective-permute-start(bf16[256,384]{1,0:T(8,128)(2,1)S(1)} %slice_bitcast_fusion.2), channel_id=1, source_target_pairs={{0,96},{32,0},{64,32},{96,64},{1,97},{33,1},{65,33},{97,65},{2,98}... | collective-permute-start | bytes 589832 | tf_op jit(solution)/shard_map/ppermute | solution.py:47
  205.6 1.9 collective-permute-start.29
  207.6 2.3 %collective-permute-done.28 = bf16[192,384]{1,0:T(8,128)(2,1)S(1)} collective-permute-done((bf16[192,384]{1,0:T(8,128)(2,1)S(1)}, bf16[192,384]{1,0:T(8,128)(2,1)S(1)}, u32[]{:S(2)}, u32[]{:S(2)}) %collective-permute-start.28) | collective-permute-done | bytes 147488 | tf_op jit(solution)/shard_map/ppermute | solution.py:32
  209.8 2.4 %collective-permute-done.29 = bf16[192,384]{1,0:T(8,128)(2,1)S(1)} collective-permute-done((bf16[192,384]{1,0:T(8,128)(2,1)S(1)}, bf16[192,384]{1,0:T(8,128)(2,1)S(1)}, u32[]{:S(2)}, u32[]{:S(2)}) %collective-permute-start.29) | collective-permute-done | bytes 147488 | tf_op jit(solution)/shard_map/ppermute | solution.py:32
  212.3 1.6 collective-permute-done.30
  213.9 2.8 %collective-permute-start.31 = (bf16[192,384]{1,0:T(8,128)(2,1)S(1)}, bf16[192,384]{1,0:T(8,128)(2,1)S(1)}, u32[]{:S(2)}, u32[]{:S(2)}) collective-permute-start(bf16[192,384]{1,0:T(8,128)(2,1)S(1)} %fusion.50), channel_id=1, source_target_pairs={{0,0},{1,1},{2,2},{3,3},{4,4},{5,5},{6,6},{7,7},{8,32},{9,33},{10,... | collective-permute-start | bytes 442376 | tf_op jit(solution)/shard_map/ppermute | solution.py:32
  216.9 4.9 %weight_grads_1.1 = bf16[1536,512]{1,0:T(8,128)(2,1)} custom-call(bf16[4,1536,384]{2,1,0:T(8,128)(2,1)S(1)} %bitcast.154, bf16[4,1,512,384]{3,2,1,0:T(8,128)(2,1)S(1)} %bitcast.152), custom_call_target="tpu_custom_call" | custom-call | flops 2415919104 | bytes 8000000 | tf_op jit(solution)/shard_map/weight_grads_1/pallas_call | solution.py:161
  221.8 2.7 %collective-permute-done.31 = bf16[192,384]{1,0:T(8,128)(2,1)S(1)} collective-permute-done((bf16[192,384]{1,0:T(8,128)(2,1)S(1)}, bf16[192,384]{1,0:T(8,128)(2,1)S(1)}, u32[]{:S(2)}, u32[]{:S(2)}) %collective-permute-start.31) | collective-permute-done | bytes 147488 | tf_op jit(solution)/shard_map/ppermute | solution.py:32
  224.5 1.1 convolution_convert_fusion
  (114 shorter events, 17.1 us)
Async XLA Ops:
  0.6 2.4 %copy-start = (bf16[768,192]{0,1:T(8,128)(2,1)S(1)}, bf16[768,192]{0,1:T(8,128)(2,1)}, u32[]{:S(2)}) copy-start(bf16[768,192]{0,1:T(8,128)(2,1)} %param.7) | copy-start | bytes 884740
  4.9 14.0 %collective-permute-start = (bf16[2,192,384]{2,1,0:T(8,128)(2,1)S(1)}, bf16[2,192,384]{2,1,0:T(8,128)(2,1)S(1)}, u32[]{:S(2)}, u32[]{:S(2)}) collective-permute-start(bf16[2,192,384]{2,1,0:T(8,128)(2,1)S(1)} %pad_maximum_fusion.9), channel_id=1, source_target_pairs={{0,0},{1,1},{2,2},{3,3},{4,4},{5,5},{6,6},{7,7},{8,40},{9,41},{10,... | collective-permute-start | bytes 884744 | tf_op jit(solution)/shard_map/ppermute | solution.py:32
  18.9 6.7 %collective-permute-start.1 = (bf16[2,192,384]{2,1,0:T(8,128)(2,1)S(1)}, bf16[2,192,384]{2,1,0:T(8,128)(2,1)S(1)}, u32[]{:S(2)}, u32[]{:S(2)}) collective-permute-start(bf16[2,192,384]{2,1,0:T(8,128)(2,1)S(1)} %collective-permute-done), channel_id=1, source_target_pairs={{0,8},{1,3},{2,10},{3,5},{4,12},{5,7},{6,14},{7,1},{8,16},{9,11},{... | collective-permute-start | bytes 884744 | tf_op jit(solution)/shard_map/ppermute | solution.py:32
  18.9 8.2 %collective-permute-start.2 = (bf16[2,192,384]{2,1,0:T(8,128)(2,1)S(1)}, bf16[2,192,384]{2,1,0:T(8,128)(2,1)S(1)}, u32[]{:S(2)}, u32[]{:S(2)}) collective-permute-start(bf16[2,192,384]{2,1,0:T(8,128)(2,1)S(1)} %collective-permute-done), channel_id=1, source_target_pairs={{0,16},{1,5},{2,18},{3,7},{4,20},{5,1},{6,22},{7,3},{8,24},{9,13},... | collective-permute-start | bytes 884744 | tf_op jit(solution)/shard_map/ppermute | solution.py:32
  22.4 7.9 %collective-permute-start.3 = (bf16[2,192,384]{2,1,0:T(8,128)(2,1)S(1)}, bf16[2,192,384]{2,1,0:T(8,128)(2,1)S(1)}, u32[]{:S(2)}, u32[]{:S(2)}) collective-permute-start(bf16[2,192,384]{2,1,0:T(8,128)(2,1)S(1)} %collective-permute-done), channel_id=1, source_target_pairs={{0,24},{1,7},{2,26},{3,1},{4,28},{5,3},{6,30},{7,5},{8,0},{9,15},{... | collective-permute-start | bytes 884744 | tf_op jit(solution)/shard_map/ppermute | solution.py:32
  31.1 11.6 %collective-permute-start.4 = (bf16[4,192,384]{2,1,0:T(8,128)(2,1)S(1)}, bf16[4,192,384]{2,1,0:T(8,128)(2,1)S(1)}, u32[]{:S(2)}, u32[]{:S(2)}) collective-permute-start(bf16[4,192,384]{2,1,0:T(8,128)(2,1)S(1)} %get-tuple-element.63), channel_id=1, source_target_pairs={{0,4},{1,17},{2,6},{3,19},{4,0},{5,21},{6,2},{7,23},{8,12},{9,25},... | collective-permute-start | bytes 1769480 | tf_op jit(solution)/shard_map/ppermute | solution.py:32
  34.4 14.5 %collective-permute-start.8 = (bf16[4,192,384]{2,1,0:T(8,128)(2,1)S(1)}, bf16[4,192,384]{2,1,0:T(8,128)(2,1)S(1)}, u32[]{:S(2)}, u32[]{:S(2)}) collective-permute-start(bf16[4,192,384]{2,1,0:T(8,128)(2,1)S(1)} %get-tuple-element.63), channel_id=1, source_target_pairs={{0,2},{1,9},{2,4},{3,11},{4,6},{5,13},{6,0},{7,15},{8,10},{9,17},{... | collective-permute-start | bytes 1769480 | tf_op jit(solution)/shard_map/ppermute | solution.py:32
  35.1 14.2 %collective-permute-start.9 = (bf16[4,192,384]{2,1,0:T(8,128)(2,1)S(1)}, bf16[4,192,384]{2,1,0:T(8,128)(2,1)S(1)}, u32[]{:S(2)}, u32[]{:S(2)}) collective-permute-start(bf16[4,192,384]{2,1,0:T(8,128)(2,1)S(1)} %get-tuple-element.63), channel_id=1, source_target_pairs={{0,6},{1,25},{2,0},{3,27},{4,2},{5,29},{6,4},{7,31},{8,14},{9,1},{... | collective-permute-start | bytes 1769480 | tf_op jit(solution)/shard_map/ppermute | solution.py:32
  49.7 4.7 %collective-permute-start.10 = (bf16[4,4,192,384]{3,2,1,0:T(8,128)(2,1)S(1)}, bf16[4,4,192,384]{3,2,1,0:T(8,128)(2,1)}, u32[]{:S(2)}, u32[]{:S(2)}) collective-permute-start(bf16[4,4,192,384]{3,2,1,0:T(8,128)(2,1)S(1)} %pad_maximum_fusion.refs_0_), channel_id=1, source_target_pairs={{0,1},{1,0},{2,3},{3,2},{4,5},{5,4},{6,7},{7,6},{8,9},{9,8},{10,11... | collective-permute-start | bytes 7077896 | tf_op jit(solution)/shard_map/ppermute | solution.py:43
  49.8 1.5 copy-start.2
  54.4 1.7 copy-start.3
  56.1 1.4 copy-start.6
  57.5 1.4 copy-start.9
  66.1 2.2 copy-start.13
  68.3 4.8 %copy-start.16 = (bf16[1,192,384]{2,1,0:T(8,128)(2,1)S(1)}, bf16[1,192,384]{2,1,0:T(8,128)(2,1)}, u32[]{:S(2)}) copy-start(bf16[1,192,384]{2,1,0:T(8,128)(2,1)} %get-tuple-element.69) | copy-start | bytes 442372
  68.3 4.8 %copy-start.17 = (bf16[1,192,384]{2,1,0:T(8,128)(2,1)S(1)}, bf16[1,192,384]{2,1,0:T(8,128)(2,1)}, u32[]{:S(2)}) copy-start(bf16[1,192,384]{2,1,0:T(8,128)(2,1)} %get-tuple-element.71) | copy-start | bytes 442372
  68.5 14.0 %collective-permute-start.11 = (bf16[512,384]{1,0:T(8,128)(2,1)S(1)}, bf16[512,384]{1,0:T(8,128)(2,1)S(1)}, u32[]{:S(2)}, u32[]{:S(2)}) collective-permute-start(bf16[512,384]{1,0:T(8,128)(2,1)S(1)} %get-tuple-element.41), channel_id=1, source_target_pairs={{0,32},{32,64},{64,96},{96,0},{1,33},{33,65},{65,97},{97,1},{2,34}... | collective-permute-start | bytes 1179656 | tf_op jit(solution)/shard_map/ppermute | solution.py:47
  70.0 12.5 %collective-permute-start.12 = (bf16[512,384]{1,0:T(8,128)(2,1)S(1)}, bf16[512,384]{1,0:T(8,128)(2,1)S(1)}, u32[]{:S(2)}, u32[]{:S(2)}) collective-permute-start(bf16[512,384]{1,0:T(8,128)(2,1)S(1)} %get-tuple-element.42), channel_id=1, source_target_pairs={{0,96},{32,0},{64,32},{96,64},{1,97},{33,1},{65,33},{97,65},{2,98}... | collective-permute-start | bytes 1179656 | tf_op jit(solution)/shard_map/ppermute | solution.py:47
  73.2 11.3 %collective-permute-start.5 = (bf16[4,192,384]{2,1,0:T(8,128)(2,1)S(1)}, bf16[4,192,384]{2,1,0:T(8,128)(2,1)S(1)}, u32[]{:S(2)}, u32[]{:S(2)}) collective-permute-start(bf16[4,192,384]{2,1,0:T(8,128)(2,1)S(1)} %pad_maximum_fusion.5), channel_id=1, source_target_pairs={{0,2},{1,9},{2,4},{3,11},{4,6},{5,13},{6,0},{7,15},{8,10},{9,17},{... | collective-permute-start | bytes 1769480 | tf_op jit(solution)/shard_map/ppermute | solution.py:32
  74.7 16.9 %collective-permute-start.6 = (bf16[4,192,384]{2,1,0:T(8,128)(2,1)S(1)}, bf16[4,192,384]{2,1,0:T(8,128)(2,1)S(1)}, u32[]{:S(2)}, u32[]{:S(2)}) collective-permute-start(bf16[4,192,384]{2,1,0:T(8,128)(2,1)S(1)} %pad_maximum_fusion.5), channel_id=1, source_target_pairs={{0,4},{1,17},{2,6},{3,19},{4,0},{5,21},{6,2},{7,23},{8,12},{9,25},... | collective-permute-start | bytes 1769480 | tf_op jit(solution)/shard_map/ppermute | solution.py:32
  77.4 14.2 %collective-permute-start.7 = (bf16[4,192,384]{2,1,0:T(8,128)(2,1)S(1)}, bf16[4,192,384]{2,1,0:T(8,128)(2,1)S(1)}, u32[]{:S(2)}, u32[]{:S(2)}) collective-permute-start(bf16[4,192,384]{2,1,0:T(8,128)(2,1)S(1)} %pad_maximum_fusion.5), channel_id=1, source_target_pairs={{0,6},{1,25},{2,0},{3,27},{4,2},{5,29},{6,4},{7,31},{8,14},{9,1},{... | collective-permute-start | bytes 1769480 | tf_op jit(solution)/shard_map/ppermute | solution.py:32
  91.6 5.0 %copy-start.5 = (bf16[1536,512]{1,0:T(8,128)(2,1)S(1)}, bf16[1536,512]{1,0:T(8,128)(2,1)}, u32[]{:S(2)}) copy-start(bf16[1536,512]{1,0:T(8,128)(2,1)} %refs_2_.3) | copy-start | bytes 4718596
  92.0 4.6 %collective-permute-start.13 = (bf16[4,4,192,384]{3,2,1,0:T(8,128)(2,1)S(1)}, bf16[4,4,192,384]{3,2,1,0:T(8,128)(2,1)S(1)}, u32[]{:S(2)}, u32[]{:S(2)}) collective-permute-start(bf16[4,4,192,384]{3,2,1,0:T(8,128)(2,1)S(1)} %pad_maximum_fusion.1.refs_0_), channel_id=1, source_target_pairs={{0,1},{1,0},{2,3},{3,2},{4,5},{5,4},{6,7},{7,6},{8,9},{9,8},{10,11... | collective-permute-start | bytes 7077896 | tf_op jit(solution)/shard_map/ppermute | solution.py:43
  92.1 29.8 %collective-permute-start.18 = (bf16[2,512,384]{2,1,0:T(8,128)(2,1)}, bf16[2,512,384]{2,1,0:T(8,128)(2,1)}, u32[]{:S(2)}, u32[]{:S(2)}) collective-permute-start(bf16[2,512,384]{2,1,0:T(8,128)(2,1)} %pad_maximum_fusion.2), channel_id=1, source_target_pairs={{0,32},{32,64},{64,96},{96,0},{1,33},{33,65},{65,97},{97,1},{2,34}... | collective-permute-start | bytes 2359304 | tf_op jit(solution)/shard_map/ppermute | solution.py:47
  92.3 29.6 %collective-permute-start.19 = (bf16[2,512,384]{2,1,0:T(8,128)(2,1)}, bf16[2,512,384]{2,1,0:T(8,128)(2,1)}, u32[]{:S(2)}, u32[]{:S(2)}) collective-permute-start(bf16[2,512,384]{2,1,0:T(8,128)(2,1)} %pad_maximum_fusion.3), channel_id=1, source_target_pairs={{0,96},{32,0},{64,32},{96,64},{1,97},{33,1},{65,33},{97,65},{2,98}... | collective-permute-start | bytes 2359304 | tf_op jit(solution)/shard_map/ppermute | solution.py:47
  100.3 2.2 copy-start.12
  102.4 15.3 %copy-start.4 = (bf16[4,1,512,384]{3,2,1,0:T(8,128)(2,1)}, bf16[4,1,512,384]{3,2,1,0:T(8,128)(2,1)S(1)}, u32[]{:S(2)}) copy-start(bf16[4,1,512,384]{3,2,1,0:T(8,128)(2,1)S(1)} %get-tuple-element.28) | copy-start | bytes 4718596
  102.5 15.1 %collective-permute-start.14 = (bf16[256,384]{1,0:T(8,128)(2,1)S(1)}, bf16[256,384]{1,0:T(8,128)(2,1)S(1)}, u32[]{:S(2)}, u32[]{:S(2)}) collective-permute-start(bf16[256,384]{1,0:T(8,128)(2,1)S(1)} %get-tuple-element.55), channel_id=1, source_target_pairs={{0,32},{32,64},{64,96},{96,0},{1,33},{33,65},{65,97},{97,1},{2,34}... | collective-permute-start | bytes 589832 | tf_op jit(solution)/shard_map/ppermute | solution.py:47
  102.6 15.1 %collective-permute-start.16 = (bf16[256,384]{1,0:T(8,128)(2,1)S(1)}, bf16[256,384]{1,0:T(8,128)(2,1)S(1)}, u32[]{:S(2)}, u32[]{:S(2)}) collective-permute-start(bf16[256,384]{1,0:T(8,128)(2,1)S(1)} %get-tuple-element.57), channel_id=1, source_target_pairs={{0,96},{32,0},{64,32},{96,64},{1,97},{33,1},{65,33},{97,65},{2,98}... | collective-permute-start | bytes 589832 | tf_op jit(solution)/shard_map/ppermute | solution.py:47
  117.8 11.8 %collective-permute-start.15 = (bf16[2,256,384]{2,1,0:T(8,128)(2,1)S(1)}, bf16[2,256,384]{2,1,0:T(8,128)(2,1)}, u32[]{:S(2)}, u32[]{:S(2)}) collective-permute-start(bf16[2,256,384]{2,1,0:T(8,128)(2,1)S(1)} %pad_maximum_fusion.7), channel_id=1, source_target_pairs={{0,32},{32,64},{64,96},{96,0},{1,33},{33,65},{65,97},{97,1},{2,34}... | collective-permute-start | bytes 1179656 | tf_op jit(solution)/shard_map/ppermute | solution.py:47
  118.8 11.1 %collective-permute-start.17 = (bf16[2,256,384]{2,1,0:T(8,128)(2,1)}, bf16[2,256,384]{2,1,0:T(8,128)(2,1)}, u32[]{:S(2)}, u32[]{:S(2)}) collective-permute-start(bf16[2,256,384]{2,1,0:T(8,128)(2,1)} %pad_maximum_fusion.8), channel_id=1, source_target_pairs={{0,96},{32,0},{64,32},{96,64},{1,97},{33,1},{65,33},{97,65},{2,98}... | collective-permute-start | bytes 1179656 | tf_op jit(solution)/shard_map/ppermute | solution.py:47
  132.8 0.7 copy-start.14
  134.5 19.9 %collective-permute-start.20 = (bf16[2,512,384]{2,1,0:T(8,128)(2,1)}, bf16[2,512,384]{2,1,0:T(8,128)(2,1)}, u32[]{:S(2)}, u32[]{:S(2)}) collective-permute-start(bf16[2,512,384]{2,1,0:T(8,128)(2,1)} %pad_maximum_fusion.4), channel_id=1, source_target_pairs={{0,32},{32,64},{64,96},{96,0},{1,33},{33,65},{65,97},{97,1},{2,34}... | collective-permute-start | bytes 2359304 | tf_op jit(solution)/shard_map/ppermute | solution.py:47
  136.1 19.5 %collective-permute-start.21 = (bf16[2,512,384]{2,1,0:T(8,128)(2,1)}, bf16[2,512,384]{2,1,0:T(8,128)(2,1)}, u32[]{:S(2)}, u32[]{:S(2)}) collective-permute-start(bf16[2,512,384]{2,1,0:T(8,128)(2,1)} %pad_maximum_fusion.4), channel_id=1, source_target_pairs={{0,96},{32,0},{64,32},{96,64},{1,97},{33,1},{65,33},{97,65},{2,98}... | collective-permute-start | bytes 2359304 | tf_op jit(solution)/shard_map/ppermute | solution.py:47
  138.2 1.0 copy-start.15
  155.5 9.9 %collective-permute-start.22 = (bf16[512,384]{1,0:T(8,128)(2,1)S(1)}, bf16[512,384]{1,0:T(8,128)(2,1)S(1)}, u32[]{:S(2)}, u32[]{:S(2)}) collective-permute-start(bf16[512,384]{1,0:T(8,128)(2,1)S(1)} %slice_bitcast_fusion.1), channel_id=1, source_target_pairs={{0,32},{32,64},{64,96},{96,0},{1,33},{33,65},{65,97},{97,1},{2,34}... | collective-permute-start | bytes 1179656 | tf_op jit(solution)/shard_map/ppermute | solution.py:47
  156.6 9.1 %collective-permute-start.23 = (bf16[512,384]{1,0:T(8,128)(2,1)S(1)}, bf16[512,384]{1,0:T(8,128)(2,1)S(1)}, u32[]{:S(2)}, u32[]{:S(2)}) collective-permute-start(bf16[512,384]{1,0:T(8,128)(2,1)S(1)} %slice_bitcast_fusion), channel_id=1, source_target_pairs={{0,96},{32,0},{64,32},{96,64},{1,97},{33,1},{65,33},{97,65},{2,98}... | collective-permute-start | bytes 1179656 | tf_op jit(solution)/shard_map/ppermute | solution.py:47
  161.2 4.7 %copy-start.7 = (bf16[1536,512]{1,0:T(8,128)(2,1)S(1)}, bf16[1536,512]{1,0:T(8,128)(2,1)}, u32[]{:S(2)}) copy-start(bf16[1536,512]{1,0:T(8,128)(2,1)} %wg.3) | copy-start | bytes 4718596
  161.2 4.7 %copy-start.10 = (bf16[1536,512]{1,0:T(8,128)(2,1)S(1)}, bf16[1536,512]{1,0:T(8,128)(2,1)}, u32[]{:S(2)}) copy-start(bf16[1536,512]{1,0:T(8,128)(2,1)} %wu.3) | copy-start | bytes 4718596
  169.9 5.9 %collective-permute-start.24 = (bf16[16,192,384]{2,1,0:T(8,128)(2,1)}, bf16[16,192,384]{2,1,0:T(8,128)(2,1)}, u32[]{:S(2)}, u32[]{:S(2)}) collective-permute-start(bf16[16,192,384]{2,1,0:T(8,128)(2,1)} %slot_partials.3), channel_id=1, source_target_pairs={{0,1},{1,0},{2,3},{3,2},{4,5},{5,4},{6,7},{7,6},{8,9},{9,8},{10,11... | collective-permute-start | bytes 7077896 | tf_op jit(solution)/shard_map/ppermute | solution.py:43
  169.9 1.9 copy-start.8
  171.8 1.4 copy-start.11
  173.2 13.9 %slice-start.2 = ((s8[4718592]{0:T(1024)(128)(4,1)}), s8[524288]{0:T(1024)(128)(4,1)S(1)}, s32[]{:S(2)}) async-start(s8[4718592]{0:T(1024)(128)(4,1)} %bitcast.155), calls=%async_computation.2 | async-start | bytes 1048576
  175.8 11.3 %slice-start.3 = ((s8[4718592]{0:T(1024)(128)(4,1)}), s8[4194304]{0:T(1024)(128)(4,1)S(1)}, s32[]{:S(2)}) async-start(s8[4718592]{0:T(1024)(128)(4,1)} %bitcast.155), calls=%async_computation.3 | async-start | bytes 8388608
  178.3 22.7 %collective-permute-start.32 = (bf16[2,256,384]{2,1,0:T(8,128)(2,1)S(1)}, bf16[2,256,384]{2,1,0:T(8,128)(2,1)S(1)}, u32[]{:S(2)}, u32[]{:S(2)}) collective-permute-start(bf16[2,256,384]{2,1,0:T(8,128)(2,1)S(1)} %multiply_convert_fusion), channel_id=1, source_target_pairs={{0,32},{32,64},{64,96},{96,0},{1,33},{33,65},{65,97},{97,1},{2,34}... | collective-permute-start | bytes 1179656 | tf_op jit(solution)/shard_map/ppermute | solution.py:47
  178.8 22.3 %collective-permute-start.33 = (bf16[2,256,384]{2,1,0:T(8,128)(2,1)S(1)}, bf16[2,256,384]{2,1,0:T(8,128)(2,1)S(1)}, u32[]{:S(2)}, u32[]{:S(2)}) collective-permute-start(bf16[2,256,384]{2,1,0:T(8,128)(2,1)S(1)} %multiply_convert_fusion), channel_id=1, source_target_pairs={{0,96},{32,0},{64,32},{96,64},{1,97},{33,1},{65,33},{97,65},{2,98}... | collective-permute-start | bytes 1179656 | tf_op jit(solution)/shard_map/ppermute | solution.py:47
  182.4 12.3 %collective-permute-start.25 = (bf16[4,192,384]{2,1,0:T(8,128)(2,1)S(1)}, bf16[4,192,384]{2,1,0:T(8,128)(2,1)S(1)}, u32[]{:S(2)}, u32[]{:S(2)}) collective-permute-start(bf16[4,192,384]{2,1,0:T(8,128)(2,1)S(1)} %get-tuple-element.46), channel_id=1, source_target_pairs={{0,2},{1,9},{2,4},{3,11},{4,6},{5,13},{6,0},{7,15},{8,10},{9,17},{... | collective-permute-start | bytes 1769480 | tf_op jit(solution)/shard_map/ppermute | solution.py:32
  183.8 16.9 %collective-permute-start.26 = (bf16[4,192,384]{2,1,0:T(8,128)(2,1)S(1)}, bf16[4,192,384]{2,1,0:T(8,128)(2,1)S(1)}, u32[]{:S(2)}, u32[]{:S(2)}) collective-permute-start(bf16[4,192,384]{2,1,0:T(8,128)(2,1)S(1)} %get-tuple-element.48), channel_id=1, source_target_pairs={{0,4},{1,17},{2,6},{3,19},{4,0},{5,21},{6,2},{7,23},{8,12},{9,25},... | collective-permute-start | bytes 1769480 | tf_op jit(solution)/shard_map/ppermute | solution.py:32
  186.6 14.2 %collective-permute-start.27 = (bf16[4,192,384]{2,1,0:T(8,128)(2,1)S(1)}, bf16[4,192,384]{2,1,0:T(8,128)(2,1)S(1)}, u32[]{:S(2)}, u32[]{:S(2)}) collective-permute-start(bf16[4,192,384]{2,1,0:T(8,128)(2,1)S(1)} %get-tuple-element.47), channel_id=1, source_target_pairs={{0,6},{1,25},{2,0},{3,27},{4,2},{5,29},{6,4},{7,31},{8,14},{9,1},{... | collective-permute-start | bytes 1769480 | tf_op jit(solution)/shard_map/ppermute | solution.py:32
  194.5 22.4 %slice-start = ((s8[4718592]{0:T(1024)(128)(4,1)}), s8[4194304]{0:T(1024)(128)(4,1)S(1)}, s32[]{:S(2)}) async-start(s8[4718592]{0:T(1024)(128)(4,1)} %bitcast.153), calls=%async_computation | async-start | bytes 8388608
  194.7 22.1 %slice-start.1 = ((s8[4718592]{0:T(1024)(128)(4,1)}), s8[524288]{0:T(1024)(128)(4,1)S(1)}, s32[]{:S(2)}) async-start(s8[4718592]{0:T(1024)(128)(4,1)} %bitcast.153), calls=%async_computation.1 | async-start | bytes 1048576
  201.2 15.5 %collective-permute-start.34 = (bf16[256,384]{1,0:T(8,128)(2,1)S(1)}, bf16[256,384]{1,0:T(8,128)(2,1)S(1)}, u32[]{:S(2)}, u32[]{:S(2)}) collective-permute-start(bf16[256,384]{1,0:T(8,128)(2,1)S(1)} %slice_bitcast_fusion.3), channel_id=1, source_target_pairs={{0,32},{32,64},{64,96},{96,0},{1,33},{33,65},{65,97},{97,1},{2,34}... | collective-permute-start | bytes 589832 | tf_op jit(solution)/shard_map/ppermute | solution.py:47
  201.3 15.4 %collective-permute-start.35 = (bf16[256,384]{1,0:T(8,128)(2,1)S(1)}, bf16[256,384]{1,0:T(8,128)(2,1)S(1)}, u32[]{:S(2)}, u32[]{:S(2)}) collective-permute-start(bf16[256,384]{1,0:T(8,128)(2,1)S(1)} %slice_bitcast_fusion.2), channel_id=1, source_target_pairs={{0,96},{32,0},{64,32},{96,64},{1,97},{33,1},{65,33},{97,65},{2,98}... | collective-permute-start | bytes 589832 | tf_op jit(solution)/shard_map/ppermute | solution.py:47
  204.6 5.2 %collective-permute-start.28 = (bf16[192,384]{1,0:T(8,128)(2,1)S(1)}, bf16[192,384]{1,0:T(8,128)(2,1)S(1)}, u32[]{:S(2)}, u32[]{:S(2)}) collective-permute-start(bf16[192,384]{1,0:T(8,128)(2,1)S(1)} %get-tuple-element.59), channel_id=1, source_target_pairs={{0,8},{1,3},{2,10},{3,5},{4,12},{5,7},{6,14},{7,1},{8,16},{9,11},{... | collective-permute-start | bytes 442376 | tf_op jit(solution)/shard_map/ppermute | solution.py:32
  205.6 6.6 %collective-permute-start.29 = (bf16[192,384]{1,0:T(8,128)(2,1)S(1)}, bf16[192,384]{1,0:T(8,128)(2,1)S(1)}, u32[]{:S(2)}, u32[]{:S(2)}) collective-permute-start(bf16[192,384]{1,0:T(8,128)(2,1)S(1)} %get-tuple-element.61), channel_id=1, source_target_pairs={{0,16},{1,5},{2,18},{3,7},{4,20},{5,1},{6,22},{7,3},{8,24},{9,13},... | collective-permute-start | bytes 442376 | tf_op jit(solution)/shard_map/ppermute | solution.py:32
  207.5 6.4 %collective-permute-start.30 = (bf16[192,384]{1,0:T(8,128)(2,1)S(1)}, bf16[192,384]{1,0:T(8,128)(2,1)S(1)}, u32[]{:S(2)}, u32[]{:S(2)}) collective-permute-start(bf16[192,384]{1,0:T(8,128)(2,1)S(1)} %get-tuple-element.60), channel_id=1, source_target_pairs={{0,24},{1,7},{2,26},{3,1},{4,28},{5,3},{6,30},{7,5},{8,0},{9,15},{... | collective-permute-start | bytes 442376 | tf_op jit(solution)/shard_map/ppermute | solution.py:32
  213.9 10.6 %collective-permute-start.31 = (bf16[192,384]{1,0:T(8,128)(2,1)S(1)}, bf16[192,384]{1,0:T(8,128)(2,1)S(1)}, u32[]{:S(2)}, u32[]{:S(2)}) collective-permute-start(bf16[192,384]{1,0:T(8,128)(2,1)S(1)} %fusion.50), channel_id=1, source_target_pairs={{0,0},{1,1},{2,2},{3,3},{4,4},{5,5},{6,6},{7,7},{8,32},{9,33},{10,... | collective-permute-start | bytes 442376 | tf_op jit(solution)/shard_map/ppermute | solution.py:32
  216.9 8.8 %copy-start.1 = (bf16[768,192]{0,1:T(8,128)(2,1)S(1)}, bf16[768,192]{0,1:T(8,128)(2,1)}, u32[]{:S(2)}) copy-start(bf16[768,192]{0,1:T(8,128)(2,1)} %param.7) | copy-start | bytes 884740
